TPU v7x, 32 devices: a whole 2x2x4 slice. The times are simulated.
32 devices in a mesh: segment: 2 (over x), blk: 16 (over z, y, core).
Axes of the slice: x: 2, y: 2, z: 4, core: 2. Of those that a mesh axis runs over, the one named last changes fastest.
Arguments:
- slabs: bfloat16 [32, 2048, 2048], P(None, 'blk'), may hold values from -6 to 6
- orbitals: bfloat16 [2048, 1024], P('blk'), may hold values from -0.125 to 0.125
- channel_orbital: int32 [1024], replicated, may hold values from 0 to 1023
- channel_target: int32 [1024], replicated, may hold values from 0 to 15
- coupling: int32 [16, 16], replicated, may hold values from -16 to 16
Outputs:
- channel_block: bfloat16 [32, 1024, 1024], P(None, 'blk', 'segment')
All inputs are finite; a program needn't handle non-finite values.
Results may differ from a plain program's by a relative error of at most 0.0056.
Values may be sent and summed in bfloat16 or wider, within the bound.
No kernel may reach another device: no remote copies, remote signals or barrier semaphores. Data moves between devices by JAX's collectives and lax.ppermute only.
A program may use at most 64 MiB of HBM per device.

v0:
```python
import jax
import jax.numpy as jnp
from jax import lax
from jax.experimental import pallas as pl
from jax.experimental.pallas import tpu as pltpu
from jax.sharding import PartitionSpec as P

VMEM = 49 * 1024 * 1024


def swap(x, bits):
    n = lax.axis_size("blk")
    return lax.ppermute(x, "blk", [(i, i ^ bits) for i in range(n)])


def plan(total):
    if total < 4:
        return [1] * total
    inner = total - 2
    return [1] + [2] * (inner // 2) + [1] * (inner % 2) + [1]


class Step:
    def __init__(self, body, outs, ins, scratch=(), aliases=None):
        self.body, self.outs, self.ins = body, outs, ins
        self.scratch, self.aliases = list(scratch), aliases or {}


def call(steps, tokens=()):
    ins = [x for step in steps for x in step.ins]
    outs = [x for step in steps for x in step.outs]
    scratch = [x for step in steps for x in step.scratch]
    aliases, first_in, first_out = {}, 0, 0
    for step in steps:
        aliases.update({first_in + i: first_out + o for i, o in step.aliases.items()})
        first_in += len(step.ins)
        first_out += len(step.outs)

    def body(*refs):
        left = [list(refs[: len(ins)]), list(refs[len(ins) + len(tokens) :])]
        left = [left[0], left[1][: len(outs)], left[1][len(outs) :]]

        def take(which, amount):
            taken, left[which] = left[which][:amount], left[which][amount:]
            return taken

        running = [
            step.body(
                take(0, len(step.ins)), take(1, len(step.outs)), take(2, len(step.scratch))
            )
            for step in steps
        ]
        for _ in range(3):
            for each in running:
                next(each, None)

    results = pl.pallas_call(
        body,
        out_shape=[jax.ShapeDtypeStruct(shape, kind) for shape, kind, _ in outs],
        in_specs=[pl.BlockSpec(memory_space=space) for _, space in ins]
        + [pl.BlockSpec(memory_space=pl.ANY)] * len(tokens),
        out_specs=[pl.BlockSpec(memory_space=space) for _, _, space in outs],
        scratch_shapes=scratch,
        input_output_aliases=aliases,
        compiler_params=pltpu.CompilerParams(vmem_limit_bytes=VMEM),
        cost_estimate=pl.CostEstimate(flops=0, bytes_accessed=0, transcendentals=0),
    )(*[x for x, _ in ins], *tokens)
    results = list(results)
    split = []
    for step in steps:
        split.append(results[: len(step.outs)])
        results = results[len(step.outs) :]
    return split


def inside(xs):
    return [(x, pltpu.VMEM) for x in xs]


def scalar(x):
    return [(x.reshape(-1).astype(jnp.int32), pltpu.SMEM)]


def after(xs, tokens):
    def body(ins, outs, scratch):
        yield

    outs = [(x.shape, x.dtype, pl.ANY) for x in xs]
    ins = [(x, pl.ANY) for x in xs]
    return call([Step(body, outs, ins, aliases={i: i for i in range(len(xs))})], tokens)[0]


def first_transform(slabs, blocks, where, group, count):
    n = len(blocks)
    rows, cols = blocks[0].shape
    depth, width = slabs.shape[1:]

    def body(ins, outs, scratch):
        place, slab_hbm, *held = ins
        panel, buffer, sems = scratch
        copies = []
        for j in range(group):
            source = slab_hbm.at[pl.ds(place[j], count)]
            copies.append(pltpu.make_async_copy(source, buffer.at[j], sems.at[j]))
            copies[j].start()
        yield
        for v in range(n):
            first = pl.multiple_of((place[group] ^ v) * rows, rows)
            panel[pl.ds(first, rows), :] = held[v][...]
        for j in range(group):
            copies[j].wait()
            result = jnp.dot(
                buffer[j].reshape(count * depth, width),
                panel[...],
                preferred_element_type=jnp.float32,
            )
            outs[j][...] = result.astype(jnp.bfloat16).reshape(count, depth, cols)

    return Step(
        body,
        [((count, depth, cols), jnp.bfloat16, pltpu.VMEM)] * group,
        scalar(where) + [(slabs, pltpu.HBM)] + inside(blocks),
        [
            pltpu.VMEM((n * rows, cols), jnp.bfloat16),
            pltpu.VMEM((group, count, depth, width), jnp.bfloat16),
            pltpu.SemaphoreType.DMA((group,)),
        ],
    )


def second_transform(picked, parts, side):
    pieces = len(parts)
    count, rows, cols = parts[0].shape
    share = picked.shape[0] // 2

    def body(ins, outs, scratch):
        side_now, picked_ref, *held = ins
        far, near = outs
        panel = scratch[0]
        yield
        here = pl.multiple_of(side_now[0] * share, share)
        there = pl.multiple_of((1 - side_now[0]) * share, share)
        for s in range(count):
            for i in range(pieces):
                panel[s, i * rows : (i + 1) * rows, :] = held[i][s]
        for s in range(count):
            far[s] = jnp.dot(
                picked_ref[pl.ds(there, share), :], panel[s], preferred_element_type=jnp.float32
            ).astype(jnp.bfloat16)
            near[s] = jnp.dot(
                picked_ref[pl.ds(here, share), :], panel[s], preferred_element_type=jnp.float32
            )

    return Step(
        body,
        [
            ((count, share, cols), jnp.bfloat16, pltpu.VMEM),
            ((count, share, cols), jnp.float32, pltpu.VMEM),
        ],
        scalar(side) + inside([picked]) + inside(parts),
        [pltpu.VMEM((count, pieces * rows, cols), jnp.bfloat16)],
    )


def add_sides(near, came, member, group):
    count, rows, cols = near.shape
    share = rows // group

    def body(ins, outs, scratch):
        member_now, near_ref, came_ref = ins
        yield
        for j in range(group):
            mine = pl.ds(pl.multiple_of((member_now[0] ^ j) * share, share), share)
            for s in range(count):
                total = near_ref[s, mine, :] + came_ref[s, mine, :].astype(jnp.float32)
                outs[j][s] = total.astype(jnp.bfloat16)

    return Step(
        body,
        [((count, share, cols), jnp.bfloat16, pltpu.VMEM)] * group,
        scalar(member) + inside([near, came]),
    )


def scale_into(out, angular, mine, place):
    group = len(mine)
    count, share, cols = mine[0].shape

    def body(ins, outs, scratch):
        place_now, angular_ref, *held = ins[:-1]
        buffer, sems = scratch
        yield
        copies = []
        for j in range(group):
            for s in range(count):
                value = angular_ref[...] * held[j][s].astype(jnp.float32)
                buffer[j, s] = value.astype(jnp.bfloat16)
            target = outs[0].at[pl.ds(place_now[j], count)]
            copies.append(pltpu.make_async_copy(buffer.at[j], target, sems.at[j]))
            copies[j].start()
        yield
        for copy in copies:
            copy.wait()

    return Step(
        body,
        [(out.shape, out.dtype, pltpu.HBM)],
        scalar(place) + inside([angular]) + inside(mine) + [(out, pltpu.HBM)],
        [
            pltpu.VMEM((group, count, share, cols), jnp.bfloat16),
            pltpu.SemaphoreType.DMA((group,)),
        ],
        {2 + group: 0},
    )


def on_device(slabs, orbitals, channel_orbital, channel_target, coupling):
    n = lax.axis_size("blk")
    group = n // 4
    segment_now = lax.axis_index("segment")
    me = lax.axis_index("blk")
    core = me % 2
    member = (me // 2) % group
    side = me // (2 * group)
    channels = channel_orbital.shape[0]
    share = channels // n
    half_cols = channels // lax.axis_size("segment")
    slab_count = slabs.shape[0]
    splines = jnp.arange(orbitals.shape[1], dtype=jnp.int32)

    picks = lax.dynamic_slice_in_dim(channel_orbital, segment_now * half_cols, half_cols)
    onehot = (splines[:, None] == picks[None, :]).astype(jnp.bfloat16)
    own = jnp.dot(orbitals, onehot, preferred_element_type=jnp.float32).astype(jnp.bfloat16)
    gathered = {0: own}
    bit = n // 2
    while bit:
        gathered.update({v ^ bit: swap(x, bit) for v, x in list(gathered.items())})
        bit //= 2
    column_blocks = [gathered[v] for v in range(n)]

    by_core = channel_orbital.reshape(n // 2, 2, share)

    def pick_rows(kind):
        wanted = lax.dynamic_index_in_dim(by_core, kind, 1, keepdims=False).reshape(-1)
        chosen = (wanted[:, None] == splines[None, :]).astype(jnp.bfloat16)
        return lax.dot_general(
            chosen, orbitals, (((1,), (1,)), ((), ())), preferred_element_type=jnp.float32
        ).astype(jnp.bfloat16)

    pair = jnp.concatenate([pick_rows(core), swap(pick_rows(1 - core), 1)], axis=1)

    def all_rows(pair):
        pairs = {0: pair}
        bit = group // 2
        while bit:
            pairs.update({j ^ bit: swap(x, 2 * bit) for j, x in list(pairs.items())})
            bit //= 2
        return jnp.concatenate([pairs[j] for j in range(group)], axis=1)

    kinds = jnp.arange(coupling.shape[0], dtype=jnp.int32)
    targets_rows = lax.dynamic_slice_in_dim(channel_target, me * share, share)
    targets_cols = lax.dynamic_slice_in_dim(channel_target, segment_now * half_cols, half_cols)
    onehot_rows = (targets_rows[:, None] == kinds[None, :]).astype(jnp.float32)
    onehot_cols = (kinds[:, None] == targets_cols[None, :]).astype(jnp.float32)
    angular = (
        jnp.dot(
            jnp.dot(
                onehot_rows, coupling.astype(jnp.float32), precision=lax.Precision.HIGHEST
            ),
            onehot_cols,
            precision=lax.Precision.HIGHEST,
        )
        / 16.0
    )

    order = member ^ jnp.arange(group, dtype=jnp.int32)
    counts = plan(slab_count // group)
    starts = [sum(counts[:k]) * group for k in range(len(counts))]

    def halves_of(k):
        where = jnp.concatenate([starts[k] + order * counts[k], me[None]])
        return first_transform(slabs, column_blocks, where, group, counts[k])

    def send(halves):
        return [halves[0]] + [swap(halves[j], 2 * j) for j in range(1, group)]

    out = jnp.zeros((slab_count, share, half_cols), jnp.bfloat16)
    last = len(counts) - 1
    halves, came, near, across, quarters = {}, {}, {}, {}, {}
    halves[0] = call([halves_of(0)])[0]
    came[0] = send(halves[0])
    token = halves[0][0]
    for k in range(1, min(3, last + 1)):
        halves[k] = call([halves_of(k)], [token])[0]
        token = halves[k][0]
    picked = all_rows(after([pair], [halves[0][0]])[0])

    for k in range(last + 4):
        steps, names = [], []
        if k <= last:
            held = after(came[k] + (halves[k + 1] if k < last else []), [token])
            came[k] = held[:group]
            parts = []
            for x in came[k]:
                parts += [x, swap(x, 1)]
            if k < last:
                came[k + 1] = send(held[group:])
            steps.append(second_transform(picked, parts, side))
            names.append("second")
        if 0 <= k - 2 <= last:
            steps.append(add_sides(near[k - 2], across[k - 2], member, group))
            names.append("add")
        if 0 <= k - 3 <= last:
            j = k - 3
            mine = [quarters[j][0]] + [swap(quarters[j][i], 2 * i) for i in range(1, group)]
            steps.append(scale_into(out, angular, mine, starts[j] + order * counts[j]))
            names.append("scale")
        if k + 3 <= last:
            steps.append(halves_of(k + 3))
            names.append("first")
        for name, result in zip(names, call(steps), strict=True):
            if name == "second":
                far, near[k] = result
                across[k] = swap(far, n // 2)
            elif name == "add":
                quarters[k - 2] = result
            elif name == "scale":
                out = result[0]
            else:
                halves[k + 3] = result
            token = result[0]
    return out


def solution(mesh):
    return jax.shard_map(
        on_device,
        mesh=mesh,
        in_specs=(P(None, "blk", None), P("blk", None), P(), P(), P()),
        out_specs=P(None, "blk", "segment"),
        check_vma=False,
    )
```

profile of v0, /device:TPU:0, one launch (start us, length us, event | category | flops | bytes accessed | tf_op | source)
XLA Modules:
  0.0 197.1 jit_solution(16692170790704891163)
XLA Ops:
  1.5 4.1 %collective-permute-start.8 = (bf16[128,512]{1,0:T(8,128)(2,1)S(1)}, bf16[128,512]{1,0:T(8,128)(2,1)S(1)}, u32[]{:S(2)}, u32[]{:S(2)}) collective-permute-start(bf16[128,512]{1,0:T(8,128)(2,1)S(1)} %fusion.6.refs_2_.refs_12_), channel_id=1, source_target_pairs={{0,8},{1,9},{2,10},{3,11},{4,12},{5,13},{6,14},{7,15},{8,0},{9,1},... | collective-permute-start | bytes 393224 | tf_op jit(solution)/shard_map/ppermute | solution.py:13
  5.6 1.6 collective-permute-start.4
  7.1 1.5 collective-permute-start.2
  10.7 1.3 collective-permute-done.8.refs_10_.refs_20_
  13.1 1.6 collective-permute-start.10
  15.5 1.5 collective-permute-done.12.refs_14_.refs_24_
  16.9 1.6 collective-permute-start.14
  19.3 2.3 %collective-permute-done.6.refs_8_.refs_18_ = bf16[128,512]{1,0:T(8,128)(2,1)S(1)} collective-permute-done((bf16[128,512]{1,0:T(8,128)(2,1)S(1)}, bf16[128,512]{1,0:T(8,128)(2,1)S(1)}, u32[]{:S(2)}, u32[]{:S(2)}) %collective-permute-start.6) | collective-permute-done | bytes 131104 | tf_op jit(solution)/shard_map/ppermute | solution.py:13
  22.1 1.8 collective-permute-done.14.refs_16_.refs_26_
  24.1 1.2 collective-permute-done.15.refs_17_.refs_27_
  25.3 3.4 %shard_map.55 = (bf16[1,128,512]{2,1,0:T(8,128)(2,1)S(1)}, bf16[1,128,512]{2,1,0:T(8,128)(2,1)S(1)}, bf16[1,128,512]{2,1,0:T(8,128)(2,1)S(1)}, bf16[1,128,512]{2,1,0:T(8,128)(2,1)S(1)}) custom-call(s32[5]{0:T(128)S(1)} %get-tuple-element.187.refs_0_, bf16[32,128,2048]{2,1,0:T(8,128)(2,1)} %refs_11_.3, bf16[128,512]{1,0:T(8,128)(2,1)S(1)} %fusion.6.refs_2_.refs_12_, ...), custom_call_target="tpu_custom_call" | custom-call | tf_op jit(solution)/shard_map/pallas_call | solution.py:57
  28.8 1.3 collective-permute-start.17
  30.1 1.6 collective-permute-start.16
  32.9 2.2 %collective-permute-start.21 = (bf16[1,128,512]{2,1,0:T(8,128)(2,1)S(1)}, bf16[1,128,512]{2,1,0:T(8,128)(2,1)S(1)}, u32[]{:S(2)}, u32[]{:S(2)}) collective-permute-start(bf16[1,128,512]{2,1,0:T(8,128)(2,1)S(1)} %get-tuple-element.98), channel_id=1, source_target_pairs={{0,6},{1,7},{2,4},{3,5},{4,2},{5,3},{6,0},{7,1},{8,14},{9,15},{10,... | collective-permute-start | bytes 393224 | tf_op jit(solution)/shard_map/ppermute | solution.py:13
  35.2 5.4 %shard_map.57 = (bf16[2,128,512]{2,1,0:T(8,128)(2,1)S(1)}, bf16[2,128,512]{2,1,0:T(8,128)(2,1)}, bf16[2,128,512]{2,1,0:T(8,128)(2,1)}, bf16[2,128,512]{2,1,0:T(8,128)(2,1)}) custom-call(s32[5]{0:T(128)S(1)} %get-tuple-element.188.refs_0_, bf16[32,128,2048]{2,1,0:T(8,128)(2,1)} %refs_11_.3, bf16[128,512]{1,0:T(8,128)(2,1)S(1)} %fusion.6.refs_2_.refs_12_, ...), custom_call_target="tpu_custom_call" | custom-call | tf_op jit(solution)/shard_map/pallas_call | solution.py:57
  40.6 4.7 %shard_map.58 = (bf16[2,128,512]{2,1,0:T(8,128)(2,1)S(1)}, bf16[2,128,512]{2,1,0:T(8,128)(2,1)S(1)}, bf16[2,128,512]{2,1,0:T(8,128)(2,1)S(1)}, bf16[2,128,512]{2,1,0:T(8,128)(2,1)S(1)}) custom-call(s32[5]{0:T(128)S(1)} %pad_add_fusion.2.refs_0_, bf16[32,128,2048]{2,1,0:T(8,128)(2,1)} %refs_11_.3, bf16[128,512]{1,0:T(8,128)(2,1)S(1)} %fusion.6.refs_2_.refs_12_, ...), custom_call_target="tpu_custom_call" | custom-call | tf_op jit(solution)/shard_map/pallas_call | solution.py:57
  46.1 1.6 collective-permute-start.22
  49.1 1.2 collective-permute-start.24
  50.5 4.5 %collective-permute-done.18 = bf16[512,256]{1,0:T(8,128)(2,1)} collective-permute-done((bf16[512,256]{1,0:T(8,128)(2,1)}, bf16[512,256]{1,0:T(8,128)(2,1)}, u32[]{:S(2)}, u32[]{:S(2)}) %collective-permute-start.18) | collective-permute-done | bytes 262176 | tf_op jit(solution)/shard_map/ppermute | solution.py:13
  54.9 2.2 %pad_maximum_fusion.refs_1_ = bf16[512,1024]{1,0:T(8,128)(2,1)} fusion(bf16[512,256]{1,0:T(8,128)(2,1)} %collective-permute-done.18, bf16[512,256]{1,0:T(8,128)(2,1)} %collective-permute-done.17, bf16[512,256]{1,0:T(8,128)(2,1)} %copy-done.32, bf16[512,256]{1,0:T(8,128)(2,1)S(1)} %shard_map.56), kind=kLoop, calls=%fused_computation.11 | loop fusion | flops 4194304 | bytes 2097152 | tf_op jit(solution)/shard_map/concatenate | solution.py:258
  57.2 5.8 %shard_map.60 = (bf16[1,256,512]{2,1,0:T(8,128)(2,1)S(1)}, f32[1,256,512]{2,1,0:T(8,128)S(1)}, bf16[2,128,512]{2,1,0:T(8,128)(2,1)S(1)}, bf16[2,128,512]{2,1,0:T...) custom-call(s32[1]{0:T(128)} %bitcast.1.refs_0_, ...), custom_call_target="tpu_custom_call" | custom-call | tf_op jit(solution)/shard_map/pallas_call | solution.py:57
  63.0 2.6 %collective-permute-done.22.refs_1_ = bf16[2,128,512]{2,1,0:T(8,128)(2,1)S(1)} collective-permute-done((bf16[2,128,512]{2,1,0:T(8,128)(2,1)}, bf16[2,128,512]{2,1,0:T(8,128)(2,1)S(1)}, u32[]{:S(2)}, u32[]{:S(2)}) %collective-permute-start.22) | collective-permute-done | bytes 262176 | tf_op jit(solution)/shard_map/ppermute | solution.py:13
  68.0 2.0 %collective-permute-start.31 = (bf16[2,128,512]{2,1,0:T(8,128)(2,1)S(1)}, bf16[2,128,512]{2,1,0:T(8,128)(2,1)S(1)}, u32[]{:S(2)}, u32[]{:S(2)}) collective-permute-start(bf16[2,128,512]{2,1,0:T(8,128)(2,1)S(1)} %get-tuple-element.119), channel_id=1, source_target_pairs={{0,6},{1,7},{2,4},{3,5},{4,2},{5,3},{6,0},{7,1},{8,14},{9,15},{10,... | collective-permute-start | bytes 786440 | tf_op jit(solution)/shard_map/ppermute | solution.py:13
  70.0 2.4 %collective-permute-start.43 = (bf16[1,256,512]{2,1,0:T(8,128)(2,1)S(1)}, bf16[1,256,512]{2,1,0:T(8,128)(2,1)S(1)}, u32[]{:S(2)}, u32[]{:S(2)}) collective-permute-start(bf16[1,256,512]{2,1,0:T(8,128)(2,1)S(1)} %get-tuple-element.140), channel_id=1, source_target_pairs={{0,8},{1,9},{2,10},{3,11},{4,12},{5,13},{6,14},{7,15},{8,0},{9,1},... | collective-permute-start | bytes 786440 | tf_op jit(solution)/shard_map/ppermute | solution.py:13
  72.5 6.2 %shard_map.62 = (bf16[2,256,512]{2,1,0:T(8,128)(2,1)}, f32[2,256,512]{2,1,0:T(8,128)}, bf16[1,128,512]{2,1,0:T(8,128)(2,1)S(1)}, bf16[1,128,512]{2,1,0:T(8,128)(...) custom-call(s32[1]{0:T(128)} %bitcast.1.refs_0_, ...), custom_call_target="tpu_custom_call" | custom-call | tf_op jit(solution)/shard_map/pallas_call | solution.py:57
  78.7 3.3 %collective-permute-done.30.refs_2_ = bf16[2,128,512]{2,1,0:T(8,128)(2,1)S(1)} collective-permute-done((bf16[2,128,512]{2,1,0:T(8,128)(2,1)S(1)}, bf16[2,128,512]{2,1,0:T(8,128)(2,1)S(1)}, u32[]{:S(2)}, u32[]{:S(2)}) %collective-permute-start.30) | collective-permute-done | bytes 262176 | tf_op jit(solution)/shard_map/ppermute | solution.py:13
  82.0 5.7 %collective-permute-done.31.refs_3_ = bf16[2,128,512]{2,1,0:T(8,128)(2,1)S(1)} collective-permute-done((bf16[2,128,512]{2,1,0:T(8,128)(2,1)S(1)}, bf16[2,128,512]{2,1,0:T(8,128)(2,1)S(1)}, u32[]{:S(2)}, u32[]{:S(2)}) %collective-permute-start.31) | collective-permute-done | bytes 262176 | tf_op jit(solution)/shard_map/ppermute | solution.py:13
  89.3 1.4 collective-permute-start.37
  90.7 1.6 collective-permute-start.38
  92.3 2.5 %shard_map.64 = (bf16[2,256,512]{2,1,0:T(8,128)(2,1)S(1)}, f32[2,256,512]{2,1,0:T(8,128)S(1)}, bf16[1,64,512]{2,1,0:T(8,128)(2,1)S(1)}, bf16[1,64,512]{2,1,0:T(8...) custom-call(s32[1]{0:T(128)} %bitcast.1.refs_0_, ...), custom_call_target="tpu_custom_call" | custom-call | tf_op jit(solution)/shard_map/pallas_call | solution.py:57
  95.4 1.4 collective-permute-start.53
  97.6 1.5 collective-permute-start.54
  99.1 2.0 %collective-permute-start.51 = (bf16[2,256,512]{2,1,0:T(8,128)(2,1)}, bf16[2,256,512]{2,1,0:T(8,128)(2,1)S(1)}, u32[]{:S(2)}, u32[]{:S(2)}) collective-permute-start(bf16[2,256,512]{2,1,0:T(8,128)(2,1)} %get-tuple-element.151), channel_id=1, source_target_pairs={{0,8},{1,9},{2,10},{3,11},{4,12},{5,13},{6,14},{7,15},{8,0},{9,1},... | collective-permute-start | bytes 1572872 | tf_op jit(solution)/shard_map/ppermute | solution.py:13
  101.1 10.6 %collective-permute-done.38.refs_3_ = bf16[2,128,512]{2,1,0:T(8,128)(2,1)S(1)} collective-permute-done((bf16[2,128,512]{2,1,0:T(8,128)(2,1)S(1)}, bf16[2,128,512]{2,1,0:T(8,128)(2,1)S(1)}, u32[]{:S(2)}, u32[]{:S(2)}) %collective-permute-start.38) | collective-permute-done | bytes 262176 | tf_op jit(solution)/shard_map/ppermute | solution.py:13
  114.0 1.3 dynamic_slice.17
  117.0 1.2 collective-permute-start.44
  118.9 2.4 %collective-permute-start.46 = (bf16[1,128,512]{2,1,0:T(8,128)(2,1)}, bf16[1,128,512]{2,1,0:T(8,128)(2,1)S(1)}, u32[]{:S(2)}, u32[]{:S(2)}) collective-permute-start(bf16[1,128,512]{2,1,0:T(8,128)(2,1)} %copy-done.24), channel_id=1, source_target_pairs={{0,6},{1,7},{2,4},{3,5},{4,2},{5,3},{6,0},{7,1},{8,14},{9,15},{10,... | collective-permute-start | bytes 393224 | tf_op jit(solution)/shard_map/ppermute | solution.py:13
  122.0 0.9 convolution_multiply_fusion.refs_14_.refs_4_.refs_1_
  124.4 1.6 broadcast_in_dim.5.refs_19_
  126.0 3.7 %shard_map.66 = (bf16[2,256,512]{2,1,0:T(8,128)(2,1)S(1)}, f32[2,256,512]{2,1,0:T(8,128)S(1)}, bf16[2,64,512]{2,1,0:T(8,128)(2,1)S(1)}, bf16[2,64,512]{2,1,0:T(8...) custom-call(s32[1]{0:T(128)} %bitcast.1.refs_0_, ...), custom_call_target="tpu_custom_call", output_to_operand_aliasing={{6}: (19, {})} | custom-call | tf_op jit(solution)/shard_map/pallas_call | solution.py:57
  129.8 1.2 collective-permute-done.46.refs_3_
  131.0 1.6 copy-done.1
  132.6 1.8 collective-permute-start.64
  136.5 3.1 %collective-permute-start.61 = (bf16[2,64,512]{2,1,0:T(8,128)(2,1)S(1)}, bf16[2,64,512]{2,1,0:T(8,128)(2,1)S(1)}, u32[]{:S(2)}, u32[]{:S(2)}) collective-permute-start(bf16[2,64,512]{2,1,0:T(8,128)(2,1)S(1)} %get-tuple-element.164), channel_id=1, source_target_pairs={{0,4},{1,5},{2,6},{3,7},{4,0},{5,1},{6,2},{7,3},{8,12},{9,13},{10,... | collective-permute-start | bytes 393224 | tf_op jit(solution)/shard_map/ppermute | solution.py:13
  139.9 1.5 collective-permute-done.60.refs_16_
  141.4 9.4 %collective-permute-done.61.refs_17_ = bf16[2,64,512]{2,1,0:T(8,128)(2,1)S(1)} collective-permute-done((bf16[2,64,512]{2,1,0:T(8,128)(2,1)S(1)}, bf16[2,64,512]{2,1,0:T(8,128)(2,1)S(1)}, u32[]{:S(2)}, u32[]{:S(2)}) %collective-permute-start.61) | collective-permute-done | bytes 131104 | tf_op jit(solution)/shard_map/ppermute | solution.py:13
  150.8 2.0 %collective-permute-done.62.refs_18_ = bf16[2,64,512]{2,1,0:T(8,128)(2,1)S(1)} collective-permute-done((bf16[2,64,512]{2,1,0:T(8,128)(2,1)S(1)}, bf16[2,64,512]{2,1,0:T(8,128)(2,1)S(1)}, u32[]{:S(2)}, u32[]{:S(2)}) %collective-permute-start.62) | collective-permute-done | bytes 131104 | tf_op jit(solution)/shard_map/ppermute | solution.py:13
  152.8 6.8 %collective-permute-done.59.refs_12_ = bf16[2,256,512]{2,1,0:T(8,128)(2,1)S(1)} collective-permute-done((bf16[2,256,512]{2,1,0:T(8,128)(2,1)}, bf16[2,256,512]{2,1,0:T(8,128)(2,1)S(1)}, u32[]{:S(2)}, u32[]{:S(2)}) %collective-permute-start.59) | collective-permute-done | bytes 524320 | tf_op jit(solution)/shard_map/ppermute | solution.py:13
  159.6 2.8 %shard_map.68 = (bf16[1,256,512]{2,1,0:T(8,128)(2,1)S(1)}, f32[1,256,512]{2,1,0:T(8,128)S(1)}, bf16[2,64,512]{2,1,0:T(8,128)(2,1)S(1)}, bf16[2,64,512]{2,1,0:T(8...) custom-call(s32[1]{0:T(128)} %bitcast.1.refs_0_, ...), custom_call_target="tpu_custom_call", output_to_operand_aliasing={{6}: (19, {})} | custom-call | tf_op jit(solution)/shard_map/pallas_call | solution.py:57
  162.4 1.4 collective-permute-start.65
  163.9 2.1 %collective-permute-start.67 = (bf16[2,64,512]{2,1,0:T(8,128)(2,1)S(1)}, bf16[2,64,512]{2,1,0:T(8,128)(2,1)S(1)}, u32[]{:S(2)}, u32[]{:S(2)}) collective-permute-start(bf16[2,64,512]{2,1,0:T(8,128)(2,1)S(1)} %get-tuple-element.173), channel_id=1, source_target_pairs={{0,6},{1,7},{2,4},{3,5},{4,2},{5,3},{6,0},{7,1},{8,14},{9,15},{10,... | collective-permute-start | bytes 393224 | tf_op jit(solution)/shard_map/ppermute | solution.py:13
  167.5 5.4 %collective-permute-done.66.refs_7_ = bf16[2,64,512]{2,1,0:T(8,128)(2,1)S(1)} collective-permute-done((bf16[2,64,512]{2,1,0:T(8,128)(2,1)S(1)}, bf16[2,64,512]{2,1,0:T(8,128)(2,1)S(1)}, u32[]{:S(2)}, u32[]{:S(2)}) %collective-permute-start.66) | collective-permute-done | bytes 131104 | tf_op jit(solution)/shard_map/ppermute | solution.py:13
  172.9 3.2 %collective-permute-done.67.refs_8_ = bf16[2,64,512]{2,1,0:T(8,128)(2,1)S(1)} collective-permute-done((bf16[2,64,512]{2,1,0:T(8,128)(2,1)S(1)}, bf16[2,64,512]{2,1,0:T(8,128)(2,1)S(1)}, u32[]{:S(2)}, u32[]{:S(2)}) %collective-permute-start.67) | collective-permute-done | bytes 131104 | tf_op jit(solution)/shard_map/ppermute | solution.py:13
  176.5 1.4 shard_map.69
  177.9 1.4 collective-permute-start.68
  179.3 2.1 %collective-permute-start.70 = (bf16[2,64,512]{2,1,0:T(8,128)(2,1)S(1)}, bf16[2,64,512]{2,1,0:T(8,128)(2,1)S(1)}, u32[]{:S(2)}, u32[]{:S(2)}) collective-permute-start(bf16[2,64,512]{2,1,0:T(8,128)(2,1)S(1)} %get-tuple-element.178), channel_id=1, source_target_pairs={{0,6},{1,7},{2,4},{3,5},{4,2},{5,3},{6,0},{7,1},{8,14},{9,15},{10,... | collective-permute-start | bytes 393224 | tf_op jit(solution)/shard_map/ppermute | solution.py:13
  181.4 1.6 collective-permute-done.68.refs_6_
  183.0 2.5 %collective-permute-done.69.refs_7_ = bf16[2,64,512]{2,1,0:T(8,128)(2,1)S(1)} collective-permute-done((bf16[2,64,512]{2,1,0:T(8,128)(2,1)S(1)}, bf16[2,64,512]{2,1,0:T(8,128)(2,1)S(1)}, u32[]{:S(2)}, u32[]{:S(2)}) %collective-permute-start.69) | collective-permute-done | bytes 131104 | tf_op jit(solution)/shard_map/ppermute | solution.py:13
  185.5 2.2 %collective-permute-done.70.refs_8_ = bf16[2,64,512]{2,1,0:T(8,128)(2,1)S(1)} collective-permute-done((bf16[2,64,512]{2,1,0:T(8,128)(2,1)S(1)}, bf16[2,64,512]{2,1,0:T(8,128)(2,1)S(1)}, u32[]{:S(2)}, u32[]{:S(2)}) %collective-permute-start.70) | collective-permute-done | bytes 131104 | tf_op jit(solution)/shard_map/ppermute | solution.py:13
  187.7 1.4 shard_map.70
  190.0 2.7 %collective-permute-start.73 = (bf16[1,64,512]{2,1,0:T(8,128)(2,1)S(1)}, bf16[1,64,512]{2,1,0:T(8,128)(2,1)S(1)}, u32[]{:S(2)}, u32[]{:S(2)}) collective-permute-start(bf16[1,64,512]{2,1,0:T(8,128)(2,1)S(1)} %get-tuple-element.183), channel_id=1, source_target_pairs={{0,6},{1,7},{2,4},{3,5},{4,2},{5,3},{6,0},{7,1},{8,14},{9,15},{10,... | collective-permute-start | bytes 196616 | tf_op jit(solution)/shard_map/ppermute | solution.py:13
  192.7 1.5 collective-permute-done.71.refs_3_
  194.2 1.5 collective-permute-done.73.refs_5_
  195.6 1.3 shard_map.71
  (191 shorter events, 28.1 us)
Async XLA Ops:
  1.5 10.5 %collective-permute-start.8 = (bf16[128,512]{1,0:T(8,128)(2,1)S(1)}, bf16[128,512]{1,0:T(8,128)(2,1)S(1)}, u32[]{:S(2)}, u32[]{:S(2)}) collective-permute-start(bf16[128,512]{1,0:T(8,128)(2,1)S(1)} %fusion.6.refs_2_.refs_12_), channel_id=1, source_target_pairs={{0,8},{1,9},{2,10},{3,11},{4,12},{5,13},{6,14},{7,15},{8,0},{9,1},... | collective-permute-start | bytes 393224 | tf_op jit(solution)/shard_map/ppermute | solution.py:13
  5.6 9.1 %collective-permute-start.4 = (bf16[128,512]{1,0:T(8,128)(2,1)S(1)}, bf16[128,512]{1,0:T(8,128)(2,1)S(1)}, u32[]{:S(2)}, u32[]{:S(2)}) collective-permute-start(bf16[128,512]{1,0:T(8,128)(2,1)S(1)} %fusion.6.refs_2_.refs_12_), channel_id=1, source_target_pairs={{0,4},{1,5},{2,6},{3,7},{4,0},{5,1},{6,2},{7,3},{8,12},{9,13},{10,... | collective-permute-start | bytes 393224 | tf_op jit(solution)/shard_map/ppermute | solution.py:13
  7.1 7.6 %collective-permute-start.2 = (bf16[128,512]{1,0:T(8,128)(2,1)S(1)}, bf16[128,512]{1,0:T(8,128)(2,1)S(1)}, u32[]{:S(2)}, u32[]{:S(2)}) collective-permute-start(bf16[128,512]{1,0:T(8,128)(2,1)S(1)} %fusion.6.refs_2_.refs_12_), channel_id=1, source_target_pairs={{0,2},{1,3},{2,0},{3,1},{4,6},{5,7},{6,4},{7,5},{8,10},{9,11},{10,... | collective-permute-start | bytes 393224 | tf_op jit(solution)/shard_map/ppermute | solution.py:13
  8.7 6.6 %collective-permute-start.1 = (bf16[128,512]{1,0:T(8,128)(2,1)S(1)}, bf16[128,512]{1,0:T(8,128)(2,1)S(1)}, u32[]{:S(2)}, u32[]{:S(2)}) collective-permute-start(bf16[128,512]{1,0:T(8,128)(2,1)S(1)} %fusion.6.refs_2_.refs_12_), channel_id=1, source_target_pairs={{0,1},{1,0},{2,3},{3,2},{4,5},{5,4},{6,7},{7,6},{8,9},{9,8},{10,11... | collective-permute-start | bytes 393224 | tf_op jit(solution)/shard_map/ppermute | solution.py:13
  10.1 3.1 %collective-permute-start = (bf16[512,128]{1,0:T(8,128)(2,1)S(1)}, bf16[512,128]{1,0:T(8,128)(2,1)S(1)}, u32[]{:S(2)}, u32[]{:S(2)}) collective-permute-start(bf16[512,128]{1,0:T(8,128)(2,1)S(1)} %fusion.4), channel_id=1, source_target_pairs={{0,1},{1,0},{2,3},{3,2},{4,5},{5,4},{6,7},{7,6},{8,9},{9,8},{10,11... | collective-permute-start | bytes 393224 | tf_op jit(solution)/shard_map/ppermute | solution.py:13
  12.0 5.0 %collective-permute-start.12 = (bf16[128,512]{1,0:T(8,128)(2,1)S(1)}, bf16[128,512]{1,0:T(8,128)(2,1)S(1)}, u32[]{:S(2)}, u32[]{:S(2)}) collective-permute-start(bf16[128,512]{1,0:T(8,128)(2,1)S(1)} %collective-permute-done.8.refs_10_.refs_20_), channel_id=1, source_target_pairs={{0,4},{1,5},{2,6},{3,7},{4,0},{5,1},{6,2},{7,3},{8,12},{9,13},{10,... | collective-permute-start | bytes 393224 | tf_op jit(solution)/shard_map/ppermute | solution.py:13
  13.1 5.7 %collective-permute-start.10 = (bf16[128,512]{1,0:T(8,128)(2,1)S(1)}, bf16[128,512]{1,0:T(8,128)(2,1)S(1)}, u32[]{:S(2)}, u32[]{:S(2)}) collective-permute-start(bf16[128,512]{1,0:T(8,128)(2,1)S(1)} %collective-permute-done.8.refs_10_.refs_20_), channel_id=1, source_target_pairs={{0,2},{1,3},{2,0},{3,1},{4,6},{5,7},{6,4},{7,5},{8,10},{9,11},{10,... | collective-permute-start | bytes 393224 | tf_op jit(solution)/shard_map/ppermute | solution.py:13
  14.7 4.1 %collective-permute-start.9 = (bf16[128,512]{1,0:T(8,128)(2,1)S(1)}, bf16[128,512]{1,0:T(8,128)(2,1)S(1)}, u32[]{:S(2)}, u32[]{:S(2)}) collective-permute-start(bf16[128,512]{1,0:T(8,128)(2,1)S(1)} %collective-permute-done.8.refs_10_.refs_20_), channel_id=1, source_target_pairs={{0,1},{1,0},{2,3},{3,2},{4,5},{5,4},{6,7},{7,6},{8,9},{9,8},{10,11... | collective-permute-start | bytes 393224 | tf_op jit(solution)/shard_map/ppermute | solution.py:13
  14.7 6.9 %collective-permute-start.6 = (bf16[128,512]{1,0:T(8,128)(2,1)S(1)}, bf16[128,512]{1,0:T(8,128)(2,1)S(1)}, u32[]{:S(2)}, u32[]{:S(2)}) collective-permute-start(bf16[128,512]{1,0:T(8,128)(2,1)S(1)} %collective-permute-done.4.refs_6_.refs_16_), channel_id=1, source_target_pairs={{0,2},{1,3},{2,0},{3,1},{4,6},{5,7},{6,4},{7,5},{8,10},{9,11},{10,... | collective-permute-start | bytes 393224 | tf_op jit(solution)/shard_map/ppermute | solution.py:13
  15.3 6.3 %collective-permute-start.5 = (bf16[128,512]{1,0:T(8,128)(2,1)S(1)}, bf16[128,512]{1,0:T(8,128)(2,1)S(1)}, u32[]{:S(2)}, u32[]{:S(2)}) collective-permute-start(bf16[128,512]{1,0:T(8,128)(2,1)S(1)} %collective-permute-done.4.refs_6_.refs_16_), channel_id=1, source_target_pairs={{0,1},{1,0},{2,3},{3,2},{4,5},{5,4},{6,7},{7,6},{8,9},{9,8},{10,11... | collective-permute-start | bytes 393224 | tf_op jit(solution)/shard_map/ppermute | solution.py:13
  16.9 7.0 %collective-permute-start.14 = (bf16[128,512]{1,0:T(8,128)(2,1)S(1)}, bf16[128,512]{1,0:T(8,128)(2,1)S(1)}, u32[]{:S(2)}, u32[]{:S(2)}) collective-permute-start(bf16[128,512]{1,0:T(8,128)(2,1)S(1)} %collective-permute-done.12.refs_14_.refs_24_), channel_id=1, source_target_pairs={{0,2},{1,3},{2,0},{3,1},{4,6},{5,7},{6,4},{7,5},{8,10},{9,11},{10,... | collective-permute-start | bytes 393224 | tf_op jit(solution)/shard_map/ppermute | solution.py:13
  18.8 5.2 %collective-permute-start.3 = (bf16[128,512]{1,0:T(8,128)(2,1)S(1)}, bf16[128,512]{1,0:T(8,128)(2,1)S(1)}, u32[]{:S(2)}, u32[]{:S(2)}) collective-permute-start(bf16[128,512]{1,0:T(8,128)(2,1)S(1)} %collective-permute-done.2.refs_4_.refs_14_), channel_id=1, source_target_pairs={{0,1},{1,0},{2,3},{3,2},{4,5},{5,4},{6,7},{7,6},{8,9},{9,8},{10,11... | collective-permute-start | bytes 393224 | tf_op jit(solution)/shard_map/ppermute | solution.py:13
  18.8 5.2 %collective-permute-start.13 = (bf16[128,512]{1,0:T(8,128)(2,1)S(1)}, bf16[128,512]{1,0:T(8,128)(2,1)S(1)}, u32[]{:S(2)}, u32[]{:S(2)}) collective-permute-start(bf16[128,512]{1,0:T(8,128)(2,1)S(1)} %collective-permute-done.12.refs_14_.refs_24_), channel_id=1, source_target_pairs={{0,1},{1,0},{2,3},{3,2},{4,5},{5,4},{6,7},{7,6},{8,9},{9,8},{10,11... | collective-permute-start | bytes 393224 | tf_op jit(solution)/shard_map/ppermute | solution.py:13
  28.8 16.7 %collective-permute-start.17 = (bf16[512,256]{1,0:T(8,128)(2,1)S(1)}, bf16[512,256]{1,0:T(8,128)(2,1)}, u32[]{:S(2)}, u32[]{:S(2)}) collective-permute-start(bf16[512,256]{1,0:T(8,128)(2,1)S(1)} %shard_map.56), channel_id=1, source_target_pairs={{0,4},{1,5},{2,6},{3,7},{4,0},{5,1},{6,2},{7,3},{8,12},{9,13},{10,... | collective-permute-start | bytes 786440 | tf_op jit(solution)/shard_map/ppermute | solution.py:13
  30.1 17.6 %collective-permute-start.16 = (bf16[512,256]{1,0:T(8,128)(2,1)S(1)}, bf16[512,256]{1,0:T(8,128)(2,1)S(1)}, u32[]{:S(2)}, u32[]{:S(2)}) collective-permute-start(bf16[512,256]{1,0:T(8,128)(2,1)S(1)} %shard_map.56), channel_id=1, source_target_pairs={{0,2},{1,3},{2,0},{3,1},{4,6},{5,7},{6,4},{7,5},{8,10},{9,11},{10,... | collective-permute-start | bytes 786440 | tf_op jit(solution)/shard_map/ppermute | solution.py:13
  31.6 13.7 %collective-permute-start.19 = (bf16[1,128,512]{2,1,0:T(8,128)(2,1)S(1)}, bf16[1,128,512]{2,1,0:T(8,128)(2,1)}, u32[]{:S(2)}, u32[]{:S(2)}) collective-permute-start(bf16[1,128,512]{2,1,0:T(8,128)(2,1)S(1)} %get-tuple-element.96), channel_id=1, source_target_pairs={{0,2},{1,3},{2,0},{3,1},{4,6},{5,7},{6,4},{7,5},{8,10},{9,11},{10,... | collective-permute-start | bytes 393224 | tf_op jit(solution)/shard_map/ppermute | solution.py:13
  32.1 13.2 %collective-permute-start.20 = (bf16[1,128,512]{2,1,0:T(8,128)(2,1)S(1)}, bf16[1,128,512]{2,1,0:T(8,128)(2,1)S(1)}, u32[]{:S(2)}, u32[]{:S(2)}) collective-permute-start(bf16[1,128,512]{2,1,0:T(8,128)(2,1)S(1)} %get-tuple-element.97), channel_id=1, source_target_pairs={{0,4},{1,5},{2,6},{3,7},{4,0},{5,1},{6,2},{7,3},{8,12},{9,13},{10,... | collective-permute-start | bytes 393224 | tf_op jit(solution)/shard_map/ppermute | solution.py:13
  32.9 12.4 %collective-permute-start.21 = (bf16[1,128,512]{2,1,0:T(8,128)(2,1)S(1)}, bf16[1,128,512]{2,1,0:T(8,128)(2,1)S(1)}, u32[]{:S(2)}, u32[]{:S(2)}) collective-permute-start(bf16[1,128,512]{2,1,0:T(8,128)(2,1)S(1)} %get-tuple-element.98), channel_id=1, source_target_pairs={{0,6},{1,7},{2,4},{3,5},{4,2},{5,3},{6,0},{7,1},{8,14},{9,15},{10,... | collective-permute-start | bytes 393224 | tf_op jit(solution)/shard_map/ppermute | solution.py:13
  45.3 3.1 %collective-permute-start.25 = (bf16[1,128,512]{2,1,0:T(8,128)(2,1)S(1)}, bf16[1,128,512]{2,1,0:T(8,128)(2,1)S(1)}, u32[]{:S(2)}, u32[]{:S(2)}) collective-permute-start(bf16[1,128,512]{2,1,0:T(8,128)(2,1)S(1)} %get-tuple-element.111.refs_2_), channel_id=1, source_target_pairs={{0,1},{1,0},{2,3},{3,2},{4,5},{5,4},{6,7},{7,6},{8,9},{9,8},{10,11... | collective-permute-start | bytes 393224 | tf_op jit(solution)/shard_map/ppermute | solution.py:13
  45.4 9.5 %collective-permute-start.18 = (bf16[512,256]{1,0:T(8,128)(2,1)}, bf16[512,256]{1,0:T(8,128)(2,1)}, u32[]{:S(2)}, u32[]{:S(2)}) collective-permute-start(bf16[512,256]{1,0:T(8,128)(2,1)} %collective-permute-done.17), channel_id=1, source_target_pairs={{0,2},{1,3},{2,0},{3,1},{4,6},{5,7},{6,4},{7,5},{8,10},{9,11},{10,... | collective-permute-start | bytes 786440 | tf_op jit(solution)/shard_map/ppermute | solution.py:13
  46.0 4.5 %collective-permute-start.26 = (bf16[1,128,512]{2,1,0:T(8,128)(2,1)}, bf16[1,128,512]{2,1,0:T(8,128)(2,1)}, u32[]{:S(2)}, u32[]{:S(2)}) collective-permute-start(bf16[1,128,512]{2,1,0:T(8,128)(2,1)} %get-tuple-element.112.refs_4_), channel_id=1, source_target_pairs={{0,1},{1,0},{2,3},{3,2},{4,5},{5,4},{6,7},{7,6},{8,9},{9,8},{10,11... | collective-permute-start | bytes 393224 | tf_op jit(solution)/shard_map/ppermute | solution.py:13
  46.1 19.5 %collective-permute-start.22 = (bf16[2,128,512]{2,1,0:T(8,128)(2,1)}, bf16[2,128,512]{2,1,0:T(8,128)(2,1)S(1)}, u32[]{:S(2)}, u32[]{:S(2)}) collective-permute-start(bf16[2,128,512]{2,1,0:T(8,128)(2,1)} %get-tuple-element.105), channel_id=1, source_target_pairs={{0,2},{1,3},{2,0},{3,1},{4,6},{5,7},{6,4},{7,5},{8,10},{9,11},{10,... | collective-permute-start | bytes 786440 | tf_op jit(solution)/shard_map/ppermute | solution.py:13
  47.7 17.9 %collective-permute-start.23 = (bf16[2,128,512]{2,1,0:T(8,128)(2,1)}, bf16[2,128,512]{2,1,0:T(8,128)(2,1)}, u32[]{:S(2)}, u32[]{:S(2)}) collective-permute-start(bf16[2,128,512]{2,1,0:T(8,128)(2,1)} %get-tuple-element.106), channel_id=1, source_target_pairs={{0,4},{1,5},{2,6},{3,7},{4,0},{5,1},{6,2},{7,3},{8,12},{9,13},{10,... | collective-permute-start | bytes 786440 | tf_op jit(solution)/shard_map/ppermute | solution.py:13
  49.1 16.5 %collective-permute-start.24 = (bf16[2,128,512]{2,1,0:T(8,128)(2,1)}, bf16[2,128,512]{2,1,0:T(8,128)(2,1)}, u32[]{:S(2)}, u32[]{:S(2)}) collective-permute-start(bf16[2,128,512]{2,1,0:T(8,128)(2,1)} %get-tuple-element.107), channel_id=1, source_target_pairs={{0,6},{1,7},{2,4},{3,5},{4,2},{5,3},{6,0},{7,1},{8,14},{9,15},{10,... | collective-permute-start | bytes 786440 | tf_op jit(solution)/shard_map/ppermute | solution.py:13
  50.4 6.7 %collective-permute-start.27 = (bf16[1,128,512]{2,1,0:T(8,128)(2,1)}, bf16[1,128,512]{2,1,0:T(8,128)(2,1)S(1)}, u32[]{:S(2)}, u32[]{:S(2)}) collective-permute-start(bf16[1,128,512]{2,1,0:T(8,128)(2,1)} %copy-done.4), channel_id=1, source_target_pairs={{0,1},{1,0},{2,3},{3,2},{4,5},{5,4},{6,7},{7,6},{8,9},{9,8},{10,11... | collective-permute-start | bytes 393224 | tf_op jit(solution)/shard_map/ppermute | solution.py:13
  66.2 3.8 %collective-permute-start.34 = (bf16[2,128,512]{2,1,0:T(8,128)(2,1)}, bf16[2,128,512]{2,1,0:T(8,128)(2,1)S(1)}, u32[]{:S(2)}, u32[]{:S(2)}) collective-permute-start(bf16[2,128,512]{2,1,0:T(8,128)(2,1)} %get-tuple-element.125.refs_6_), channel_id=1, source_target_pairs={{0,1},{1,0},{2,3},{3,2},{4,5},{5,4},{6,7},{7,6},{8,9},{9,8},{10,11... | collective-permute-start | bytes 786440 | tf_op jit(solution)/shard_map/ppermute | solution.py:13
  66.3 12.4 %collective-permute-start.29 = (bf16[2,128,512]{2,1,0:T(8,128)(2,1)S(1)}, bf16[2,128,512]{2,1,0:T(8,128)(2,1)S(1)}, u32[]{:S(2)}, u32[]{:S(2)}) collective-permute-start(bf16[2,128,512]{2,1,0:T(8,128)(2,1)S(1)} %get-tuple-element.117), channel_id=1, source_target_pairs={{0,2},{1,3},{2,0},{3,1},{4,6},{5,7},{6,4},{7,5},{8,10},{9,11},{10,... | collective-permute-start | bytes 786440 | tf_op jit(solution)/shard_map/ppermute | solution.py:13
  66.8 5.7 %collective-permute-start.35 = (bf16[2,128,512]{2,1,0:T(8,128)(2,1)}, bf16[2,128,512]{2,1,0:T(8,128)(2,1)S(1)}, u32[]{:S(2)}, u32[]{:S(2)}) collective-permute-start(bf16[2,128,512]{2,1,0:T(8,128)(2,1)} %get-tuple-element.126.refs_8_), channel_id=1, source_target_pairs={{0,1},{1,0},{2,3},{3,2},{4,5},{5,4},{6,7},{7,6},{8,9},{9,8},{10,11... | collective-permute-start | bytes 786440 | tf_op jit(solution)/shard_map/ppermute | solution.py:13
  67.2 14.8 %collective-permute-start.30 = (bf16[2,128,512]{2,1,0:T(8,128)(2,1)S(1)}, bf16[2,128,512]{2,1,0:T(8,128)(2,1)S(1)}, u32[]{:S(2)}, u32[]{:S(2)}) collective-permute-start(bf16[2,128,512]{2,1,0:T(8,128)(2,1)S(1)} %get-tuple-element.118), channel_id=1, source_target_pairs={{0,4},{1,5},{2,6},{3,7},{4,0},{5,1},{6,2},{7,3},{8,12},{9,13},{10,... | collective-permute-start | bytes 786440 | tf_op jit(solution)/shard_map/ppermute | solution.py:13
  68.0 19.7 %collective-permute-start.31 = (bf16[2,128,512]{2,1,0:T(8,128)(2,1)S(1)}, bf16[2,128,512]{2,1,0:T(8,128)(2,1)S(1)}, u32[]{:S(2)}, u32[]{:S(2)}) collective-permute-start(bf16[2,128,512]{2,1,0:T(8,128)(2,1)S(1)} %get-tuple-element.119), channel_id=1, source_target_pairs={{0,6},{1,7},{2,4},{3,5},{4,2},{5,3},{6,0},{7,1},{8,14},{9,15},{10,... | collective-permute-start | bytes 786440 | tf_op jit(solution)/shard_map/ppermute | solution.py:13
  70.0 18.8 %collective-permute-start.43 = (bf16[1,256,512]{2,1,0:T(8,128)(2,1)S(1)}, bf16[1,256,512]{2,1,0:T(8,128)(2,1)S(1)}, u32[]{:S(2)}, u32[]{:S(2)}) collective-permute-start(bf16[1,256,512]{2,1,0:T(8,128)(2,1)S(1)} %get-tuple-element.140), channel_id=1, source_target_pairs={{0,8},{1,9},{2,10},{3,11},{4,12},{5,13},{6,14},{7,15},{8,0},{9,1},... | collective-permute-start | bytes 786440 | tf_op jit(solution)/shard_map/ppermute | solution.py:13
  87.7 3.0 %collective-permute-start.40 = (bf16[2,128,512]{2,1,0:T(8,128)(2,1)S(1)}, bf16[2,128,512]{2,1,0:T(8,128)(2,1)S(1)}, u32[]{:S(2)}, u32[]{:S(2)}) collective-permute-start(bf16[2,128,512]{2,1,0:T(8,128)(2,1)S(1)} %get-tuple-element.136.refs_4_), channel_id=1, source_target_pairs={{0,1},{1,0},{2,3},{3,2},{4,5},{5,4},{6,7},{7,6},{8,9},{9,8},{10,11... | collective-permute-start | bytes 786440 | tf_op jit(solution)/shard_map/ppermute | solution.py:13
  88.2 4.0 %collective-permute-start.41 = (bf16[2,128,512]{2,1,0:T(8,128)(2,1)S(1)}, bf16[2,128,512]{2,1,0:T(8,128)(2,1)S(1)}, u32[]{:S(2)}, u32[]{:S(2)}) collective-permute-start(bf16[2,128,512]{2,1,0:T(8,128)(2,1)S(1)} %get-tuple-element.137.refs_6_), channel_id=1, source_target_pairs={{0,1},{1,0},{2,3},{3,2},{4,5},{5,4},{6,7},{7,6},{8,9},{9,8},{10,11... | collective-permute-start | bytes 786440 | tf_op jit(solution)/shard_map/ppermute | solution.py:13
  88.2 4.0 %collective-permute-start.42 = (bf16[2,128,512]{2,1,0:T(8,128)(2,1)S(1)}, bf16[2,128,512]{2,1,0:T(8,128)(2,1)S(1)}, u32[]{:S(2)}, u32[]{:S(2)}) collective-permute-start(bf16[2,128,512]{2,1,0:T(8,128)(2,1)S(1)} %get-tuple-element.138.refs_8_), channel_id=1, source_target_pairs={{0,1},{1,0},{2,3},{3,2},{4,5},{5,4},{6,7},{7,6},{8,9},{9,8},{10,11... | collective-permute-start | bytes 786440 | tf_op jit(solution)/shard_map/ppermute | solution.py:13
  88.7 8.8 %collective-permute-start.36 = (bf16[2,128,512]{2,1,0:T(8,128)(2,1)S(1)}, bf16[2,128,512]{2,1,0:T(8,128)(2,1)S(1)}, u32[]{:S(2)}, u32[]{:S(2)}) collective-permute-start(bf16[2,128,512]{2,1,0:T(8,128)(2,1)S(1)} %get-tuple-element.129), channel_id=1, source_target_pairs={{0,2},{1,3},{2,0},{3,1},{4,6},{5,7},{6,4},{7,5},{8,10},{9,11},{10,... | collective-permute-start | bytes 786440 | tf_op jit(solution)/shard_map/ppermute | solution.py:13
  89.3 9.8 %collective-permute-start.37 = (bf16[2,128,512]{2,1,0:T(8,128)(2,1)S(1)}, bf16[2,128,512]{2,1,0:T(8,128)(2,1)S(1)}, u32[]{:S(2)}, u32[]{:S(2)}) collective-permute-start(bf16[2,128,512]{2,1,0:T(8,128)(2,1)S(1)} %get-tuple-element.130), channel_id=1, source_target_pairs={{0,4},{1,5},{2,6},{3,7},{4,0},{5,1},{6,2},{7,3},{8,12},{9,13},{10,... | collective-permute-start | bytes 786440 | tf_op jit(solution)/shard_map/ppermute | solution.py:13
  90.7 21.0 %collective-permute-start.38 = (bf16[2,128,512]{2,1,0:T(8,128)(2,1)S(1)}, bf16[2,128,512]{2,1,0:T(8,128)(2,1)S(1)}, u32[]{:S(2)}, u32[]{:S(2)}) collective-permute-start(bf16[2,128,512]{2,1,0:T(8,128)(2,1)S(1)} %get-tuple-element.131), channel_id=1, source_target_pairs={{0,6},{1,7},{2,4},{3,5},{4,2},{5,3},{6,0},{7,1},{8,14},{9,15},{10,... | collective-permute-start | bytes 786440 | tf_op jit(solution)/shard_map/ppermute | solution.py:13
  94.8 17.5 %collective-permute-start.52 = (bf16[1,64,512]{2,1,0:T(8,128)(2,1)S(1)}, bf16[1,64,512]{2,1,0:T(8,128)(2,1)S(1)}, u32[]{:S(2)}, u32[]{:S(2)}) collective-permute-start(bf16[1,64,512]{2,1,0:T(8,128)(2,1)S(1)} %get-tuple-element.152), channel_id=1, source_target_pairs={{0,2},{1,3},{2,0},{3,1},{4,6},{5,7},{6,4},{7,5},{8,10},{9,11},{10,... | collective-permute-start | bytes 196616 | tf_op jit(solution)/shard_map/ppermute | solution.py:13
  95.4 17.4 %collective-permute-start.53 = (bf16[1,64,512]{2,1,0:T(8,128)(2,1)S(1)}, bf16[1,64,512]{2,1,0:T(8,128)(2,1)S(1)}, u32[]{:S(2)}, u32[]{:S(2)}) collective-permute-start(bf16[1,64,512]{2,1,0:T(8,128)(2,1)S(1)} %get-tuple-element.153), channel_id=1, source_target_pairs={{0,4},{1,5},{2,6},{3,7},{4,0},{5,1},{6,2},{7,3},{8,12},{9,13},{10,... | collective-permute-start | bytes 196616 | tf_op jit(solution)/shard_map/ppermute | solution.py:13
  97.6 15.6 %collective-permute-start.54 = (bf16[1,64,512]{2,1,0:T(8,128)(2,1)S(1)}, bf16[1,64,512]{2,1,0:T(8,128)(2,1)S(1)}, u32[]{:S(2)}, u32[]{:S(2)}) collective-permute-start(bf16[1,64,512]{2,1,0:T(8,128)(2,1)S(1)} %get-tuple-element.154), channel_id=1, source_target_pairs={{0,6},{1,7},{2,4},{3,5},{4,2},{5,3},{6,0},{7,1},{8,14},{9,15},{10,... | collective-permute-start | bytes 196616 | tf_op jit(solution)/shard_map/ppermute | solution.py:13
  99.1 24.5 %collective-permute-start.51 = (bf16[2,256,512]{2,1,0:T(8,128)(2,1)}, bf16[2,256,512]{2,1,0:T(8,128)(2,1)S(1)}, u32[]{:S(2)}, u32[]{:S(2)}) collective-permute-start(bf16[2,256,512]{2,1,0:T(8,128)(2,1)} %get-tuple-element.151), channel_id=1, source_target_pairs={{0,8},{1,9},{2,10},{3,11},{4,12},{5,13},{6,14},{7,15},{8,0},{9,1},... | collective-permute-start | bytes 1572872 | tf_op jit(solution)/shard_map/ppermute | solution.py:13
  112.3 4.7 %collective-permute-start.47 = (bf16[2,128,512]{2,1,0:T(8,128)(2,1)S(1)}, bf16[2,128,512]{2,1,0:T(8,128)(2,1)S(1)}, u32[]{:S(2)}, u32[]{:S(2)}) collective-permute-start(bf16[2,128,512]{2,1,0:T(8,128)(2,1)S(1)} %get-tuple-element.146.refs_2_), channel_id=1, source_target_pairs={{0,1},{1,0},{2,3},{3,2},{4,5},{5,4},{6,7},{7,6},{8,9},{9,8},{10,11... | collective-permute-start | bytes 786440 | tf_op jit(solution)/shard_map/ppermute | solution.py:13
  112.3 5.9 %collective-permute-start.48 = (bf16[2,128,512]{2,1,0:T(8,128)(2,1)S(1)}, bf16[2,128,512]{2,1,0:T(8,128)(2,1)S(1)}, u32[]{:S(2)}, u32[]{:S(2)}) collective-permute-start(bf16[2,128,512]{2,1,0:T(8,128)(2,1)S(1)} %get-tuple-element.147.refs_4_), channel_id=1, source_target_pairs={{0,1},{1,0},{2,3},{3,2},{4,5},{5,4},{6,7},{7,6},{8,9},{9,8},{10,11... | collective-permute-start | bytes 786440 | tf_op jit(solution)/shard_map/ppermute | solution.py:13
  112.8 5.4 %collective-permute-start.49 = (bf16[2,128,512]{2,1,0:T(8,128)(2,1)S(1)}, bf16[2,128,512]{2,1,0:T(8,128)(2,1)S(1)}, u32[]{:S(2)}, u32[]{:S(2)}) collective-permute-start(bf16[2,128,512]{2,1,0:T(8,128)(2,1)S(1)} %get-tuple-element.148.refs_6_), channel_id=1, source_target_pairs={{0,1},{1,0},{2,3},{3,2},{4,5},{5,4},{6,7},{7,6},{8,9},{9,8},{10,11... | collective-permute-start | bytes 786440 | tf_op jit(solution)/shard_map/ppermute | solution.py:13
  113.8 7.5 %collective-permute-start.50 = (bf16[2,128,512]{2,1,0:T(8,128)(2,1)S(1)}, bf16[2,128,512]{2,1,0:T(8,128)(2,1)S(1)}, u32[]{:S(2)}, u32[]{:S(2)}) collective-permute-start(bf16[2,128,512]{2,1,0:T(8,128)(2,1)S(1)} %get-tuple-element.149.refs_8_), channel_id=1, source_target_pairs={{0,1},{1,0},{2,3},{3,2},{4,5},{5,4},{6,7},{7,6},{8,9},{9,8},{10,11... | collective-permute-start | bytes 786440 | tf_op jit(solution)/shard_map/ppermute | solution.py:13
  117.0 12.7 %collective-permute-start.44 = (bf16[1,128,512]{2,1,0:T(8,128)(2,1)}, bf16[1,128,512]{2,1,0:T(8,128)(2,1)S(1)}, u32[]{:S(2)}, u32[]{:S(2)}) collective-permute-start(bf16[1,128,512]{2,1,0:T(8,128)(2,1)} %copy-done.22), channel_id=1, source_target_pairs={{0,2},{1,3},{2,0},{3,1},{4,6},{5,7},{6,4},{7,5},{8,10},{9,11},{10,... | collective-permute-start | bytes 393224 | tf_op jit(solution)/shard_map/ppermute | solution.py:13
  118.2 11.5 %collective-permute-start.45 = (bf16[1,128,512]{2,1,0:T(8,128)(2,1)}, bf16[1,128,512]{2,1,0:T(8,128)(2,1)S(1)}, u32[]{:S(2)}, u32[]{:S(2)}) collective-permute-start(bf16[1,128,512]{2,1,0:T(8,128)(2,1)} %copy-done.23), channel_id=1, source_target_pairs={{0,4},{1,5},{2,6},{3,7},{4,0},{5,1},{6,2},{7,3},{8,12},{9,13},{10,... | collective-permute-start | bytes 393224 | tf_op jit(solution)/shard_map/ppermute | solution.py:13
  118.9 12.1 %collective-permute-start.46 = (bf16[1,128,512]{2,1,0:T(8,128)(2,1)}, bf16[1,128,512]{2,1,0:T(8,128)(2,1)S(1)}, u32[]{:S(2)}, u32[]{:S(2)}) collective-permute-start(bf16[1,128,512]{2,1,0:T(8,128)(2,1)} %copy-done.24), channel_id=1, source_target_pairs={{0,6},{1,7},{2,4},{3,5},{4,2},{5,3},{6,0},{7,1},{8,14},{9,15},{10,... | collective-permute-start | bytes 393224 | tf_op jit(solution)/shard_map/ppermute | solution.py:13
  122.0 37.6 %collective-permute-start.59 = (bf16[2,256,512]{2,1,0:T(8,128)(2,1)}, bf16[2,256,512]{2,1,0:T(8,128)(2,1)S(1)}, u32[]{:S(2)}, u32[]{:S(2)}) collective-permute-start(bf16[2,256,512]{2,1,0:T(8,128)(2,1)} %copy-done.31), channel_id=1, source_target_pairs={{0,8},{1,9},{2,10},{3,11},{4,12},{5,13},{6,14},{7,15},{8,0},{9,1},... | collective-permute-start | bytes 1572872 | tf_op jit(solution)/shard_map/ppermute | solution.py:13
  132.6 43.9 %collective-permute-start.64 = (bf16[2,256,512]{2,1,0:T(8,128)(2,1)S(1)}, bf16[2,256,512]{2,1,0:T(8,128)(2,1)S(1)}, u32[]{:S(2)}, u32[]{:S(2)}) collective-permute-start(bf16[2,256,512]{2,1,0:T(8,128)(2,1)S(1)} %get-tuple-element.169), channel_id=1, source_target_pairs={{0,8},{1,9},{2,10},{3,11},{4,12},{5,13},{6,14},{7,15},{8,0},{9,1},... | collective-permute-start | bytes 1572872 | tf_op jit(solution)/shard_map/ppermute | solution.py:13
  135.0 4.7 %collective-permute-start.58 = (bf16[1,128,512]{2,1,0:T(8,128)(2,1)S(1)}, bf16[1,128,512]{2,1,0:T(8,128)(2,1)S(1)}, u32[]{:S(2)}, u32[]{:S(2)}) collective-permute-start(bf16[1,128,512]{2,1,0:T(8,128)(2,1)S(1)} %get-tuple-element.159.refs_8_), channel_id=1, source_target_pairs={{0,1},{1,0},{2,3},{3,2},{4,5},{5,4},{6,7},{7,6},{8,9},{9,8},{10,11... | collective-permute-start | bytes 393224 | tf_op jit(solution)/shard_map/ppermute | solution.py:13
  135.8 5.6 %collective-permute-start.60 = (bf16[2,64,512]{2,1,0:T(8,128)(2,1)S(1)}, bf16[2,64,512]{2,1,0:T(8,128)(2,1)S(1)}, u32[]{:S(2)}, u32[]{:S(2)}) collective-permute-start(bf16[2,64,512]{2,1,0:T(8,128)(2,1)S(1)} %get-tuple-element.163), channel_id=1, source_target_pairs={{0,2},{1,3},{2,0},{3,1},{4,6},{5,7},{6,4},{7,5},{8,10},{9,11},{10,... | collective-permute-start | bytes 393224 | tf_op jit(solution)/shard_map/ppermute | solution.py:13
  136.5 14.2 %collective-permute-start.61 = (bf16[2,64,512]{2,1,0:T(8,128)(2,1)S(1)}, bf16[2,64,512]{2,1,0:T(8,128)(2,1)S(1)}, u32[]{:S(2)}, u32[]{:S(2)}) collective-permute-start(bf16[2,64,512]{2,1,0:T(8,128)(2,1)S(1)} %get-tuple-element.164), channel_id=1, source_target_pairs={{0,4},{1,5},{2,6},{3,7},{4,0},{5,1},{6,2},{7,3},{8,12},{9,13},{10,... | collective-permute-start | bytes 393224 | tf_op jit(solution)/shard_map/ppermute | solution.py:13
  139.6 13.2 %collective-permute-start.62 = (bf16[2,64,512]{2,1,0:T(8,128)(2,1)S(1)}, bf16[2,64,512]{2,1,0:T(8,128)(2,1)S(1)}, u32[]{:S(2)}, u32[]{:S(2)}) collective-permute-start(bf16[2,64,512]{2,1,0:T(8,128)(2,1)S(1)} %get-tuple-element.165), channel_id=1, source_target_pairs={{0,6},{1,7},{2,4},{3,5},{4,2},{5,3},{6,0},{7,1},{8,14},{9,15},{10,... | collective-permute-start | bytes 393224 | tf_op jit(solution)/shard_map/ppermute | solution.py:13
  162.4 5.0 %collective-permute-start.65 = (bf16[2,64,512]{2,1,0:T(8,128)(2,1)S(1)}, bf16[2,64,512]{2,1,0:T(8,128)(2,1)S(1)}, u32[]{:S(2)}, u32[]{:S(2)}) collective-permute-start(bf16[2,64,512]{2,1,0:T(8,128)(2,1)S(1)} %get-tuple-element.171), channel_id=1, source_target_pairs={{0,2},{1,3},{2,0},{3,1},{4,6},{5,7},{6,4},{7,5},{8,10},{9,11},{10,... | collective-permute-start | bytes 393224 | tf_op jit(solution)/shard_map/ppermute | solution.py:13
  163.9 9.0 %collective-permute-start.66 = (bf16[2,64,512]{2,1,0:T(8,128)(2,1)S(1)}, bf16[2,64,512]{2,1,0:T(8,128)(2,1)S(1)}, u32[]{:S(2)}, u32[]{:S(2)}) collective-permute-start(bf16[2,64,512]{2,1,0:T(8,128)(2,1)S(1)} %get-tuple-element.172), channel_id=1, source_target_pairs={{0,4},{1,5},{2,6},{3,7},{4,0},{5,1},{6,2},{7,3},{8,12},{9,13},{10,... | collective-permute-start | bytes 393224 | tf_op jit(solution)/shard_map/ppermute | solution.py:13
  163.9 12.2 %collective-permute-start.67 = (bf16[2,64,512]{2,1,0:T(8,128)(2,1)S(1)}, bf16[2,64,512]{2,1,0:T(8,128)(2,1)S(1)}, u32[]{:S(2)}, u32[]{:S(2)}) collective-permute-start(bf16[2,64,512]{2,1,0:T(8,128)(2,1)S(1)} %get-tuple-element.173), channel_id=1, source_target_pairs={{0,6},{1,7},{2,4},{3,5},{4,2},{5,3},{6,0},{7,1},{8,14},{9,15},{10,... | collective-permute-start | bytes 393224 | tf_op jit(solution)/shard_map/ppermute | solution.py:13
  166.0 15.5 %collective-permute-start.63 = (bf16[1,256,512]{2,1,0:T(8,128)(2,1)S(1)}, bf16[1,256,512]{2,1,0:T(8,128)(2,1)S(1)}, u32[]{:S(2)}, u32[]{:S(2)}) collective-permute-start(bf16[1,256,512]{2,1,0:T(8,128)(2,1)S(1)} %get-tuple-element.167), channel_id=1, source_target_pairs={{0,8},{1,9},{2,10},{3,11},{4,12},{5,13},{6,14},{7,15},{8,0},{9,1},... | collective-permute-start | bytes 786440 | tf_op jit(solution)/shard_map/ppermute | solution.py:13
  177.9 5.1 %collective-permute-start.68 = (bf16[2,64,512]{2,1,0:T(8,128)(2,1)S(1)}, bf16[2,64,512]{2,1,0:T(8,128)(2,1)S(1)}, u32[]{:S(2)}, u32[]{:S(2)}) collective-permute-start(bf16[2,64,512]{2,1,0:T(8,128)(2,1)S(1)} %get-tuple-element.176), channel_id=1, source_target_pairs={{0,2},{1,3},{2,0},{3,1},{4,6},{5,7},{6,4},{7,5},{8,10},{9,11},{10,... | collective-permute-start | bytes 393224 | tf_op jit(solution)/shard_map/ppermute | solution.py:13
  179.3 6.2 %collective-permute-start.69 = (bf16[2,64,512]{2,1,0:T(8,128)(2,1)S(1)}, bf16[2,64,512]{2,1,0:T(8,128)(2,1)S(1)}, u32[]{:S(2)}, u32[]{:S(2)}) collective-permute-start(bf16[2,64,512]{2,1,0:T(8,128)(2,1)S(1)} %get-tuple-element.177), channel_id=1, source_target_pairs={{0,4},{1,5},{2,6},{3,7},{4,0},{5,1},{6,2},{7,3},{8,12},{9,13},{10,... | collective-permute-start | bytes 393224 | tf_op jit(solution)/shard_map/ppermute | solution.py:13
  179.3 8.4 %collective-permute-start.70 = (bf16[2,64,512]{2,1,0:T(8,128)(2,1)S(1)}, bf16[2,64,512]{2,1,0:T(8,128)(2,1)S(1)}, u32[]{:S(2)}, u32[]{:S(2)}) collective-permute-start(bf16[2,64,512]{2,1,0:T(8,128)(2,1)S(1)} %get-tuple-element.178), channel_id=1, source_target_pairs={{0,6},{1,7},{2,4},{3,5},{4,2},{5,3},{6,0},{7,1},{8,14},{9,15},{10,... | collective-permute-start | bytes 393224 | tf_op jit(solution)/shard_map/ppermute | solution.py:13
  189.1 5.0 %collective-permute-start.71 = (bf16[1,64,512]{2,1,0:T(8,128)(2,1)S(1)}, bf16[1,64,512]{2,1,0:T(8,128)(2,1)S(1)}, u32[]{:S(2)}, u32[]{:S(2)}) collective-permute-start(bf16[1,64,512]{2,1,0:T(8,128)(2,1)S(1)} %get-tuple-element.181), channel_id=1, source_target_pairs={{0,2},{1,3},{2,0},{3,1},{4,6},{5,7},{6,4},{7,5},{8,10},{9,11},{10,... | collective-permute-start | bytes 196616 | tf_op jit(solution)/shard_map/ppermute | solution.py:13
  189.8 4.3 %collective-permute-start.72 = (bf16[1,64,512]{2,1,0:T(8,128)(2,1)S(1)}, bf16[1,64,512]{2,1,0:T(8,128)(2,1)S(1)}, u32[]{:S(2)}, u32[]{:S(2)}) collective-permute-start(bf16[1,64,512]{2,1,0:T(8,128)(2,1)S(1)} %get-tuple-element.182), channel_id=1, source_target_pairs={{0,4},{1,5},{2,6},{3,7},{4,0},{5,1},{6,2},{7,3},{8,12},{9,13},{10,... | collective-permute-start | bytes 196616 | tf_op jit(solution)/shard_map/ppermute | solution.py:13
  190.0 5.6 %collective-permute-start.73 = (bf16[1,64,512]{2,1,0:T(8,128)(2,1)S(1)}, bf16[1,64,512]{2,1,0:T(8,128)(2,1)S(1)}, u32[]{:S(2)}, u32[]{:S(2)}) collective-permute-start(bf16[1,64,512]{2,1,0:T(8,128)(2,1)S(1)} %get-tuple-element.183), channel_id=1, source_target_pairs={{0,6},{1,7},{2,4},{3,5},{4,2},{5,3},{6,0},{7,1},{8,14},{9,15},{10,... | collective-permute-start | bytes 196616 | tf_op jit(solution)/shard_map/ppermute | solution.py:13
  (43 other events, 230.7 us)
where the time goes:
time: 198 us; the launch traced here: 197 us
  waiting for transfers between devices  77.7 us (39%)
  starting transfers between devices  62.8 us (32%)
  Pallas kernels  38.6 us (19%)
  local copies, waits for them, and re-layouts  11.4 us (6%)
  matrix products  3.3 us (2%)
  other arithmetic  2.58 us (1%)
    ppermute x74, waiting for transfers between devices, swap(): return lax.ppermute(x, 'blk', [(i, i ^ bits) for i in range(n)])  77.7 us
    ppermute x74, starting transfers between devices, swap(): return lax.ppermute(x, 'blk', [(i, i ^ bits) for i in range(n)])  62.8 us
    pallas_call x17, Pallas kernels, call(): pl.pallas_call(body, out_shape=[jax.ShapeDtypeStruct(shape, kind) for sha...  38.6 us
    unnamed x66, local copies, waits for them, and re-layouts  5.97 us
  transfers between devices with their start and end apart: 74, of which 30 were waited for; matrix products, arithmetic and copies ran while one was open for 5% of the time, Pallas kernels for 16%

commit v1 on v0

v1 whole, which is shorter than its diff:
```python
import jax
import jax.numpy as jnp
from jax import lax
from jax.experimental import pallas as pl
from jax.experimental.pallas import tpu as pltpu
from jax.sharding import PartitionSpec as P

MIB = 1024 * 1024
LONG = 10**11


def swap(x, bits):
    n = lax.axis_size("blk")
    return lax.ppermute(x, "blk", [(i, i ^ bits) for i in range(n)])


class Step:
    def __init__(self, body, outs, ins, scratch=(), aliases=None, work=0):
        self.body, self.outs, self.ins, self.work = body, outs, ins, work
        self.scratch, self.aliases = list(scratch), aliases or {}


def call(steps, tokens=(), room=20):
    ins = [x for step in steps for x in step.ins]
    outs = [x for step in steps for x in step.outs]
    scratch = [x for step in steps for x in step.scratch]
    aliases, first_in, first_out = {}, 0, 0
    for step in steps:
        aliases.update({first_in + i: first_out + o for i, o in step.aliases.items()})
        first_in += len(step.ins)
        first_out += len(step.outs)

    def body(*refs):
        left = [list(refs[: len(ins)]), list(refs[len(ins) + len(tokens) :])]
        left = [left[0], left[1][: len(outs)], left[1][len(outs) :]]

        def take(which, amount):
            taken, left[which] = left[which][:amount], left[which][amount:]
            return taken

        running = [
            step.body(
                take(0, len(step.ins)), take(1, len(step.outs)), take(2, len(step.scratch))
            )
            for step in steps
        ]
        for _ in range(3):
            for each in running:
                next(each, None)

    results = pl.pallas_call(
        body,
        out_shape=[jax.ShapeDtypeStruct(shape, kind) for shape, kind, _ in outs],
        in_specs=[pl.BlockSpec(memory_space=space) for _, space in ins]
        + [pl.BlockSpec(memory_space=pl.ANY)] * len(tokens),
        out_specs=[pl.BlockSpec(memory_space=space) for _, _, space in outs],
        scratch_shapes=scratch,
        input_output_aliases=aliases,
        compiler_params=pltpu.CompilerParams(vmem_limit_bytes=room * MIB),
        cost_estimate=pl.CostEstimate(
            flops=sum(step.work for step in steps), bytes_accessed=0, transcendentals=0
        ),
    )(*[x for x, _ in ins], *tokens)
    results = list(results)
    split = []
    for step in steps:
        split.append(results[: len(step.outs)])
        results = results[len(step.outs) :]
    return split


def inside(xs):
    return [(x, pltpu.VMEM) for x in xs]


def outside(xs):
    return [(x, pl.ANY) for x in xs]


def scalar(x):
    return [(x.reshape(-1).astype(jnp.int32), pltpu.SMEM)]


def plan(slab_count, group):
    full = slab_count // (2 * group)
    return [1] if full < 2 else [2] + [1] * (full - 1) + [2]


def after(xs, tokens, work=0):
    def body(ins, outs, scratch):
        yield

    outs = [(x.shape, x.dtype, pl.ANY) for x in xs]
    step = Step(body, outs, outside(xs), aliases={i: i for i in range(len(xs))}, work=work)
    return call([step], tokens)[0]


def first_transform(slabs, blocks, me, core, firsts, cuts, group, work=0):
    n = len(blocks)
    rows, cols = blocks[0].shape
    depth, width = slabs.shape[1:]
    amounts = [group if cut == 2 else 2 * group for cut in cuts]
    begins = [sum(amounts[:i]) for i in range(len(cuts))]

    def body(ins, outs, scratch):
        me_now, core_now, place, slab_hbm, *held = ins
        panel, buffer, sems = scratch
        copies = [
            [
                pltpu.make_async_copy(
                    slab_hbm.at[place[begins[i] + j]], buffer.at[i % 2, j], sems.at[i % 2, j]
                )
                for j in range(amount)
            ]
            for i, amount in enumerate(amounts)
        ]
        for batch in copies[:2]:
            for copy in batch:
                copy.start()
        yield
        for v in range(n):
            first = pl.multiple_of((me_now[0] ^ v) * rows, rows)
            panel[pl.ds(first, rows), :] = held[v][...]
        for i, amount in enumerate(amounts):
            for copy in copies[i]:
                copy.wait()
            result = jnp.dot(
                buffer[i % 2, :amount].reshape(amount * depth, width),
                panel[...],
                preferred_element_type=jnp.float32,
            )
            result = result.astype(jnp.bfloat16).reshape(amount, depth, cols)
            kept, other = outs[2 * i : 2 * i + 2]
            if cuts[i] == 1:
                kept[...], other[...] = result[:group], result[group:]
            else:
                low, high = result[:, :, : cols // 2], result[:, :, cols // 2 :]

                @pl.when(core_now[0] == 0)
                def _(kept=kept, other=other, low=low, high=high):
                    kept[...], other[...] = low, high

                @pl.when(core_now[0] == 1)
                def _(kept=kept, other=other, low=low, high=high):
                    kept[...], other[...] = high, low

            for batch in copies[i + 2 : i + 3]:
                for copy in batch:
                    copy.start()

    return Step(
        body,
        [
            ((group, depth, cols // cut), jnp.bfloat16, pltpu.VMEM)
            for cut in cuts
            for _ in range(2)
        ],
        scalar(me) + scalar(core) + scalar(firsts) + [(slabs, pltpu.HBM)] + inside(blocks),
        [
            pltpu.VMEM((n * rows, cols), jnp.bfloat16),
            pltpu.VMEM((2, max(amounts), depth, width), jnp.bfloat16),
            pltpu.SemaphoreType.DMA((2, max(amounts))),
        ],
        work=work,
    )


def merge_cores(kept, came):
    group, depth, cols = kept.shape

    def body(ins, outs, scratch):
        yield
        for j in range(group):
            outs[j][:depth, :] = ins[0][j]
            outs[j][depth:, :] = ins[1][j]

    return Step(
        body, [((2 * depth, cols), jnp.bfloat16, pltpu.VMEM)] * group, inside([kept, came])
    )


def pick_rows(chosen, blocks, work):
    rows, width = blocks[0].shape
    listed = chosen.shape[0]
    amount = len(blocks)

    def body(ins, outs, scratch):
        chosen_ref, *held = ins
        buffer, sems = scratch
        copies = []
        for i in range(amount):
            target = buffer.at[pl.ds(i * rows, rows)]
            copies.append(pltpu.make_async_copy(held[i], target, sems.at[i]))
            copies[i].start()
        yield
        for i in range(0, amount, 2):
            copies[i].wait()
            copies[i + 1].wait()
            result = lax.dot_general(
                chosen_ref[...],
                buffer[i * rows : (i + 2) * rows, :],
                (((1,), (1,)), ((), ())),
                preferred_element_type=jnp.float32,
            )
            outs[0][:, i * rows : (i + 2) * rows] = result.astype(jnp.bfloat16)

    return Step(
        body,
        [((listed, rows * amount), jnp.bfloat16, pltpu.VMEM)],
        inside([chosen]) + outside(blocks),
        [
            pltpu.VMEM((rows * amount, width), jnp.bfloat16),
            pltpu.SemaphoreType.DMA((amount,)),
        ],
        work=work,
    )


def second_transform(picked, parts, side, work):
    rows, cols = parts[0].shape
    share = picked.shape[0] // 2

    def body(ins, outs, scratch):
        side_now, picked_ref, *held = ins
        far, near = outs
        yield
        here = pl.ds(pl.multiple_of(side_now[0] * share, share), share)
        there = pl.ds(pl.multiple_of((1 - side_now[0]) * share, share), share)

        def total(lines):
            return sum(
                jnp.dot(
                    picked_ref[lines, j * rows : (j + 1) * rows],
                    x[...],
                    preferred_element_type=jnp.float32,
                )
                for j, x in enumerate(held)
            )

        far[...] = total(there).astype(jnp.bfloat16)
        near[...] = total(here)

    return Step(
        body,
        [
            ((share, cols), jnp.bfloat16, pltpu.VMEM),
            ((share, cols), jnp.float32, pltpu.VMEM),
        ],
        scalar(side) + inside([picked] + parts),
        work=work,
    )


def add_sides(near, came, member, group, work):
    rows, cols = near.shape
    share = rows // group

    def body(ins, outs, scratch):
        member_now, near_ref, came_ref = ins
        yield
        for j in range(group):
            lines = pl.ds(pl.multiple_of((member_now[0] ^ j) * share, share), share)
            total = near_ref[lines, :] + came_ref[lines, :].astype(jnp.float32)
            outs[j][...] = total.astype(jnp.bfloat16)

    return Step(
        body,
        [((share, cols), jnp.bfloat16, pltpu.VMEM)] * group,
        scalar(member) + inside([near, came]),
        work=work,
    )


def for_other_core(held, core):
    group = len(held)
    share, cols = held[0].shape[0] // 2, held[0].shape[1]

    def body(ins, outs, scratch):
        core_now, *refs = ins
        yield
        lines = pl.ds(pl.multiple_of((1 - core_now[0]) * share, share), share)
        for j, x in enumerate(refs):
            outs[0][j] = x[lines, :]

    return Step(
        body,
        [((group, share, cols), jnp.bfloat16, pltpu.VMEM)],
        scalar(core) + inside(held),
    )


def scale(slab_count, angular, held, came, order, core, cuts):
    share, cols = angular.shape
    group = len(held[0])
    chunks = len(cuts)

    def body(ins, outs, scratch):
        place, core_now, angular_ref, *refs = ins
        mine, theirs, sems = scratch
        lines = pl.ds(pl.multiple_of(core_now[0] * share, share), share)
        copies = []
        for k, cut in enumerate(cuts):
            wide = pl.ds(0, cols // cut)
            pairs = [(refs[k * group + j].at[lines], mine.at[k, j, :, wide]) for j in range(group)]
            pairs.append((refs[chunks * group + k], theirs.at[k, :, :, wide]))
            for source, target in pairs:
                copies.append(pltpu.make_async_copy(source, target, sems.at[len(copies)]))
                copies[-1].start()
        yield
        first = 0
        for k, cut in enumerate(cuts):
            for copy in copies[k * (group + 1) : (k + 1) * (group + 1)]:
                copy.wait()
            for kind in range(2):
                source = core_now[0] if kind == 0 else 1 - core_now[0]
                lanes = slice(None)
                if cut == 2:
                    lanes = pl.ds(pl.multiple_of(source * (cols // 2), cols // 2), cols // 2)
                factor = angular_ref[:, lanes]
                for j in range(group):
                    slab = first + place[j] * (3 - cut) + (source if cut == 1 else 0)
                    x = (mine if kind == 0 else theirs)[k, j, :, : cols // cut]
                    value = factor * x.astype(jnp.float32)
                    outs[0][slab, :, lanes] = value.astype(jnp.bfloat16)
            first += group * (3 - cut)

    flat = [x for xs in held for x in xs]
    return Step(
        body,
        [((slab_count, share, cols), jnp.bfloat16, pltpu.VMEM)],
        scalar(order) + scalar(core) + inside([angular]) + outside(flat + came),
        [
            pltpu.VMEM((chunks, group, share, cols), jnp.bfloat16),
            pltpu.VMEM((chunks, group, share, cols), jnp.bfloat16),
            pltpu.SemaphoreType.DMA((chunks * (group + 1),)),
        ],
    )


def on_device(slabs, orbitals, channel_orbital, channel_target, coupling):
    n = lax.axis_size("blk")
    group = n // 4
    segment_now = lax.axis_index("segment")
    me = lax.axis_index("blk")
    core = me % 2
    member = (me // 2) % group
    side = me // (2 * group)
    channels = channel_orbital.shape[0]
    share = channels // n
    half_cols = channels // lax.axis_size("segment")
    slab_count = slabs.shape[0]
    splines = jnp.arange(orbitals.shape[1], dtype=jnp.int32)

    picks = lax.dynamic_slice_in_dim(channel_orbital, segment_now * half_cols, half_cols)
    onehot = (splines[:, None] == picks[None, :]).astype(jnp.bfloat16)
    mine = jnp.dot(orbitals, onehot, preferred_element_type=jnp.float32).astype(jnp.bfloat16)
    gathered = {0: mine}
    rows_of = {0: orbitals}
    bit = n // 2
    while bit:
        for v, x in list(gathered.items()):
            gathered[v ^ bit] = swap(x, bit)
        if bit == n // 2:
            rows_of[n // 4] = swap(orbitals, n // 4)
            gathered[bit] = after([gathered[bit]], [rows_of[n // 4]])[0]
        bit //= 2
    column_blocks = [gathered[v] for v in range(n)]

    kinds = jnp.arange(coupling.shape[0], dtype=jnp.int32)
    targets_rows = lax.dynamic_slice_in_dim(channel_target, me * share, share)
    targets_cols = lax.dynamic_slice_in_dim(channel_target, segment_now * half_cols, half_cols)
    onehot_rows = (targets_rows[:, None] == kinds[None, :]).astype(jnp.float32)
    onehot_cols = (kinds[:, None] == targets_cols[None, :]).astype(jnp.float32)
    angular = (
        jnp.dot(
            jnp.dot(
                onehot_rows, coupling.astype(jnp.float32), precision=lax.Precision.HIGHEST
            ),
            onehot_cols,
            precision=lax.Precision.HIGHEST,
        )
        / 16.0
    )

    order = member ^ jnp.arange(group, dtype=jnp.int32)
    cuts = plan(slab_count, group)
    last = len(cuts) - 1
    starts = [sum(group * (3 - cut) for cut in cuts[:k]) for k in range(last + 1)]
    kept, other, own, came, near, across, sums, held = {}, {}, {}, {}, {}, {}, {}, {}

    def transform(ks, tokens, work=0, trade=True):
        firsts = []
        for k in ks:
            if cuts[k] == 2:
                firsts.append(starts[k] + order)
            else:
                firsts += [starts[k] + 2 * order + core, starts[k] + 2 * order + 1 - core]
        step = first_transform(
            slabs,
            column_blocks,
            me,
            core,
            jnp.concatenate(firsts),
            [cuts[k] for k in ks],
            group,
            work,
        )
        flat = call([step], tokens, 46)[0]
        for i, k in enumerate(ks):
            kept[k], other[k] = flat[2 * i : 2 * i + 2]
            if trade:
                other[k] = swap(other[k], 1)

    def merge(ks, tokens):
        steps = [merge_cores(kept[k], other[k]) for k in ks]
        for k, result in zip(ks, call(steps, tokens), strict=True):
            own[k] = result

    def send(xs):
        return [swap(xs[j], 2 * j) for j in range(1, group)]

    transform([0], [angular])
    merge([0], [])
    came[0] = send(own[0])
    bit = group // 2
    while bit > 1:
        for v, x in list(rows_of.items()):
            rows_of[v ^ bit] = swap(x, bit)
        bit //= 2
    clock = after([jnp.zeros((8, 128), jnp.float32)], [own[0][0]], LONG)[0]
    if last:
        transform(list(range(1, last + 1)), [clock], 0, False)
        clock = kept[last]
    arrived = [v for v in rows_of if v]
    ready = after(
        came[0] + [rows_of[v] for v in arrived] + [other[k] for k in range(1, last + 1)], [clock]
    )
    came[0], ready = ready[: group - 1], ready[group - 1 :]
    rows_of.update(zip(arrived, ready, strict=False))
    for k in range(1, last + 1):
        other[k] = swap(ready[len(arrived) + k - 1], 1)
    token = came[0][0]
    if last:
        merge([1], [token])
        came[1] = send(own[1])
    for v, x in list(rows_of.items()):
        rows_of[v ^ 1] = swap(x, 1)

    chosen = (channel_orbital[:, None] == splines[None, :]).astype(jnp.bfloat16)
    rows = [rows_of[2 * j + c] for j in range(group) for c in range(2)]
    picked = call([pick_rows(chosen, rows, LONG)], [token])[0][0]

    token = picked
    for k in range(last + 1):
        step = second_transform(picked, [own[k][0]] + came[k], side, LONG if k else 0)
        far, near[k] = call([step], [token])[0]
        across[k] = swap(far, n // 2)
        token = far
        if k == 0 and last > 1:
            merge(list(range(2, last + 1)), [token])
        if 0 < k < last:
            came[k + 1] = send([None] + after(own[k + 1][1:], [before]))
        before = far
        if k:
            late = held[k - 2][1:] if k > 1 else []
            sums[k - 1] = call(
                [add_sides(near[k - 1], across[k - 1], member, group, LONG)], [token] + late
            )[0]
            held[k - 1] = [sums[k - 1][0]] + send(sums[k - 1])
            token = sums[k - 1][0]
    clock = token
    final = {}
    for k in range(last):
        final[k] = swap(call([for_other_core(held[k], core)], [token])[0][0], 1)
    sums[last] = call([add_sides(near[last], across[last], member, group, 0)], [clock])[0]
    held[last] = [sums[last][0]] + send(sums[last])
    final[last] = swap(call([for_other_core(held[last], core)])[0][0], 1)
    ks = range(last + 1)
    step = scale(
        slab_count, angular, [held[k] for k in ks], [final[k] for k in ks], order, core, cuts
    )
    return call([step], (), 40)[0][0]


def solution(mesh):
    return jax.shard_map(
        on_device,
        mesh=mesh,
        in_specs=(P(None, "blk", None), P("blk", None), P(), P(), P()),
        out_specs=P(None, "blk", "segment"),
        check_vma=False,
    )
```

time: 198 us -> 188 us (0.949)
  local copies, waits for them, and re-layouts: 11.4 us -> 6.95 us
  starting transfers between devices: 62.8 us -> 60.3 us
  other arithmetic: 2.58 us -> 0.43 us
    concatenate x6 -> x0, other arithmetic: 2.56 us -> none  [the longest x1 2.22 us: all_rows(): return jnp.concatenate([pairs[j] for j in range(group)], axis=1)]
    ppermute x74 -> x67, starting transfers between devices: 62.8 us -> 60.3 us  [swap(): return lax.ppermute(x, 'blk', [(i, i ^ bits) for i in range(n)])]
    unnamed x66 -> x72, local copies, waits for them, and re-layouts: 5.97 us -> 4.59 us
    ppermute x74 -> x67, waiting for transfers between devices: 77.7 us -> 77 us  [swap(): return lax.ppermute(x, 'blk', [(i, i ^ bits) for i in range(n)])]
    pallas_call x17 -> x28, Pallas kernels: 38.6 us -> 39.1 us  [call(): pl.pallas_call(body, out_shape=[jax.ShapeDtypeStruct(shape, kind) for sha...]
  transfers between devices with their start and end apart: 74 -> 67, of which waited for: 30 -> 23; matrix products, arithmetic and copies ran while one was open for 5% -> 3% of each run, Pallas kernels for 16% -> 19%
where the time goes in v1:
time: 188 us; the launch traced here: 187 us
  waiting for transfers between devices  77 us (41%)
  starting transfers between devices  60.3 us (32%)
  Pallas kernels  39.1 us (21%)
  local copies, waits for them, and re-layouts  6.95 us (4%)
  matrix products  2.53 us (1%)
    ppermute x67, waiting for transfers between devices, swap(): return lax.ppermute(x, 'blk', [(i, i ^ bits) for i in range(n)])  77 us
    ppermute x67, starting transfers between devices, swap(): return lax.ppermute(x, 'blk', [(i, i ^ bits) for i in range(n)])  60.3 us
    pallas_call x28, Pallas kernels, call(): pl.pallas_call(body, out_shape=[jax.ShapeDtypeStruct(shape, kind) for sha...  39.1 us
    unnamed x72, local copies, waits for them, and re-layouts  4.59 us
  transfers between devices with their start and end apart: 67, of which 23 were waited for; matrix products, arithmetic and copies ran while one was open for 3% of the time, Pallas kernels for 19%

profile of v1, /device:TPU:0, one launch (start us, length us, event | category | flops | bytes accessed | tf_op | source)
XLA Modules:
  0.0 187.1 jit_solution(669688102160719996)
XLA Ops:
  0.0 3.0 %collective-permute-start.9 = (bf16[128,1024]{1,0:T(8,128)(2,1)}, bf16[128,1024]{1,0:T(8,128)(2,1)S(1)}, u32[]{:S(2)}, u32[]{:S(2)}) collective-permute-start(bf16[128,1024]{1,0:T(8,128)(2,1)} %refs_1_.1), channel_id=1, source_target_pairs={{0,4},{1,5},{2,6},{3,7},{4,0},{5,1},{6,2},{7,3},{8,12},{9,13},{10,... | collective-permute-start | bytes 786440 | tf_op jit(solution)/shard_map/ppermute | solution.py:14
  3.8 1.4 fusion.3.refs_4_
  5.2 2.7 %collective-permute-start.8 = (bf16[128,512]{1,0:T(8,128)(2,1)S(1)}, bf16[128,512]{1,0:T(8,128)(2,1)S(1)}, u32[]{:S(2)}, u32[]{:S(2)}) collective-permute-start(bf16[128,512]{1,0:T(8,128)(2,1)S(1)} %fusion.3.refs_4_), channel_id=1, source_target_pairs={{0,8},{1,9},{2,10},{3,11},{4,12},{5,13},{6,14},{7,15},{8,0},{9,1},... | collective-permute-start | bytes 393224 | tf_op jit(solution)/shard_map/ppermute | solution.py:14
  8.3 1.5 collective-permute-start.2
  11.4 1.4 collective-permute-done.8.refs_0_
  13.2 3.1 %collective-permute-start.13 = (bf16[128,512]{1,0:T(8,128)(2,1)S(1)}, bf16[128,512]{1,0:T(8,128)(2,1)S(1)}, u32[]{:S(2)}, u32[]{:S(2)}) collective-permute-start(bf16[128,512]{1,0:T(8,128)(2,1)S(1)} %shard_map.55.refs_12_), channel_id=1, source_target_pairs={{0,4},{1,5},{2,6},{3,7},{4,0},{5,1},{6,2},{7,3},{8,12},{9,13},{10,... | collective-permute-start | bytes 393224 | tf_op jit(solution)/shard_map/ppermute | solution.py:14
  17.2 1.6 collective-permute-start.6
  19.8 1.5 collective-permute-start.15
  21.5 1.0 collective-permute-done.6.refs_10_
  23.1 2.5 %collective-permute-done.11.refs_14_ = bf16[128,512]{1,0:T(8,128)(2,1)S(1)} collective-permute-done((bf16[128,512]{1,0:T(8,128)(2,1)S(1)}, bf16[128,512]{1,0:T(8,128)(2,1)S(1)}, u32[]{:S(2)}, u32[]{:S(2)}) %collective-permute-start.11) | collective-permute-done | bytes 131104 | tf_op jit(solution)/shard_map/ppermute | solution.py:14
  25.6 2.2 %collective-permute-done.15.refs_18_ = bf16[128,512]{1,0:T(8,128)(2,1)S(1)} collective-permute-done((bf16[128,512]{1,0:T(8,128)(2,1)S(1)}, bf16[128,512]{1,0:T(8,128)(2,1)S(1)}, u32[]{:S(2)}, u32[]{:S(2)}) %collective-permute-start.15) | collective-permute-done | bytes 131104 | tf_op jit(solution)/shard_map/ppermute | solution.py:14
  27.9 1.6 collective-permute-start.21
  29.5 3.5 %shard_map.56 = (bf16[4,128,256]{2,1,0:T(8,128)(2,1)S(1)}, bf16[4,128,256]{2,1,0:T(8,128)(2,1)S(1)}) custom-call(s32[1]{0:T(128)} %bitcast.3.refs_0_, s32[1]{0:T(128)} %bitcast.refs_1_.refs_0_, s32[4]{0:T(128)S(1)} %iota_xor_fusion.refs_2_.refs_0_, bf16[32,128,2048]{2,1,0:T(8,128)(2,1)} %refs_3_.3, bf16[128,512]{1,0:T(8,128)(2,1)S(1)} %fusion.3.refs_4_, ...), custom_call_target="tpu_custom_call" | custom-call | tf_op jit(solution)/shard_map/pallas_call | solution.py:51
  33.3 1.2 collective-permute-start.22
  34.6 1.3 collective-permute-start.18
  35.9 2.3 %collective-permute-start.20 = (bf16[256,256]{1,0:T(8,128)(2,1)S(1)}, bf16[256,256]{1,0:T(8,128)(2,1)S(1)}, u32[]{:S(2)}, u32[]{:S(2)}) collective-permute-start(bf16[256,256]{1,0:T(8,128)(2,1)S(1)} %get-tuple-element.88), channel_id=1, source_target_pairs={{0,6},{1,7},{2,4},{3,5},{4,2},{5,3},{6,0},{7,1},{8,14},{9,15},{10,... | collective-permute-start | bytes 393224 | tf_op jit(solution)/shard_map/ppermute | solution.py:14
  38.8 11.3 %shard_map.59 = (bf16[4,128,512]{2,1,0:T(8,128)(2,1)S(1)}, bf16[4,128,512]{2,1,0:T(8,128)(2,1)S(1)}, bf16[4,128,512]{2,1,0:T(8,128)(2,1)S(1)}, bf16[4,128,512]{2...) custom-call(s32[1]{0:T(128)} %bitcast.3.refs_0_, ...), custom_call_target="tpu_custom_call" | custom-call | tf_op jit(solution)/shard_map/pallas_call | solution.py:51
  56.7 1.1 shard_map.63
  58.4 1.2 collective-permute-start.28
  59.7 2.3 %collective-permute-start.30 = (bf16[256,512]{1,0:T(8,128)(2,1)S(1)}, bf16[256,512]{1,0:T(8,128)(2,1)S(1)}, u32[]{:S(2)}, u32[]{:S(2)}) collective-permute-start(bf16[256,512]{1,0:T(8,128)(2,1)S(1)} %get-tuple-element.108), channel_id=1, source_target_pairs={{0,6},{1,7},{2,4},{3,5},{4,2},{5,3},{6,0},{7,1},{8,14},{9,15},{10,... | collective-permute-start | bytes 786440 | tf_op jit(solution)/shard_map/ppermute | solution.py:14
  61.9 6.2 %shard_map.61.refs_1_.refs_6_ = bf16[1024,1024]{1,0:T(8,128)(2,1)S(1)} custom-call(bf16[1024,1024]{1,0:T(8,128)(2,1)S(1)} %fusion.refs_0_, bf16[128,1024]{1,0:T(8,128)(2,1)} %refs_1_.1, bf16[128,1024]{1,0:T(8,128)(2,1)} %collective-permute-done.refs_2_, bf16[128,1024]{1,0:T(8,128)(2,1)} %get-tuple-element.95.refs_3_, ...), custom_call_target="tpu_custom_call" | custom-call | flops 99999997952 | tf_op jit(solution)/shard_map/pallas_call | solution.py:51
  68.9 1.9 %collective-permute-start.26 = (bf16[512,256]{1,0:T(8,128)(2,1)S(1)}, bf16[512,256]{1,0:T(8,128)(2,1)S(1)}, u32[]{:S(2)}, u32[]{:S(2)}) collective-permute-start(bf16[512,256]{1,0:T(8,128)(2,1)S(1)} %get-tuple-element.102.refs_6_.refs_3_), channel_id=1, source_target_pairs={{0,8},{1,9},{2,10},{3,11},{4,12},{5,13},{6,14},{7,15},{8,0},{9,1},... | collective-permute-start | bytes 786440 | tf_op jit(solution)/shard_map/ppermute | solution.py:14
  70.8 1.0 shard_map.66
  71.8 1.2 collective-permute-start.38
  73.0 1.6 collective-permute-start.39
  75.3 1.7 collective-permute-done.30.refs_5_
  77.0 1.8 shard_map.64
  78.8 6.0 %collective-permute-done.26.refs_2_ = bf16[512,256]{1,0:T(8,128)(2,1)S(1)} collective-permute-done((bf16[512,256]{1,0:T(8,128)(2,1)S(1)}, bf16[512,256]{1,0:T(8,128)(2,1)S(1)}, u32[]{:S(2)}, u32[]{:S(2)}) %collective-permute-start.26) | collective-permute-done | bytes 262176 | tf_op jit(solution)/shard_map/ppermute | solution.py:14
  84.9 1.3 collective-permute-start.31
  86.1 8.2 %collective-permute-done.39.refs_4_ = bf16[256,512]{1,0:T(8,128)(2,1)} collective-permute-done((bf16[256,512]{1,0:T(8,128)(2,1)}, bf16[256,512]{1,0:T(8,128)(2,1)}, u32[]{:S(2)}, u32[]{:S(2)}) %collective-permute-start.39) | collective-permute-done | bytes 262176 | tf_op jit(solution)/shard_map/ppermute | solution.py:14
  94.3 5.4 %collective-permute-done.40.refs_5_ = bf16[256,512]{1,0:T(8,128)(2,1)} collective-permute-done((bf16[256,512]{1,0:T(8,128)(2,1)}, bf16[256,512]{1,0:T(8,128)(2,1)}, u32[]{:S(2)}, u32[]{:S(2)}) %collective-permute-start.40) | collective-permute-done | bytes 262176 | tf_op jit(solution)/shard_map/ppermute | solution.py:14
  99.8 2.6 %shard_map.68 = (bf16[512,512]{1,0:T(8,128)(2,1)}, f32[512,512]{1,0:T(8,128)S(1)}) custom-call(s32[1]{0:T(128)} %bitcast.2.refs_0_, bf16[1024,1024]{1,0:T(8,128)(2,1)S(1)} %shard_map.61.refs_1_.refs_6_, bf16[256,512]{1,0:T(8,128)(2,1)S(1)} %get-tuple-element.120.refs_2_, bf16[256,512]{1,0:T(8,128)(2,1)} %collective-permute-done.38.refs_3_, ...), custom_call_target="tpu_custom_call" | custom-call | flops 99999997952 | tf_op jit(solution)/shard_map/pallas_call | solution.py:51
  102.4 1.7 collective-permute-start.45
  104.1 1.4 collective-permute-start.46
  106.3 11.9 %collective-permute-done.34.refs_2_ = bf16[512,512]{1,0:T(8,128)(2,1)} collective-permute-done((bf16[512,512]{1,0:T(8,128)(2,1)}, bf16[512,512]{1,0:T(8,128)(2,1)}, u32[]{:S(2)}, u32[]{:S(2)}) %collective-permute-start.34) | collective-permute-done | bytes 524320 | tf_op jit(solution)/shard_map/ppermute | solution.py:14
  118.2 1.1 collective-permute-start.52
  119.3 1.1 shard_map.69
  120.5 1.0 collective-permute-start.41
  121.5 1.6 collective-permute-start.42
  123.1 3.2 %collective-permute-done.47.refs_5_ = bf16[256,512]{1,0:T(8,128)(2,1)S(1)} collective-permute-done((bf16[256,512]{1,0:T(8,128)(2,1)S(1)}, bf16[256,512]{1,0:T(8,128)(2,1)S(1)}, u32[]{:S(2)}, u32[]{:S(2)}) %collective-permute-start.47) | collective-permute-done | bytes 262176 | tf_op jit(solution)/shard_map/ppermute | solution.py:14
  126.3 3.4 %collective-permute-start.43 = (bf16[128,512]{1,0:T(8,128)(2,1)S(1)}, bf16[128,512]{1,0:T(8,128)(2,1)S(1)}, u32[]{:S(2)}, u32[]{:S(2)}) collective-permute-start(bf16[128,512]{1,0:T(8,128)(2,1)S(1)} %get-tuple-element.131), channel_id=1, source_target_pairs={{0,6},{1,7},{2,4},{3,5},{4,2},{5,3},{6,0},{7,1},{8,14},{9,15},{10,... | collective-permute-start | bytes 393224 | tf_op jit(solution)/shard_map/ppermute | solution.py:14
  129.7 1.8 shard_map.71
  131.5 2.4 %collective-permute-start.54 = (bf16[256,256]{1,0:T(8,128)(2,1)S(1)}, bf16[256,256]{1,0:T(8,128)(2,1)S(1)}, u32[]{:S(2)}, u32[]{:S(2)}) collective-permute-start(bf16[256,256]{1,0:T(8,128)(2,1)S(1)} %get-tuple-element.152), channel_id=1, source_target_pairs={{0,6},{1,7},{2,4},{3,5},{4,2},{5,3},{6,0},{7,1},{8,14},{9,15},{10,... | collective-permute-start | bytes 393224 | tf_op jit(solution)/shard_map/ppermute | solution.py:14
  133.9 3.2 %collective-permute-start.51 = (bf16[512,512]{1,0:T(8,128)(2,1)}, bf16[512,512]{1,0:T(8,128)(2,1)}, u32[]{:S(2)}, u32[]{:S(2)}) collective-permute-start(bf16[512,512]{1,0:T(8,128)(2,1)} %get-tuple-element.140.refs_3_), channel_id=1, source_target_pairs={{0,8},{1,9},{2,10},{3,11},{4,12},{5,13},{6,14},{7,15},{8,0},{9,1},... | collective-permute-start | bytes 1572872 | tf_op jit(solution)/shard_map/ppermute | solution.py:14
  137.1 1.2 shard_map.72
  138.3 1.6 collective-permute-start.48
  140.0 2.1 %collective-permute-done.53.refs_4_ = bf16[256,256]{1,0:T(8,128)(2,1)S(1)} collective-permute-done((bf16[256,256]{1,0:T(8,128)(2,1)S(1)}, bf16[256,256]{1,0:T(8,128)(2,1)S(1)}, u32[]{:S(2)}, u32[]{:S(2)}) %collective-permute-start.53) | collective-permute-done | bytes 131104 | tf_op jit(solution)/shard_map/ppermute | solution.py:14
  142.0 3.8 %collective-permute-done.54.refs_5_ = bf16[256,256]{1,0:T(8,128)(2,1)S(1)} collective-permute-done((bf16[256,256]{1,0:T(8,128)(2,1)S(1)}, bf16[256,256]{1,0:T(8,128)(2,1)S(1)}, u32[]{:S(2)}, u32[]{:S(2)}) %collective-permute-start.54) | collective-permute-done | bytes 131104 | tf_op jit(solution)/shard_map/ppermute | solution.py:14
  145.8 1.6 shard_map.74
  147.6 5.8 %collective-permute-done.49.refs_5_.refs_3_.refs_13_ = bf16[128,512]{1,0:T(8,128)(2,1)S(1)} collective-permute-done((bf16[128,512]{1,0:T(8,128)(2,1)S(1)}, bf16[128,512]{1,0:T(8,128)(2,1)S(1)}, u32[]{:S(2)}, u32[]{:S(2)}) %collective-permute-start.49) | collective-permute-done | bytes 131104 | tf_op jit(solution)/shard_map/ppermute | solution.py:14
  153.3 2.5 %collective-permute-done.50.refs_6_.refs_4_.refs_14_ = bf16[128,512]{1,0:T(8,128)(2,1)S(1)} collective-permute-done((bf16[128,512]{1,0:T(8,128)(2,1)S(1)}, bf16[128,512]{1,0:T(8,128)(2,1)S(1)}, u32[]{:S(2)}, u32[]{:S(2)}) %collective-permute-start.50) | collective-permute-done | bytes 131104 | tf_op jit(solution)/shard_map/ppermute | solution.py:14
  155.9 10.0 %collective-permute-done.51.refs_2_ = bf16[512,512]{1,0:T(8,128)(2,1)} collective-permute-done((bf16[512,512]{1,0:T(8,128)(2,1)}, bf16[512,512]{1,0:T(8,128)(2,1)}, u32[]{:S(2)}, u32[]{:S(2)}) %collective-permute-start.51) | collective-permute-done | bytes 524320 | tf_op jit(solution)/shard_map/ppermute | solution.py:14
  165.9 1.1 shard_map.75
  167.0 1.4 collective-permute-start.55
  168.4 2.2 %collective-permute-start.57 = (bf16[128,512]{1,0:T(8,128)(2,1)S(1)}, bf16[128,512]{1,0:T(8,128)(2,1)S(1)}, u32[]{:S(2)}, u32[]{:S(2)}) collective-permute-start(bf16[128,512]{1,0:T(8,128)(2,1)S(1)} %get-tuple-element.157), channel_id=1, source_target_pairs={{0,6},{1,7},{2,4},{3,5},{4,2},{5,3},{6,0},{7,1},{8,14},{9,15},{10,... | collective-permute-start | bytes 393224 | tf_op jit(solution)/shard_map/ppermute | solution.py:14
  170.7 1.4 collective-permute-start.59
  172.2 1.2 collective-permute-done.55.refs_2_.refs_16_
  173.4 1.6 collective-permute-done.57.refs_4_.refs_18_
  175.1 1.4 collective-permute-start.60
  176.6 1.4 collective-permute-start.61
  178.0 1.8 collective-permute-done.60.refs_3_.refs_21_
  179.8 2.0 %collective-permute-done.61.refs_4_.refs_22_ = bf16[128,256]{1,0:T(8,128)(2,1)S(1)} collective-permute-done((bf16[128,256]{1,0:T(8,128)(2,1)S(1)}, bf16[128,256]{1,0:T(8,128)(2,1)S(1)}, u32[]{:S(2)}, u32[]{:S(2)}) %collective-permute-start.61) | collective-permute-done | bytes 65568 | tf_op jit(solution)/shard_map/ppermute | solution.py:14
  181.9 1.3 collective-permute-done.66.refs_27_
  183.3 3.7 %shard_map.82 = bf16[32,64,512]{2,1,0:T(8,128)(2,1)} custom-call(s32[4]{0:T(128)S(1)} %copy-done.34, s32[1]{0:T(128)} %bitcast.refs_1_.refs_0_, f32[64,512]{1,0:T(8,128)S(1)} %convolution_multiply_fusion.refs_20_.refs_2_, bf16[128,256]{1,0:T(8,128)(2,1)S(1)} %copy-done.21, bf16[128,256]{1,0:T(8,128)(2,1)S(1)} %copy-done.23, bf16[128,256]{1,0:T(8,128)(2,1)S(1)} %copy-done.25, ...), custom_call_target="tpu_custom_call" | custom-call | tf_op jit(solution)/shard_map/pallas_call | solution.py:51
  (184 shorter events, 17.0 us)
Async XLA Ops:
  0.0 13.2 %collective-permute-start.9 = (bf16[128,1024]{1,0:T(8,128)(2,1)}, bf16[128,1024]{1,0:T(8,128)(2,1)S(1)}, u32[]{:S(2)}, u32[]{:S(2)}) collective-permute-start(bf16[128,1024]{1,0:T(8,128)(2,1)} %refs_1_.1), channel_id=1, source_target_pairs={{0,4},{1,5},{2,6},{3,7},{4,0},{5,1},{6,2},{7,3},{8,12},{9,13},{10,... | collective-permute-start | bytes 786440 | tf_op jit(solution)/shard_map/ppermute | solution.py:14
  5.2 7.5 %collective-permute-start.8 = (bf16[128,512]{1,0:T(8,128)(2,1)S(1)}, bf16[128,512]{1,0:T(8,128)(2,1)S(1)}, u32[]{:S(2)}, u32[]{:S(2)}) collective-permute-start(bf16[128,512]{1,0:T(8,128)(2,1)S(1)} %fusion.3.refs_4_), channel_id=1, source_target_pairs={{0,8},{1,9},{2,10},{3,11},{4,12},{5,13},{6,14},{7,15},{8,0},{9,1},... | collective-permute-start | bytes 393224 | tf_op jit(solution)/shard_map/ppermute | solution.py:14
  7.9 9.3 %collective-permute-start.4 = (bf16[128,512]{1,0:T(8,128)(2,1)S(1)}, bf16[128,512]{1,0:T(8,128)(2,1)S(1)}, u32[]{:S(2)}, u32[]{:S(2)}) collective-permute-start(bf16[128,512]{1,0:T(8,128)(2,1)S(1)} %fusion.3.refs_4_), channel_id=1, source_target_pairs={{0,4},{1,5},{2,6},{3,7},{4,0},{5,1},{6,2},{7,3},{8,12},{9,13},{10,... | collective-permute-start | bytes 393224 | tf_op jit(solution)/shard_map/ppermute | solution.py:14
  8.3 10.4 %collective-permute-start.2 = (bf16[128,512]{1,0:T(8,128)(2,1)S(1)}, bf16[128,512]{1,0:T(8,128)(2,1)S(1)}, u32[]{:S(2)}, u32[]{:S(2)}) collective-permute-start(bf16[128,512]{1,0:T(8,128)(2,1)S(1)} %fusion.3.refs_4_), channel_id=1, source_target_pairs={{0,2},{1,3},{2,0},{3,1},{4,6},{5,7},{6,4},{7,5},{8,10},{9,11},{10,... | collective-permute-start | bytes 393224 | tf_op jit(solution)/shard_map/ppermute | solution.py:14
  9.9 9.4 %collective-permute-start.1 = (bf16[128,512]{1,0:T(8,128)(2,1)S(1)}, bf16[128,512]{1,0:T(8,128)(2,1)S(1)}, u32[]{:S(2)}, u32[]{:S(2)}) collective-permute-start(bf16[128,512]{1,0:T(8,128)(2,1)S(1)} %fusion.3.refs_4_), channel_id=1, source_target_pairs={{0,1},{1,0},{2,3},{3,2},{4,5},{5,4},{6,7},{7,6},{8,9},{9,8},{10,11... | collective-permute-start | bytes 393224 | tf_op jit(solution)/shard_map/ppermute | solution.py:14
  13.2 6.6 %collective-permute-start.13 = (bf16[128,512]{1,0:T(8,128)(2,1)S(1)}, bf16[128,512]{1,0:T(8,128)(2,1)S(1)}, u32[]{:S(2)}, u32[]{:S(2)}) collective-permute-start(bf16[128,512]{1,0:T(8,128)(2,1)S(1)} %shard_map.55.refs_12_), channel_id=1, source_target_pairs={{0,4},{1,5},{2,6},{3,7},{4,0},{5,1},{6,2},{7,3},{8,12},{9,13},{10,... | collective-permute-start | bytes 393224 | tf_op jit(solution)/shard_map/ppermute | solution.py:14
  17.2 5.3 %collective-permute-start.6 = (bf16[128,512]{1,0:T(8,128)(2,1)S(1)}, bf16[128,512]{1,0:T(8,128)(2,1)S(1)}, u32[]{:S(2)}, u32[]{:S(2)}) collective-permute-start(bf16[128,512]{1,0:T(8,128)(2,1)S(1)} %collective-permute-done.4.refs_8_), channel_id=1, source_target_pairs={{0,2},{1,3},{2,0},{3,1},{4,6},{5,7},{6,4},{7,5},{8,10},{9,11},{10,... | collective-permute-start | bytes 393224 | tf_op jit(solution)/shard_map/ppermute | solution.py:14
  18.8 3.8 %collective-permute-start.5 = (bf16[128,512]{1,0:T(8,128)(2,1)S(1)}, bf16[128,512]{1,0:T(8,128)(2,1)S(1)}, u32[]{:S(2)}, u32[]{:S(2)}) collective-permute-start(bf16[128,512]{1,0:T(8,128)(2,1)S(1)} %collective-permute-done.4.refs_8_), channel_id=1, source_target_pairs={{0,1},{1,0},{2,3},{3,2},{4,5},{5,4},{6,7},{7,6},{8,9},{9,8},{10,11... | collective-permute-start | bytes 393224 | tf_op jit(solution)/shard_map/ppermute | solution.py:14
  18.8 4.3 %collective-permute-start.3 = (bf16[128,512]{1,0:T(8,128)(2,1)S(1)}, bf16[128,512]{1,0:T(8,128)(2,1)S(1)}, u32[]{:S(2)}, u32[]{:S(2)}) collective-permute-start(bf16[128,512]{1,0:T(8,128)(2,1)S(1)} %collective-permute-done.2.refs_6_), channel_id=1, source_target_pairs={{0,1},{1,0},{2,3},{3,2},{4,5},{5,4},{6,7},{7,6},{8,9},{9,8},{10,11... | collective-permute-start | bytes 393224 | tf_op jit(solution)/shard_map/ppermute | solution.py:14
  19.3 6.4 %collective-permute-start.11 = (bf16[128,512]{1,0:T(8,128)(2,1)S(1)}, bf16[128,512]{1,0:T(8,128)(2,1)S(1)}, u32[]{:S(2)}, u32[]{:S(2)}) collective-permute-start(bf16[128,512]{1,0:T(8,128)(2,1)S(1)} %shard_map.55.refs_12_), channel_id=1, source_target_pairs={{0,2},{1,3},{2,0},{3,1},{4,6},{5,7},{6,4},{7,5},{8,10},{9,11},{10,... | collective-permute-start | bytes 393224 | tf_op jit(solution)/shard_map/ppermute | solution.py:14
  19.8 8.0 %collective-permute-start.15 = (bf16[128,512]{1,0:T(8,128)(2,1)S(1)}, bf16[128,512]{1,0:T(8,128)(2,1)S(1)}, u32[]{:S(2)}, u32[]{:S(2)}) collective-permute-start(bf16[128,512]{1,0:T(8,128)(2,1)S(1)} %collective-permute-done.13.refs_16_), channel_id=1, source_target_pairs={{0,2},{1,3},{2,0},{3,1},{4,6},{5,7},{6,4},{7,5},{8,10},{9,11},{10,... | collective-permute-start | bytes 393224 | tf_op jit(solution)/shard_map/ppermute | solution.py:14
  22.5 6.9 %collective-permute-start.10 = (bf16[128,512]{1,0:T(8,128)(2,1)S(1)}, bf16[128,512]{1,0:T(8,128)(2,1)S(1)}, u32[]{:S(2)}, u32[]{:S(2)}) collective-permute-start(bf16[128,512]{1,0:T(8,128)(2,1)S(1)} %shard_map.55.refs_12_), channel_id=1, source_target_pairs={{0,1},{1,0},{2,3},{3,2},{4,5},{5,4},{6,7},{7,6},{8,9},{9,8},{10,11... | collective-permute-start | bytes 393224 | tf_op jit(solution)/shard_map/ppermute | solution.py:14
  22.5 5.3 %collective-permute-start.7 = (bf16[128,512]{1,0:T(8,128)(2,1)S(1)}, bf16[128,512]{1,0:T(8,128)(2,1)S(1)}, u32[]{:S(2)}, u32[]{:S(2)}) collective-permute-start(bf16[128,512]{1,0:T(8,128)(2,1)S(1)} %collective-permute-done.6.refs_10_), channel_id=1, source_target_pairs={{0,1},{1,0},{2,3},{3,2},{4,5},{5,4},{6,7},{7,6},{8,9},{9,8},{10,11... | collective-permute-start | bytes 393224 | tf_op jit(solution)/shard_map/ppermute | solution.py:14
  23.0 6.4 %collective-permute-start.14 = (bf16[128,512]{1,0:T(8,128)(2,1)S(1)}, bf16[128,512]{1,0:T(8,128)(2,1)S(1)}, u32[]{:S(2)}, u32[]{:S(2)}) collective-permute-start(bf16[128,512]{1,0:T(8,128)(2,1)S(1)} %collective-permute-done.13.refs_16_), channel_id=1, source_target_pairs={{0,1},{1,0},{2,3},{3,2},{4,5},{5,4},{6,7},{7,6},{8,9},{9,8},{10,11... | collective-permute-start | bytes 393224 | tf_op jit(solution)/shard_map/ppermute | solution.py:14
  25.6 3.8 %collective-permute-start.12 = (bf16[128,512]{1,0:T(8,128)(2,1)S(1)}, bf16[128,512]{1,0:T(8,128)(2,1)S(1)}, u32[]{:S(2)}, u32[]{:S(2)}) collective-permute-start(bf16[128,512]{1,0:T(8,128)(2,1)S(1)} %collective-permute-done.11.refs_14_), channel_id=1, source_target_pairs={{0,1},{1,0},{2,3},{3,2},{4,5},{5,4},{6,7},{7,6},{8,9},{9,8},{10,11... | collective-permute-start | bytes 393224 | tf_op jit(solution)/shard_map/ppermute | solution.py:14
  27.9 22.3 %collective-permute-start.21 = (bf16[128,1024]{1,0:T(8,128)(2,1)}, bf16[128,1024]{1,0:T(8,128)(2,1)}, u32[]{:S(2)}, u32[]{:S(2)}) collective-permute-start(bf16[128,1024]{1,0:T(8,128)(2,1)} %refs_1_.1), channel_id=1, source_target_pairs={{0,2},{1,3},{2,0},{3,1},{4,6},{5,7},{6,4},{7,5},{8,10},{9,11},{10,... | collective-permute-start | bytes 786440 | tf_op jit(solution)/shard_map/ppermute | solution.py:14
  33.3 16.9 %collective-permute-start.22 = (bf16[128,1024]{1,0:T(8,128)(2,1)S(1)}, bf16[128,1024]{1,0:T(8,128)(2,1)S(1)}, u32[]{:S(2)}, u32[]{:S(2)}) collective-permute-start(bf16[128,1024]{1,0:T(8,128)(2,1)S(1)} %collective-permute-done.9.refs_1_.refs_3_), channel_id=1, source_target_pairs={{0,2},{1,3},{2,0},{3,1},{4,6},{5,7},{6,4},{7,5},{8,10},{9,11},{10,... | collective-permute-start | bytes 786440 | tf_op jit(solution)/shard_map/ppermute | solution.py:14
  34.6 15.6 %collective-permute-start.18 = (bf16[256,256]{1,0:T(8,128)(2,1)S(1)}, bf16[256,256]{1,0:T(8,128)(2,1)S(1)}, u32[]{:S(2)}, u32[]{:S(2)}) collective-permute-start(bf16[256,256]{1,0:T(8,128)(2,1)S(1)} %get-tuple-element.86), channel_id=1, source_target_pairs={{0,2},{1,3},{2,0},{3,1},{4,6},{5,7},{6,4},{7,5},{8,10},{9,11},{10,... | collective-permute-start | bytes 393224 | tf_op jit(solution)/shard_map/ppermute | solution.py:14
  35.9 14.4 %collective-permute-start.19 = (bf16[256,256]{1,0:T(8,128)(2,1)S(1)}, bf16[256,256]{1,0:T(8,128)(2,1)S(1)}, u32[]{:S(2)}, u32[]{:S(2)}) collective-permute-start(bf16[256,256]{1,0:T(8,128)(2,1)S(1)} %get-tuple-element.87), channel_id=1, source_target_pairs={{0,4},{1,5},{2,6},{3,7},{4,0},{5,1},{6,2},{7,3},{8,12},{9,13},{10,... | collective-permute-start | bytes 393224 | tf_op jit(solution)/shard_map/ppermute | solution.py:14
  35.9 14.4 %collective-permute-start.20 = (bf16[256,256]{1,0:T(8,128)(2,1)S(1)}, bf16[256,256]{1,0:T(8,128)(2,1)S(1)}, u32[]{:S(2)}, u32[]{:S(2)}) collective-permute-start(bf16[256,256]{1,0:T(8,128)(2,1)S(1)} %get-tuple-element.88), channel_id=1, source_target_pairs={{0,6},{1,7},{2,4},{3,5},{4,2},{5,3},{6,0},{7,1},{8,14},{9,15},{10,... | collective-permute-start | bytes 393224 | tf_op jit(solution)/shard_map/ppermute | solution.py:14
  54.1 2.0 %collective-permute-start.27 = (bf16[4,128,512]{2,1,0:T(8,128)(2,1)S(1)}, bf16[4,128,512]{2,1,0:T(8,128)(2,1)}, u32[]{:S(2)}, u32[]{:S(2)}) collective-permute-start(bf16[4,128,512]{2,1,0:T(8,128)(2,1)S(1)} %get-tuple-element.104), channel_id=1, source_target_pairs={{0,1},{1,0},{2,3},{3,2},{4,5},{5,4},{6,7},{7,6},{8,9},{9,8},{10,11... | collective-permute-start | bytes 1572872 | tf_op jit(solution)/shard_map/ppermute | solution.py:14
  54.1 3.7 %collective-permute-start = (bf16[128,1024]{1,0:T(8,128)(2,1)}, bf16[128,1024]{1,0:T(8,128)(2,1)}, u32[]{:S(2)}, u32[]{:S(2)}) collective-permute-start(bf16[128,1024]{1,0:T(8,128)(2,1)} %refs_1_.1), channel_id=1, source_target_pairs={{0,1},{1,0},{2,3},{3,2},{4,5},{5,4},{6,7},{7,6},{8,9},{9,8},{10,11... | collective-permute-start | bytes 786440 | tf_op jit(solution)/shard_map/ppermute | solution.py:14
  54.7 3.6 %collective-permute-start.37 = (bf16[4,128,256]{2,1,0:T(8,128)(2,1)}, bf16[4,128,256]{2,1,0:T(8,128)(2,1)S(1)}, u32[]{:S(2)}, u32[]{:S(2)}) collective-permute-start(bf16[4,128,256]{2,1,0:T(8,128)(2,1)} %copy-done.30), channel_id=1, source_target_pairs={{0,1},{1,0},{2,3},{3,2},{4,5},{5,4},{6,7},{7,6},{8,9},{9,8},{10,11... | collective-permute-start | bytes 786440 | tf_op jit(solution)/shard_map/ppermute | solution.py:14
  54.8 3.6 %collective-permute-start.23 = (bf16[128,1024]{1,0:T(8,128)(2,1)}, bf16[128,1024]{1,0:T(8,128)(2,1)S(1)}, u32[]{:S(2)}, u32[]{:S(2)}) collective-permute-start(bf16[128,1024]{1,0:T(8,128)(2,1)} %get-tuple-element.95.refs_3_), channel_id=1, source_target_pairs={{0,1},{1,0},{2,3},{3,2},{4,5},{5,4},{6,7},{7,6},{8,9},{9,8},{10,11... | collective-permute-start | bytes 786440 | tf_op jit(solution)/shard_map/ppermute | solution.py:14
  55.2 4.4 %collective-permute-start.24 = (bf16[128,1024]{1,0:T(8,128)(2,1)S(1)}, bf16[128,1024]{1,0:T(8,128)(2,1)S(1)}, u32[]{:S(2)}, u32[]{:S(2)}) collective-permute-start(bf16[128,1024]{1,0:T(8,128)(2,1)S(1)} %get-tuple-element.96.refs_5_), channel_id=1, source_target_pairs={{0,1},{1,0},{2,3},{3,2},{4,5},{5,4},{6,7},{7,6},{8,9},{9,8},{10,11... | collective-permute-start | bytes 786440 | tf_op jit(solution)/shard_map/ppermute | solution.py:14
  56.1 3.5 %collective-permute-start.25 = (bf16[128,1024]{1,0:T(8,128)(2,1)}, bf16[128,1024]{1,0:T(8,128)(2,1)S(1)}, u32[]{:S(2)}, u32[]{:S(2)}) collective-permute-start(bf16[128,1024]{1,0:T(8,128)(2,1)} %copy-done.28), channel_id=1, source_target_pairs={{0,1},{1,0},{2,3},{3,2},{4,5},{5,4},{6,7},{7,6},{8,9},{9,8},{10,11... | collective-permute-start | bytes 786440 | tf_op jit(solution)/shard_map/ppermute | solution.py:14
  57.8 11.0 %collective-permute-start.35 = (bf16[4,128,512]{2,1,0:T(8,128)(2,1)S(1)}, bf16[4,128,512]{2,1,0:T(8,128)(2,1)S(1)}, u32[]{:S(2)}, u32[]{:S(2)}) collective-permute-start(bf16[4,128,512]{2,1,0:T(8,128)(2,1)S(1)} %copy-done.1), channel_id=1, source_target_pairs={{0,1},{1,0},{2,3},{3,2},{4,5},{5,4},{6,7},{7,6},{8,9},{9,8},{10,11... | collective-permute-start | bytes 1572872 | tf_op jit(solution)/shard_map/ppermute | solution.py:14
  58.3 12.5 %collective-permute-start.36 = (bf16[4,128,512]{2,1,0:T(8,128)(2,1)S(1)}, bf16[4,128,512]{2,1,0:T(8,128)(2,1)S(1)}, u32[]{:S(2)}, u32[]{:S(2)}) collective-permute-start(bf16[4,128,512]{2,1,0:T(8,128)(2,1)S(1)} %copy-done.3), channel_id=1, source_target_pairs={{0,1},{1,0},{2,3},{3,2},{4,5},{5,4},{6,7},{7,6},{8,9},{9,8},{10,11... | collective-permute-start | bytes 1572872 | tf_op jit(solution)/shard_map/ppermute | solution.py:14
  58.4 14.6 %collective-permute-start.28 = (bf16[256,512]{1,0:T(8,128)(2,1)S(1)}, bf16[256,512]{1,0:T(8,128)(2,1)S(1)}, u32[]{:S(2)}, u32[]{:S(2)}) collective-permute-start(bf16[256,512]{1,0:T(8,128)(2,1)S(1)} %get-tuple-element.106), channel_id=1, source_target_pairs={{0,2},{1,3},{2,0},{3,1},{4,6},{5,7},{6,4},{7,5},{8,10},{9,11},{10,... | collective-permute-start | bytes 786440 | tf_op jit(solution)/shard_map/ppermute | solution.py:14
  59.6 15.0 %collective-permute-start.29 = (bf16[256,512]{1,0:T(8,128)(2,1)S(1)}, bf16[256,512]{1,0:T(8,128)(2,1)S(1)}, u32[]{:S(2)}, u32[]{:S(2)}) collective-permute-start(bf16[256,512]{1,0:T(8,128)(2,1)S(1)} %get-tuple-element.107), channel_id=1, source_target_pairs={{0,4},{1,5},{2,6},{3,7},{4,0},{5,1},{6,2},{7,3},{8,12},{9,13},{10,... | collective-permute-start | bytes 786440 | tf_op jit(solution)/shard_map/ppermute | solution.py:14
  59.7 17.3 %collective-permute-start.30 = (bf16[256,512]{1,0:T(8,128)(2,1)S(1)}, bf16[256,512]{1,0:T(8,128)(2,1)S(1)}, u32[]{:S(2)}, u32[]{:S(2)}) collective-permute-start(bf16[256,512]{1,0:T(8,128)(2,1)S(1)} %get-tuple-element.108), channel_id=1, source_target_pairs={{0,6},{1,7},{2,4},{3,5},{4,2},{5,3},{6,0},{7,1},{8,14},{9,15},{10,... | collective-permute-start | bytes 786440 | tf_op jit(solution)/shard_map/ppermute | solution.py:14
  68.9 15.9 %collective-permute-start.26 = (bf16[512,256]{1,0:T(8,128)(2,1)S(1)}, bf16[512,256]{1,0:T(8,128)(2,1)S(1)}, u32[]{:S(2)}, u32[]{:S(2)}) collective-permute-start(bf16[512,256]{1,0:T(8,128)(2,1)S(1)} %get-tuple-element.102.refs_6_.refs_3_), channel_id=1, source_target_pairs={{0,8},{1,9},{2,10},{3,11},{4,12},{5,13},{6,14},{7,15},{8,0},{9,1},... | collective-permute-start | bytes 786440 | tf_op jit(solution)/shard_map/ppermute | solution.py:14
  71.8 14.3 %collective-permute-start.38 = (bf16[256,512]{1,0:T(8,128)(2,1)}, bf16[256,512]{1,0:T(8,128)(2,1)}, u32[]{:S(2)}, u32[]{:S(2)}) collective-permute-start(bf16[256,512]{1,0:T(8,128)(2,1)} %get-tuple-element.124), channel_id=1, source_target_pairs={{0,2},{1,3},{2,0},{3,1},{4,6},{5,7},{6,4},{7,5},{8,10},{9,11},{10,... | collective-permute-start | bytes 786440 | tf_op jit(solution)/shard_map/ppermute | solution.py:14
  73.0 21.3 %collective-permute-start.39 = (bf16[256,512]{1,0:T(8,128)(2,1)}, bf16[256,512]{1,0:T(8,128)(2,1)}, u32[]{:S(2)}, u32[]{:S(2)}) collective-permute-start(bf16[256,512]{1,0:T(8,128)(2,1)} %get-tuple-element.125), channel_id=1, source_target_pairs={{0,4},{1,5},{2,6},{3,7},{4,0},{5,1},{6,2},{7,3},{8,12},{9,13},{10,... | collective-permute-start | bytes 786440 | tf_op jit(solution)/shard_map/ppermute | solution.py:14
  74.6 25.1 %collective-permute-start.40 = (bf16[256,512]{1,0:T(8,128)(2,1)}, bf16[256,512]{1,0:T(8,128)(2,1)}, u32[]{:S(2)}, u32[]{:S(2)}) collective-permute-start(bf16[256,512]{1,0:T(8,128)(2,1)} %get-tuple-element.126), channel_id=1, source_target_pairs={{0,6},{1,7},{2,4},{3,5},{4,2},{5,3},{6,0},{7,1},{8,14},{9,15},{10,... | collective-permute-start | bytes 786440 | tf_op jit(solution)/shard_map/ppermute | solution.py:14
  78.8 39.4 %collective-permute-start.34 = (bf16[512,512]{1,0:T(8,128)(2,1)}, bf16[512,512]{1,0:T(8,128)(2,1)}, u32[]{:S(2)}, u32[]{:S(2)}) collective-permute-start(bf16[512,512]{1,0:T(8,128)(2,1)} %get-tuple-element.109.refs_3_), channel_id=1, source_target_pairs={{0,8},{1,9},{2,10},{3,11},{4,12},{5,13},{6,14},{7,15},{8,0},{9,1},... | collective-permute-start | bytes 1572872 | tf_op jit(solution)/shard_map/ppermute | solution.py:14
  84.9 17.5 %collective-permute-start.31 = (bf16[128,256]{1,0:T(8,128)(2,1)S(1)}, bf16[128,256]{1,0:T(8,128)(2,1)S(1)}, u32[]{:S(2)}, u32[]{:S(2)}) collective-permute-start(bf16[128,256]{1,0:T(8,128)(2,1)S(1)} %get-tuple-element.111), channel_id=1, source_target_pairs={{0,2},{1,3},{2,0},{3,1},{4,6},{5,7},{6,4},{7,5},{8,10},{9,11},{10,... | collective-permute-start | bytes 196616 | tf_op jit(solution)/shard_map/ppermute | solution.py:14
  86.1 18.0 %collective-permute-start.32 = (bf16[128,256]{1,0:T(8,128)(2,1)S(1)}, bf16[128,256]{1,0:T(8,128)(2,1)S(1)}, u32[]{:S(2)}, u32[]{:S(2)}) collective-permute-start(bf16[128,256]{1,0:T(8,128)(2,1)S(1)} %get-tuple-element.112), channel_id=1, source_target_pairs={{0,4},{1,5},{2,6},{3,7},{4,0},{5,1},{6,2},{7,3},{8,12},{9,13},{10,... | collective-permute-start | bytes 196616 | tf_op jit(solution)/shard_map/ppermute | solution.py:14
  94.3 11.2 %collective-permute-start.33 = (bf16[128,256]{1,0:T(8,128)(2,1)S(1)}, bf16[128,256]{1,0:T(8,128)(2,1)S(1)}, u32[]{:S(2)}, u32[]{:S(2)}) collective-permute-start(bf16[128,256]{1,0:T(8,128)(2,1)S(1)} %get-tuple-element.113), channel_id=1, source_target_pairs={{0,6},{1,7},{2,4},{3,5},{4,2},{5,3},{6,0},{7,1},{8,14},{9,15},{10,... | collective-permute-start | bytes 196616 | tf_op jit(solution)/shard_map/ppermute | solution.py:14
  102.4 29.1 %collective-permute-start.44 = (bf16[512,512]{1,0:T(8,128)(2,1)}, bf16[512,512]{1,0:T(8,128)(2,1)}, u32[]{:S(2)}, u32[]{:S(2)}) collective-permute-start(bf16[512,512]{1,0:T(8,128)(2,1)} %get-tuple-element.127.refs_3_), channel_id=1, source_target_pairs={{0,8},{1,9},{2,10},{3,11},{4,12},{5,13},{6,14},{7,15},{8,0},{9,1},... | collective-permute-start | bytes 1572872 | tf_op jit(solution)/shard_map/ppermute | solution.py:14
  102.4 18.0 %collective-permute-start.45 = (bf16[256,512]{1,0:T(8,128)(2,1)S(1)}, bf16[256,512]{1,0:T(8,128)(2,1)S(1)}, u32[]{:S(2)}, u32[]{:S(2)}) collective-permute-start(bf16[256,512]{1,0:T(8,128)(2,1)S(1)} %get-tuple-element.137), channel_id=1, source_target_pairs={{0,2},{1,3},{2,0},{3,1},{4,6},{5,7},{6,4},{7,5},{8,10},{9,11},{10,... | collective-permute-start | bytes 786440 | tf_op jit(solution)/shard_map/ppermute | solution.py:14
  104.1 17.4 %collective-permute-start.46 = (bf16[256,512]{1,0:T(8,128)(2,1)S(1)}, bf16[256,512]{1,0:T(8,128)(2,1)S(1)}, u32[]{:S(2)}, u32[]{:S(2)}) collective-permute-start(bf16[256,512]{1,0:T(8,128)(2,1)S(1)} %get-tuple-element.138), channel_id=1, source_target_pairs={{0,4},{1,5},{2,6},{3,7},{4,0},{5,1},{6,2},{7,3},{8,12},{9,13},{10,... | collective-permute-start | bytes 786440 | tf_op jit(solution)/shard_map/ppermute | solution.py:14
  105.5 20.8 %collective-permute-start.47 = (bf16[256,512]{1,0:T(8,128)(2,1)S(1)}, bf16[256,512]{1,0:T(8,128)(2,1)S(1)}, u32[]{:S(2)}, u32[]{:S(2)}) collective-permute-start(bf16[256,512]{1,0:T(8,128)(2,1)S(1)} %get-tuple-element.139), channel_id=1, source_target_pairs={{0,6},{1,7},{2,4},{3,5},{4,2},{5,3},{6,0},{7,1},{8,14},{9,15},{10,... | collective-permute-start | bytes 786440 | tf_op jit(solution)/shard_map/ppermute | solution.py:14
  118.2 21.7 %collective-permute-start.52 = (bf16[256,256]{1,0:T(8,128)(2,1)}, bf16[256,256]{1,0:T(8,128)(2,1)}, u32[]{:S(2)}, u32[]{:S(2)}) collective-permute-start(bf16[256,256]{1,0:T(8,128)(2,1)} %get-tuple-element.150), channel_id=1, source_target_pairs={{0,2},{1,3},{2,0},{3,1},{4,6},{5,7},{6,4},{7,5},{8,10},{9,11},{10,... | collective-permute-start | bytes 393224 | tf_op jit(solution)/shard_map/ppermute | solution.py:14
  120.5 11.1 %collective-permute-start.41 = (bf16[128,512]{1,0:T(8,128)(2,1)S(1)}, bf16[128,512]{1,0:T(8,128)(2,1)S(1)}, u32[]{:S(2)}, u32[]{:S(2)}) collective-permute-start(bf16[128,512]{1,0:T(8,128)(2,1)S(1)} %get-tuple-element.129), channel_id=1, source_target_pairs={{0,2},{1,3},{2,0},{3,1},{4,6},{5,7},{6,4},{7,5},{8,10},{9,11},{10,... | collective-permute-start | bytes 393224 | tf_op jit(solution)/shard_map/ppermute | solution.py:14
  121.5 12.4 %collective-permute-start.42 = (bf16[128,512]{1,0:T(8,128)(2,1)S(1)}, bf16[128,512]{1,0:T(8,128)(2,1)S(1)}, u32[]{:S(2)}, u32[]{:S(2)}) collective-permute-start(bf16[128,512]{1,0:T(8,128)(2,1)S(1)} %get-tuple-element.130), channel_id=1, source_target_pairs={{0,4},{1,5},{2,6},{3,7},{4,0},{5,1},{6,2},{7,3},{8,12},{9,13},{10,... | collective-permute-start | bytes 393224 | tf_op jit(solution)/shard_map/ppermute | solution.py:14
  126.3 10.8 %collective-permute-start.43 = (bf16[128,512]{1,0:T(8,128)(2,1)S(1)}, bf16[128,512]{1,0:T(8,128)(2,1)S(1)}, u32[]{:S(2)}, u32[]{:S(2)}) collective-permute-start(bf16[128,512]{1,0:T(8,128)(2,1)S(1)} %get-tuple-element.131), channel_id=1, source_target_pairs={{0,6},{1,7},{2,4},{3,5},{4,2},{5,3},{6,0},{7,1},{8,14},{9,15},{10,... | collective-permute-start | bytes 393224 | tf_op jit(solution)/shard_map/ppermute | solution.py:14
  131.5 10.5 %collective-permute-start.53 = (bf16[256,256]{1,0:T(8,128)(2,1)S(1)}, bf16[256,256]{1,0:T(8,128)(2,1)S(1)}, u32[]{:S(2)}, u32[]{:S(2)}) collective-permute-start(bf16[256,256]{1,0:T(8,128)(2,1)S(1)} %get-tuple-element.151), channel_id=1, source_target_pairs={{0,4},{1,5},{2,6},{3,7},{4,0},{5,1},{6,2},{7,3},{8,12},{9,13},{10,... | collective-permute-start | bytes 393224 | tf_op jit(solution)/shard_map/ppermute | solution.py:14
  131.5 14.3 %collective-permute-start.54 = (bf16[256,256]{1,0:T(8,128)(2,1)S(1)}, bf16[256,256]{1,0:T(8,128)(2,1)S(1)}, u32[]{:S(2)}, u32[]{:S(2)}) collective-permute-start(bf16[256,256]{1,0:T(8,128)(2,1)S(1)} %get-tuple-element.152), channel_id=1, source_target_pairs={{0,6},{1,7},{2,4},{3,5},{4,2},{5,3},{6,0},{7,1},{8,14},{9,15},{10,... | collective-permute-start | bytes 393224 | tf_op jit(solution)/shard_map/ppermute | solution.py:14
  133.9 32.0 %collective-permute-start.51 = (bf16[512,512]{1,0:T(8,128)(2,1)}, bf16[512,512]{1,0:T(8,128)(2,1)}, u32[]{:S(2)}, u32[]{:S(2)}) collective-permute-start(bf16[512,512]{1,0:T(8,128)(2,1)} %get-tuple-element.140.refs_3_), channel_id=1, source_target_pairs={{0,8},{1,9},{2,10},{3,11},{4,12},{5,13},{6,14},{7,15},{8,0},{9,1},... | collective-permute-start | bytes 1572872 | tf_op jit(solution)/shard_map/ppermute | solution.py:14
  138.3 9.3 %collective-permute-start.48 = (bf16[128,512]{1,0:T(8,128)(2,1)S(1)}, bf16[128,512]{1,0:T(8,128)(2,1)S(1)}, u32[]{:S(2)}, u32[]{:S(2)}) collective-permute-start(bf16[128,512]{1,0:T(8,128)(2,1)S(1)} %get-tuple-element.142), channel_id=1, source_target_pairs={{0,2},{1,3},{2,0},{3,1},{4,6},{5,7},{6,4},{7,5},{8,10},{9,11},{10,... | collective-permute-start | bytes 393224 | tf_op jit(solution)/shard_map/ppermute | solution.py:14
  139.9 13.4 %collective-permute-start.49 = (bf16[128,512]{1,0:T(8,128)(2,1)S(1)}, bf16[128,512]{1,0:T(8,128)(2,1)S(1)}, u32[]{:S(2)}, u32[]{:S(2)}) collective-permute-start(bf16[128,512]{1,0:T(8,128)(2,1)S(1)} %get-tuple-element.143), channel_id=1, source_target_pairs={{0,4},{1,5},{2,6},{3,7},{4,0},{5,1},{6,2},{7,3},{8,12},{9,13},{10,... | collective-permute-start | bytes 393224 | tf_op jit(solution)/shard_map/ppermute | solution.py:14
  142.0 13.8 %collective-permute-start.50 = (bf16[128,512]{1,0:T(8,128)(2,1)S(1)}, bf16[128,512]{1,0:T(8,128)(2,1)S(1)}, u32[]{:S(2)}, u32[]{:S(2)}) collective-permute-start(bf16[128,512]{1,0:T(8,128)(2,1)S(1)} %get-tuple-element.144), channel_id=1, source_target_pairs={{0,6},{1,7},{2,4},{3,5},{4,2},{5,3},{6,0},{7,1},{8,14},{9,15},{10,... | collective-permute-start | bytes 393224 | tf_op jit(solution)/shard_map/ppermute | solution.py:14
  147.5 23.2 %collective-permute-start.58 = (bf16[512,256]{1,0:T(8,128)(2,1)S(1)}, bf16[512,256]{1,0:T(8,128)(2,1)S(1)}, u32[]{:S(2)}, u32[]{:S(2)}) collective-permute-start(bf16[512,256]{1,0:T(8,128)(2,1)S(1)} %get-tuple-element.153.refs_3_), channel_id=1, source_target_pairs={{0,8},{1,9},{2,10},{3,11},{4,12},{5,13},{6,14},{7,15},{8,0},{9,1},... | collective-permute-start | bytes 786440 | tf_op jit(solution)/shard_map/ppermute | solution.py:14
  167.0 6.4 %collective-permute-start.55 = (bf16[128,512]{1,0:T(8,128)(2,1)S(1)}, bf16[128,512]{1,0:T(8,128)(2,1)S(1)}, u32[]{:S(2)}, u32[]{:S(2)}) collective-permute-start(bf16[128,512]{1,0:T(8,128)(2,1)S(1)} %get-tuple-element.155), channel_id=1, source_target_pairs={{0,2},{1,3},{2,0},{3,1},{4,6},{5,7},{6,4},{7,5},{8,10},{9,11},{10,... | collective-permute-start | bytes 393224 | tf_op jit(solution)/shard_map/ppermute | solution.py:14
  168.4 5.0 %collective-permute-start.56 = (bf16[128,512]{1,0:T(8,128)(2,1)S(1)}, bf16[128,512]{1,0:T(8,128)(2,1)S(1)}, u32[]{:S(2)}, u32[]{:S(2)}) collective-permute-start(bf16[128,512]{1,0:T(8,128)(2,1)S(1)} %get-tuple-element.156), channel_id=1, source_target_pairs={{0,4},{1,5},{2,6},{3,7},{4,0},{5,1},{6,2},{7,3},{8,12},{9,13},{10,... | collective-permute-start | bytes 393224 | tf_op jit(solution)/shard_map/ppermute | solution.py:14
  168.4 6.6 %collective-permute-start.57 = (bf16[128,512]{1,0:T(8,128)(2,1)S(1)}, bf16[128,512]{1,0:T(8,128)(2,1)S(1)}, u32[]{:S(2)}, u32[]{:S(2)}) collective-permute-start(bf16[128,512]{1,0:T(8,128)(2,1)S(1)} %get-tuple-element.157), channel_id=1, source_target_pairs={{0,6},{1,7},{2,4},{3,5},{4,2},{5,3},{6,0},{7,1},{8,14},{9,15},{10,... | collective-permute-start | bytes 393224 | tf_op jit(solution)/shard_map/ppermute | solution.py:14
  170.7 5.9 %collective-permute-start.59 = (bf16[128,256]{1,0:T(8,128)(2,1)S(1)}, bf16[128,256]{1,0:T(8,128)(2,1)S(1)}, u32[]{:S(2)}, u32[]{:S(2)}) collective-permute-start(bf16[128,256]{1,0:T(8,128)(2,1)S(1)} %get-tuple-element.160), channel_id=1, source_target_pairs={{0,2},{1,3},{2,0},{3,1},{4,6},{5,7},{6,4},{7,5},{8,10},{9,11},{10,... | collective-permute-start | bytes 196616 | tf_op jit(solution)/shard_map/ppermute | solution.py:14
  172.1 11.1 %collective-permute-start.63 = (bf16[4,64,512]{2,1,0:T(8,128)(2,1)S(1)}, bf16[4,64,512]{2,1,0:T(8,128)(2,1)S(1)}, u32[]{:S(2)}, u32[]{:S(2)}) collective-permute-start(bf16[4,64,512]{2,1,0:T(8,128)(2,1)S(1)} %shard_map.78), channel_id=1, source_target_pairs={{0,1},{1,0},{2,3},{3,2},{4,5},{5,4},{6,7},{7,6},{8,9},{9,8},{10,11... | collective-permute-start | bytes 786440 | tf_op jit(solution)/shard_map/ppermute | solution.py:14
  173.4 9.8 %collective-permute-start.64 = (bf16[4,64,512]{2,1,0:T(8,128)(2,1)S(1)}, bf16[4,64,512]{2,1,0:T(8,128)(2,1)S(1)}, u32[]{:S(2)}, u32[]{:S(2)}) collective-permute-start(bf16[4,64,512]{2,1,0:T(8,128)(2,1)S(1)} %shard_map.79), channel_id=1, source_target_pairs={{0,1},{1,0},{2,3},{3,2},{4,5},{5,4},{6,7},{7,6},{8,9},{9,8},{10,11... | collective-permute-start | bytes 786440 | tf_op jit(solution)/shard_map/ppermute | solution.py:14
  175.0 8.2 %collective-permute-start.65 = (bf16[4,64,512]{2,1,0:T(8,128)(2,1)S(1)}, bf16[4,64,512]{2,1,0:T(8,128)(2,1)S(1)}, u32[]{:S(2)}, u32[]{:S(2)}) collective-permute-start(bf16[4,64,512]{2,1,0:T(8,128)(2,1)S(1)} %shard_map.80), channel_id=1, source_target_pairs={{0,1},{1,0},{2,3},{3,2},{4,5},{5,4},{6,7},{7,6},{8,9},{9,8},{10,11... | collective-permute-start | bytes 786440 | tf_op jit(solution)/shard_map/ppermute | solution.py:14
  175.1 4.7 %collective-permute-start.60 = (bf16[128,256]{1,0:T(8,128)(2,1)S(1)}, bf16[128,256]{1,0:T(8,128)(2,1)S(1)}, u32[]{:S(2)}, u32[]{:S(2)}) collective-permute-start(bf16[128,256]{1,0:T(8,128)(2,1)S(1)} %get-tuple-element.161), channel_id=1, source_target_pairs={{0,4},{1,5},{2,6},{3,7},{4,0},{5,1},{6,2},{7,3},{8,12},{9,13},{10,... | collective-permute-start | bytes 196616 | tf_op jit(solution)/shard_map/ppermute | solution.py:14
  176.6 5.2 %collective-permute-start.61 = (bf16[128,256]{1,0:T(8,128)(2,1)S(1)}, bf16[128,256]{1,0:T(8,128)(2,1)S(1)}, u32[]{:S(2)}, u32[]{:S(2)}) collective-permute-start(bf16[128,256]{1,0:T(8,128)(2,1)S(1)} %get-tuple-element.162), channel_id=1, source_target_pairs={{0,6},{1,7},{2,4},{3,5},{4,2},{5,3},{6,0},{7,1},{8,14},{9,15},{10,... | collective-permute-start | bytes 196616 | tf_op jit(solution)/shard_map/ppermute | solution.py:14
  179.8 2.1 %collective-permute-start.62 = (bf16[4,64,256]{2,1,0:T(8,128)(2,1)S(1)}, bf16[4,64,256]{2,1,0:T(8,128)(2,1)S(1)}, u32[]{:S(2)}, u32[]{:S(2)}) collective-permute-start(bf16[4,64,256]{2,1,0:T(8,128)(2,1)S(1)} %shard_map.77), channel_id=1, source_target_pairs={{0,1},{1,0},{2,3},{3,2},{4,5},{5,4},{6,7},{7,6},{8,9},{9,8},{10,11... | collective-permute-start | bytes 393224 | tf_op jit(solution)/shard_map/ppermute | solution.py:14
  (39 other events, 405.2 us)

commit v2 on v1

--- a/solution.py
+++ b/solution.py
@@ -6,6 +6,7 @@
 from jax.sharding import PartitionSpec as P
 
 MIB = 1024 * 1024
+MIDDLE = 3 * 10**9
 LONG = 10**11
 
 
@@ -292,47 +293,66 @@
 def scale(slab_count, angular, held, came, order, core, cuts):
     share, cols = angular.shape
     group = len(held[0])
-    chunks = len(cuts)
+    batches = len(cuts)
+    widths = [sum(cols // cut for cut in batch) for batch in cuts]
+    amounts = [[group * (3 - cut) for cut in batch] for batch in cuts]
+    chunks = sum(len(batch) for batch in cuts)
 
     def body(ins, outs, scratch):
         place, core_now, angular_ref, *refs = ins
-        mine, theirs, sems = scratch
+        mine, theirs, sems, buffer, out_sems = scratch
         lines = pl.ds(pl.multiple_of(core_now[0] * share, share), share)
         copies = []
-        for k, cut in enumerate(cuts):
-            wide = pl.ds(0, cols // cut)
+        for k in range(batches):
+            wide = pl.ds(0, widths[k])
             pairs = [(refs[k * group + j].at[lines], mine.at[k, j, :, wide]) for j in range(group)]
-            pairs.append((refs[chunks * group + k], theirs.at[k, :, :, wide]))
+            pairs.append((refs[batches * group + k], theirs.at[k, :, :, wide]))
             for source, target in pairs:
                 copies.append(pltpu.make_async_copy(source, target, sems.at[len(copies)]))
                 copies[-1].start()
         yield
-        first = 0
-        for k, cut in enumerate(cuts):
+        first, leaving = 0, []
+        for k, batch in enumerate(cuts):
             for copy in copies[k * (group + 1) : (k + 1) * (group + 1)]:
                 copy.wait()
-            for kind in range(2):
-                source = core_now[0] if kind == 0 else 1 - core_now[0]
-                lanes = slice(None)
-                if cut == 2:
-                    lanes = pl.ds(pl.multiple_of(source * (cols // 2), cols // 2), cols // 2)
-                factor = angular_ref[:, lanes]
-                for j in range(group):
-                    slab = first + place[j] * (3 - cut) + (source if cut == 1 else 0)
-                    x = (mine if kind == 0 else theirs)[k, j, :, : cols // cut]
-                    value = factor * x.astype(jnp.float32)
-                    outs[0][slab, :, lanes] = value.astype(jnp.bfloat16)
-            first += group * (3 - cut)
+            begin = 0
+            for cut in batch:
+                wide = slice(begin, begin + cols // cut)
+                for kind in range(2):
+                    source = core_now[0] if kind == 0 else 1 - core_now[0]
+                    lanes = slice(None)
+                    if cut == 2:
+                        lanes = pl.ds(pl.multiple_of(source * (cols // 2), cols // 2), cols // 2)
+                    factor = angular_ref[:, lanes]
+                    for j in range(group):
+                        slab = first + place[j] * (3 - cut) + (source if cut == 1 else 0)
+                        x = (mine if kind == 0 else theirs)[k, j, :, wide]
+                        value = factor * x.astype(jnp.float32)
+                        buffer[slab, :, lanes] = value.astype(jnp.bfloat16)
+                amount = group * (3 - cut)
+                slabs_now = pl.ds(first, amount)
+                copy = pltpu.make_async_copy(
+                    buffer.at[slabs_now], outs[0].at[slabs_now], out_sems.at[len(leaving)]
+                )
+                copy.start()
+                leaving.append(copy)
+                first += amount
+                begin += cols // cut
+        yield
+        for copy in leaving:
+            copy.wait()
 
     flat = [x for xs in held for x in xs]
     return Step(
         body,
-        [((slab_count, share, cols), jnp.bfloat16, pltpu.VMEM)],
+        [((slab_count, share, cols), jnp.bfloat16, pl.ANY)],
         scalar(order) + scalar(core) + inside([angular]) + outside(flat + came),
         [
-            pltpu.VMEM((chunks, group, share, cols), jnp.bfloat16),
-            pltpu.VMEM((chunks, group, share, cols), jnp.bfloat16),
-            pltpu.SemaphoreType.DMA((chunks * (group + 1),)),
+            pltpu.VMEM((batches, group, share, max(widths)), jnp.bfloat16),
+            pltpu.VMEM((batches, group, share, max(widths)), jnp.bfloat16),
+            pltpu.SemaphoreType.DMA((batches * (group + 1),)),
+            pltpu.VMEM((slab_count, share, cols), jnp.bfloat16),
+            pltpu.SemaphoreType.DMA((chunks,)),
         ],
     )
 
@@ -360,9 +380,6 @@
     while bit:
         for v, x in list(gathered.items()):
             gathered[v ^ bit] = swap(x, bit)
-        if bit == n // 2:
-            rows_of[n // 4] = swap(orbitals, n // 4)
-            gathered[bit] = after([gathered[bit]], [rows_of[n // 4]])[0]
         bit //= 2
     column_blocks = [gathered[v] for v in range(n)]
 
@@ -405,7 +422,7 @@
             group,
             work,
         )
-        flat = call([step], tokens, 46)[0]
+        flat = call([step], tokens, 36)[0]
         for i, k in enumerate(ks):
             kept[k], other[k] = flat[2 * i : 2 * i + 2]
             if trade:
@@ -422,11 +439,7 @@
     transform([0], [angular])
     merge([0], [])
     came[0] = send(own[0])
-    bit = group // 2
-    while bit > 1:
-        for v, x in list(rows_of.items()):
-            rows_of[v ^ bit] = swap(x, bit)
-        bit //= 2
+    rows_of.update({2 * j: swap(orbitals, 2 * j) for j in range(1, group)})
     clock = after([jnp.zeros((8, 128), jnp.float32)], [own[0][0]], LONG)[0]
     if last:
         transform(list(range(1, last + 1)), [clock], 0, False)
@@ -452,7 +465,8 @@
 
     token = picked
     for k in range(last + 1):
-        step = second_transform(picked, [own[k][0]] + came[k], side, LONG if k else 0)
+        work = MIDDLE if k else 0
+        step = second_transform(picked, [own[k][0]] + came[k], side, work)
         far, near[k] = call([step], [token])[0]
         across[k] = swap(far, n // 2)
         token = far
@@ -463,9 +477,8 @@
         before = far
         if k:
             late = held[k - 2][1:] if k > 1 else []
-            sums[k - 1] = call(
-                [add_sides(near[k - 1], across[k - 1], member, group, LONG)], [token] + late
-            )[0]
+            step = add_sides(near[k - 1], across[k - 1], member, group, MIDDLE)
+            sums[k - 1] = call([step], [token] + late)[0]
             held[k - 1] = [sums[k - 1][0]] + send(sums[k - 1])
             token = sums[k - 1][0]
     clock = token
@@ -477,7 +490,13 @@
     final[last] = swap(call([for_other_core(held[last], core)])[0][0], 1)
     ks = range(last + 1)
     step = scale(
-        slab_count, angular, [held[k] for k in ks], [final[k] for k in ks], order, core, cuts
+        slab_count,
+        angular,
+        [held[k] for k in ks],
+        [final[k] for k in ks],
+        order,
+        core,
+        [[cut] for cut in cuts],
     )
     return call([step], (), 40)[0][0]
 

time: 188 us -> 182 us (0.968)
  starting transfers between devices: 60.3 us -> 75.7 us
  waiting for transfers between devices: 77 us -> 67.2 us
  Pallas kernels: 39.1 us -> 30.4 us
  local copies, waits for them, and re-layouts: 6.95 us -> 4.84 us
    ppermute x67, starting transfers between devices: 60.3 us -> 75.7 us  [swap(): return lax.ppermute(x, 'blk', [(i, i ^ bits) for i in range(n)])]
    ppermute x67, waiting for transfers between devices: 77 us -> 67.2 us  [swap(): return lax.ppermute(x, 'blk', [(i, i ^ bits) for i in range(n)])]
    pallas_call x28 -> x27, Pallas kernels: 39.1 us -> 30.4 us  [call(): pl.pallas_call(body, out_shape=[jax.ShapeDtypeStruct(shape, kind) for sha...]
    unnamed x72 -> x36, local copies, waits for them, and re-layouts: 4.59 us -> 2.48 us
  transfers between devices with their start and end apart: 67 -> 67, of which waited for: 23 -> 27; matrix products, arithmetic and copies ran while one was open for 3% -> 2% of each run, Pallas kernels for 19% -> 15%
where the time goes in v2:
time: 182 us
  starting transfers between devices  75.7 us (42%)
  waiting for transfers between devices  67.2 us (37%)
  Pallas kernels  30.4 us (17%)
  local copies, waits for them, and re-layouts  4.84 us (3%)
  matrix products  2.53 us (1%)
    ppermute x67, starting transfers between devices, swap(): return lax.ppermute(x, 'blk', [(i, i ^ bits) for i in range(n)])  75.7 us
    ppermute x67, waiting for transfers between devices, swap(): return lax.ppermute(x, 'blk', [(i, i ^ bits) for i in range(n)])  67.2 us
    pallas_call x27, Pallas kernels, call(): pl.pallas_call(body, out_shape=[jax.ShapeDtypeStruct(shape, kind) for sha...  30.4 us
  transfers between devices with their start and end apart: 67, of which 27 were waited for; matrix products, arithmetic and copies ran while one was open for 2% of the time, Pallas kernels for 15%

profile of v2, /device:TPU:0, one launch (start us, length us, event | category | flops | bytes accessed | tf_op | source)
XLA Modules:
  0.0 181.8 jit_solution(15955685671845300290)
XLA Ops:
  0.0 0.8 dynamic_slice.11
  0.8 1.4 fusion.3.refs_4_
  2.2 4.1 %collective-permute-start.8 = (bf16[128,512]{1,0:T(8,128)(2,1)S(1)}, bf16[128,512]{1,0:T(8,128)(2,1)S(1)}, u32[]{:S(2)}, u32[]{:S(2)}) collective-permute-start(bf16[128,512]{1,0:T(8,128)(2,1)S(1)} %fusion.3.refs_4_), channel_id=1, source_target_pairs={{0,8},{1,9},{2,10},{3,11},{4,12},{5,13},{6,14},{7,15},{8,0},{9,1},... | collective-permute-start | bytes 393224 | tf_op jit(solution)/shard_map/ppermute | solution.py:15
  6.3 1.6 collective-permute-start.4
  7.9 1.5 collective-permute-start.2
  9.4 0.8 dynamic_slice.10
  10.2 0.8 dynamic_slice.9
  10.9 1.8 collective-permute-done.8.refs_12_
  13.3 0.9 fusion.5
  14.2 1.6 collective-permute-start.10
  16.6 1.1 collective-permute-done.12.refs_16_
  17.7 1.6 collective-permute-start.14
  20.5 2.3 %collective-permute-done.6.refs_10_ = bf16[128,512]{1,0:T(8,128)(2,1)S(1)} collective-permute-done((bf16[128,512]{1,0:T(8,128)(2,1)S(1)}, bf16[128,512]{1,0:T(8,128)(2,1)S(1)}, u32[]{:S(2)}, u32[]{:S(2)}) %collective-permute-start.6) | collective-permute-done | bytes 131104 | tf_op jit(solution)/shard_map/ppermute | solution.py:15
  23.3 1.8 collective-permute-done.14.refs_18_
  25.1 1.3 collective-permute-start.21
  26.4 1.6 collective-permute-start.20
  28.7 3.5 %shard_map.55 = (bf16[4,128,256]{2,1,0:T(8,128)(2,1)S(1)}, bf16[4,128,256]{2,1,0:T(8,128)(2,1)S(1)}) custom-call(s32[1]{0:T(128)} %bitcast.3.refs_0_, s32[1]{0:T(128)} %bitcast.refs_1_.refs_0_, s32[4]{0:T(128)S(1)} %iota_xor_fusion.refs_2_.refs_0_, bf16[32,128,2048]{2,1,0:T(8,128)(2,1)} %refs_3_.3, bf16[128,512]{1,0:T(8,128)(2,1)S(1)} %fusion.3.refs_4_, ...), custom_call_target="tpu_custom_call" | custom-call | tf_op jit(solution)/shard_map/pallas_call | solution.py:52
  32.3 1.4 collective-permute-done.16.refs_1_
  33.8 1.6 collective-permute-start.17
  35.4 1.3 collective-permute-start.18
  37.4 11.3 %shard_map.58 = (bf16[4,128,512]{2,1,0:T(8,128)(2,1)S(1)}, bf16[4,128,512]{2,1,0:T(8,128)(2,1)S(1)}, bf16[4,128,512]{2,1,0:T(8,128)(2,1)S(1)}, bf16[4,128,512]{2...) custom-call(s32[1]{0:T(128)} %bitcast.3.refs_0_, ...), custom_call_target="tpu_custom_call" | custom-call | tf_op jit(solution)/shard_map/pallas_call | solution.py:52
  48.9 0.9 copy-done
  49.8 0.8 copy-done.2
  53.9 1.5 collective-permute-start.28
  55.4 1.3 collective-permute-start.29
  57.4 6.2 %shard_map.60.refs_1_.refs_6_ = bf16[1024,1024]{1,0:T(8,128)(2,1)S(1)} custom-call(bf16[1024,1024]{1,0:T(8,128)(2,1)S(1)} %fusion.refs_0_, bf16[128,1024]{1,0:T(8,128)(2,1)} %refs_1_.1, bf16[128,1024]{1,0:T(8,128)(2,1)} %collective-permute-done.refs_2_, bf16[128,1024]{1,0:T(8,128)(2,1)} %get-tuple-element.95.refs_3_, ...), custom_call_target="tpu_custom_call" | custom-call | flops 99999997952 | tf_op jit(solution)/shard_map/pallas_call | solution.py:52
  64.3 3.4 %collective-permute-start.26 = (bf16[512,256]{1,0:T(8,128)(2,1)S(1)}, bf16[512,256]{1,0:T(8,128)(2,1)S(1)}, u32[]{:S(2)}, u32[]{:S(2)}) collective-permute-start(bf16[512,256]{1,0:T(8,128)(2,1)S(1)} %get-tuple-element.102.refs_6_.refs_3_), channel_id=1, source_target_pairs={{0,8},{1,9},{2,10},{3,11},{4,12},{5,13},{6,14},{7,15},{8,0},{9,1},... | collective-permute-start | bytes 786440 | tf_op jit(solution)/shard_map/ppermute | solution.py:15
  68.0 1.6 collective-permute-start.38
  69.8 1.7 collective-permute-start.40
  71.5 1.3 shard_map.63
  72.8 2.1 %collective-permute-start.34 = (bf16[512,512]{1,0:T(8,128)(2,1)S(1)}, bf16[512,512]{1,0:T(8,128)(2,1)S(1)}, u32[]{:S(2)}, u32[]{:S(2)}) collective-permute-start(bf16[512,512]{1,0:T(8,128)(2,1)S(1)} %get-tuple-element.109.refs_3_), channel_id=1, source_target_pairs={{0,8},{1,9},{2,10},{3,11},{4,12},{5,13},{6,14},{7,15},{8,0},{9,1},... | collective-permute-start | bytes 1572872 | tf_op jit(solution)/shard_map/ppermute | solution.py:15
  74.8 5.8 %collective-permute-done.26.refs_2_ = bf16[512,256]{1,0:T(8,128)(2,1)S(1)} collective-permute-done((bf16[512,256]{1,0:T(8,128)(2,1)S(1)}, bf16[512,256]{1,0:T(8,128)(2,1)S(1)}, u32[]{:S(2)}, u32[]{:S(2)}) %collective-permute-start.26) | collective-permute-done | bytes 262176 | tf_op jit(solution)/shard_map/ppermute | solution.py:15
  80.7 1.6 collective-permute-start.31
  82.3 8.8 %collective-permute-done.39.refs_4_ = bf16[256,512]{1,0:T(8,128)(2,1)S(1)} collective-permute-done((bf16[256,512]{1,0:T(8,128)(2,1)S(1)}, bf16[256,512]{1,0:T(8,128)(2,1)S(1)}, u32[]{:S(2)}, u32[]{:S(2)}) %collective-permute-start.39) | collective-permute-done | bytes 262176 | tf_op jit(solution)/shard_map/ppermute | solution.py:15
  91.2 4.5 %collective-permute-done.40.refs_5_ = bf16[256,512]{1,0:T(8,128)(2,1)S(1)} collective-permute-done((bf16[256,512]{1,0:T(8,128)(2,1)S(1)}, bf16[256,512]{1,0:T(8,128)(2,1)S(1)}, u32[]{:S(2)}, u32[]{:S(2)}) %collective-permute-start.40) | collective-permute-done | bytes 262176 | tf_op jit(solution)/shard_map/ppermute | solution.py:15
  95.7 1.2 shard_map.67
  97.0 2.7 %collective-permute-start.45 = (bf16[256,512]{1,0:T(8,128)(2,1)S(1)}, bf16[256,512]{1,0:T(8,128)(2,1)S(1)}, u32[]{:S(2)}, u32[]{:S(2)}) collective-permute-start(bf16[256,512]{1,0:T(8,128)(2,1)S(1)} %get-tuple-element.137), channel_id=1, source_target_pairs={{0,2},{1,3},{2,0},{3,1},{4,6},{5,7},{6,4},{7,5},{8,10},{9,11},{10,... | collective-permute-start | bytes 786440 | tf_op jit(solution)/shard_map/ppermute | solution.py:15
  99.7 1.3 collective-permute-start.46
  101.0 2.3 %collective-permute-start.47 = (bf16[256,512]{1,0:T(8,128)(2,1)S(1)}, bf16[256,512]{1,0:T(8,128)(2,1)S(1)}, u32[]{:S(2)}, u32[]{:S(2)}) collective-permute-start(bf16[256,512]{1,0:T(8,128)(2,1)S(1)} %get-tuple-element.139), channel_id=1, source_target_pairs={{0,6},{1,7},{2,4},{3,5},{4,2},{5,3},{6,0},{7,1},{8,14},{9,15},{10,... | collective-permute-start | bytes 786440 | tf_op jit(solution)/shard_map/ppermute | solution.py:15
  104.0 11.8 %collective-permute-start.52 = (bf16[256,256]{1,0:T(8,128)(2,1)S(1)}, bf16[256,256]{1,0:T(8,128)(2,1)S(1)}, u32[]{:S(2)}, u32[]{:S(2)}) collective-permute-start(bf16[256,256]{1,0:T(8,128)(2,1)S(1)} %get-tuple-element.150), channel_id=1, source_target_pairs={{0,2},{1,3},{2,0},{3,1},{4,6},{5,7},{6,4},{7,5},{8,10},{9,11},{10,... | collective-permute-start | bytes 393224 | tf_op jit(solution)/shard_map/ppermute | solution.py:15
  116.0 0.8 collective-permute-done.46.refs_4_
  116.8 2.5 %collective-permute-start.42 = (bf16[128,512]{1,0:T(8,128)(2,1)S(1)}, bf16[128,512]{1,0:T(8,128)(2,1)S(1)}, u32[]{:S(2)}, u32[]{:S(2)}) collective-permute-start(bf16[128,512]{1,0:T(8,128)(2,1)S(1)} %get-tuple-element.130), channel_id=1, source_target_pairs={{0,4},{1,5},{2,6},{3,7},{4,0},{5,1},{6,2},{7,3},{8,12},{9,13},{10,... | collective-permute-start | bytes 393224 | tf_op jit(solution)/shard_map/ppermute | solution.py:15
  119.3 3.2 %collective-permute-done.47.refs_5_ = bf16[256,512]{1,0:T(8,128)(2,1)S(1)} collective-permute-done((bf16[256,512]{1,0:T(8,128)(2,1)S(1)}, bf16[256,512]{1,0:T(8,128)(2,1)S(1)}, u32[]{:S(2)}, u32[]{:S(2)}) %collective-permute-start.47) | collective-permute-done | bytes 262176 | tf_op jit(solution)/shard_map/ppermute | solution.py:15
  122.5 3.4 %collective-permute-start.43 = (bf16[128,512]{1,0:T(8,128)(2,1)S(1)}, bf16[128,512]{1,0:T(8,128)(2,1)S(1)}, u32[]{:S(2)}, u32[]{:S(2)}) collective-permute-start(bf16[128,512]{1,0:T(8,128)(2,1)S(1)} %get-tuple-element.131), channel_id=1, source_target_pairs={{0,6},{1,7},{2,4},{3,5},{4,2},{5,3},{6,0},{7,1},{8,14},{9,15},{10,... | collective-permute-start | bytes 393224 | tf_op jit(solution)/shard_map/ppermute | solution.py:15
  125.9 1.3 shard_map.70
  127.2 2.7 %collective-permute-start.54 = (bf16[256,256]{1,0:T(8,128)(2,1)S(1)}, bf16[256,256]{1,0:T(8,128)(2,1)S(1)}, u32[]{:S(2)}, u32[]{:S(2)}) collective-permute-start(bf16[256,256]{1,0:T(8,128)(2,1)S(1)} %get-tuple-element.152), channel_id=1, source_target_pairs={{0,6},{1,7},{2,4},{3,5},{4,2},{5,3},{6,0},{7,1},{8,14},{9,15},{10,... | collective-permute-start | bytes 393224 | tf_op jit(solution)/shard_map/ppermute | solution.py:15
  130.0 4.0 %collective-permute-start.51 = (bf16[512,512]{1,0:T(8,128)(2,1)S(1)}, bf16[512,512]{1,0:T(8,128)(2,1)S(1)}, u32[]{:S(2)}, u32[]{:S(2)}) collective-permute-start(bf16[512,512]{1,0:T(8,128)(2,1)S(1)} %get-tuple-element.140.refs_3_), channel_id=1, source_target_pairs={{0,8},{1,9},{2,10},{3,11},{4,12},{5,13},{6,14},{7,15},{8,0},{9,1},... | collective-permute-start | bytes 1572872 | tf_op jit(solution)/shard_map/ppermute | solution.py:15
  134.3 0.8 collective-permute-start.49
  135.1 4.8 %collective-permute-done.53.refs_4_ = bf16[256,256]{1,0:T(8,128)(2,1)S(1)} collective-permute-done((bf16[256,256]{1,0:T(8,128)(2,1)S(1)}, bf16[256,256]{1,0:T(8,128)(2,1)S(1)}, u32[]{:S(2)}, u32[]{:S(2)}) %collective-permute-start.53) | collective-permute-done | bytes 131104 | tf_op jit(solution)/shard_map/ppermute | solution.py:15
  139.9 2.5 %collective-permute-done.54.refs_5_ = bf16[256,256]{1,0:T(8,128)(2,1)S(1)} collective-permute-done((bf16[256,256]{1,0:T(8,128)(2,1)S(1)}, bf16[256,256]{1,0:T(8,128)(2,1)S(1)}, u32[]{:S(2)}, u32[]{:S(2)}) %collective-permute-start.54) | collective-permute-done | bytes 131104 | tf_op jit(solution)/shard_map/ppermute | solution.py:15
  142.4 0.7 shard_map.73
  143.7 5.7 %collective-permute-done.49.refs_5_.refs_3_.refs_13_ = bf16[128,512]{1,0:T(8,128)(2,1)S(1)} collective-permute-done((bf16[128,512]{1,0:T(8,128)(2,1)S(1)}, bf16[128,512]{1,0:T(8,128)(2,1)S(1)}, u32[]{:S(2)}, u32[]{:S(2)}) %collective-permute-start.49) | collective-permute-done | bytes 131104 | tf_op jit(solution)/shard_map/ppermute | solution.py:15
  149.5 2.8 %collective-permute-done.50.refs_6_.refs_4_.refs_14_ = bf16[128,512]{1,0:T(8,128)(2,1)S(1)} collective-permute-done((bf16[128,512]{1,0:T(8,128)(2,1)S(1)}, bf16[128,512]{1,0:T(8,128)(2,1)S(1)}, u32[]{:S(2)}, u32[]{:S(2)}) %collective-permute-start.50) | collective-permute-done | bytes 131104 | tf_op jit(solution)/shard_map/ppermute | solution.py:15
  152.3 9.4 %collective-permute-done.51.refs_2_ = bf16[512,512]{1,0:T(8,128)(2,1)S(1)} collective-permute-done((bf16[512,512]{1,0:T(8,128)(2,1)S(1)}, bf16[512,512]{1,0:T(8,128)(2,1)S(1)}, u32[]{:S(2)}, u32[]{:S(2)}) %collective-permute-start.51) | collective-permute-done | bytes 524320 | tf_op jit(solution)/shard_map/ppermute | solution.py:15
  161.8 1.3 collective-permute-start.55
  163.1 2.3 %collective-permute-start.57 = (bf16[128,512]{1,0:T(8,128)(2,1)S(1)}, bf16[128,512]{1,0:T(8,128)(2,1)S(1)}, u32[]{:S(2)}, u32[]{:S(2)}) collective-permute-start(bf16[128,512]{1,0:T(8,128)(2,1)S(1)} %get-tuple-element.157), channel_id=1, source_target_pairs={{0,6},{1,7},{2,4},{3,5},{4,2},{5,3},{6,0},{7,1},{8,14},{9,15},{10,... | collective-permute-start | bytes 393224 | tf_op jit(solution)/shard_map/ppermute | solution.py:15
  165.5 1.3 collective-permute-start.59
  166.9 1.4 collective-permute-done.55.refs_2_.refs_16_
  168.4 2.2 %collective-permute-done.57.refs_4_.refs_18_ = bf16[128,512]{1,0:T(8,128)(2,1)S(1)} collective-permute-done((bf16[128,512]{1,0:T(8,128)(2,1)S(1)}, bf16[128,512]{1,0:T(8,128)(2,1)S(1)}, u32[]{:S(2)}, u32[]{:S(2)}) %collective-permute-start.57) | collective-permute-done | bytes 131104 | tf_op jit(solution)/shard_map/ppermute | solution.py:15
  171.3 1.7 collective-permute-start.61
  173.0 2.6 %collective-permute-done.60.refs_3_.refs_21_ = bf16[128,256]{1,0:T(8,128)(2,1)S(1)} collective-permute-done((bf16[128,256]{1,0:T(8,128)(2,1)S(1)}, bf16[128,256]{1,0:T(8,128)(2,1)S(1)}, u32[]{:S(2)}, u32[]{:S(2)}) %collective-permute-start.60) | collective-permute-done | bytes 65568 | tf_op jit(solution)/shard_map/ppermute | solution.py:15
  175.6 1.2 collective-permute-done.61.refs_4_.refs_22_
  176.9 1.3 collective-permute-done.66.refs_27_
  178.2 3.4 %shard_map.81 = bf16[32,64,512]{2,1,0:T(8,128)(2,1)} custom-call(s32[4]{0:T(128)S(1)} %copy-done.16, s32[1]{0:T(128)} %bitcast.refs_1_.refs_0_, f32[64,512]{1,0:T(8,128)S(1)} %convolution_multiply_fusion.refs_20_.refs_2_, bf16[128,256]{1,0:T(8,128)(2,1)S(1)} %get-tuple-element.110.refs_6_.refs_1_.refs_3_, ...), custom_call_target="tpu_custom_call" | custom-call | tf_op jit(solution)/shard_map/pallas_call | solution.py:52
  (147 shorter events, 13.2 us)
Async XLA Ops:
  2.2 10.5 %collective-permute-start.8 = (bf16[128,512]{1,0:T(8,128)(2,1)S(1)}, bf16[128,512]{1,0:T(8,128)(2,1)S(1)}, u32[]{:S(2)}, u32[]{:S(2)}) collective-permute-start(bf16[128,512]{1,0:T(8,128)(2,1)S(1)} %fusion.3.refs_4_), channel_id=1, source_target_pairs={{0,8},{1,9},{2,10},{3,11},{4,12},{5,13},{6,14},{7,15},{8,0},{9,1},... | collective-permute-start | bytes 393224 | tf_op jit(solution)/shard_map/ppermute | solution.py:15
  6.3 9.5 %collective-permute-start.4 = (bf16[128,512]{1,0:T(8,128)(2,1)S(1)}, bf16[128,512]{1,0:T(8,128)(2,1)S(1)}, u32[]{:S(2)}, u32[]{:S(2)}) collective-permute-start(bf16[128,512]{1,0:T(8,128)(2,1)S(1)} %fusion.3.refs_4_), channel_id=1, source_target_pairs={{0,4},{1,5},{2,6},{3,7},{4,0},{5,1},{6,2},{7,3},{8,12},{9,13},{10,... | collective-permute-start | bytes 393224 | tf_op jit(solution)/shard_map/ppermute | solution.py:15
  7.9 7.9 %collective-permute-start.2 = (bf16[128,512]{1,0:T(8,128)(2,1)S(1)}, bf16[128,512]{1,0:T(8,128)(2,1)S(1)}, u32[]{:S(2)}, u32[]{:S(2)}) collective-permute-start(bf16[128,512]{1,0:T(8,128)(2,1)S(1)} %fusion.3.refs_4_), channel_id=1, source_target_pairs={{0,2},{1,3},{2,0},{3,1},{4,6},{5,7},{6,4},{7,5},{8,10},{9,11},{10,... | collective-permute-start | bytes 393224 | tf_op jit(solution)/shard_map/ppermute | solution.py:15
  9.4 7.0 %collective-permute-start.1 = (bf16[128,512]{1,0:T(8,128)(2,1)S(1)}, bf16[128,512]{1,0:T(8,128)(2,1)S(1)}, u32[]{:S(2)}, u32[]{:S(2)}) collective-permute-start(bf16[128,512]{1,0:T(8,128)(2,1)S(1)} %fusion.3.refs_4_), channel_id=1, source_target_pairs={{0,1},{1,0},{2,3},{3,2},{4,5},{5,4},{6,7},{7,6},{8,9},{9,8},{10,11... | collective-permute-start | bytes 393224 | tf_op jit(solution)/shard_map/ppermute | solution.py:15
  12.7 5.0 %collective-permute-start.12 = (bf16[128,512]{1,0:T(8,128)(2,1)S(1)}, bf16[128,512]{1,0:T(8,128)(2,1)S(1)}, u32[]{:S(2)}, u32[]{:S(2)}) collective-permute-start(bf16[128,512]{1,0:T(8,128)(2,1)S(1)} %collective-permute-done.8.refs_12_), channel_id=1, source_target_pairs={{0,4},{1,5},{2,6},{3,7},{4,0},{5,1},{6,2},{7,3},{8,12},{9,13},{10,... | collective-permute-start | bytes 393224 | tf_op jit(solution)/shard_map/ppermute | solution.py:15
  14.2 5.7 %collective-permute-start.10 = (bf16[128,512]{1,0:T(8,128)(2,1)S(1)}, bf16[128,512]{1,0:T(8,128)(2,1)S(1)}, u32[]{:S(2)}, u32[]{:S(2)}) collective-permute-start(bf16[128,512]{1,0:T(8,128)(2,1)S(1)} %collective-permute-done.8.refs_12_), channel_id=1, source_target_pairs={{0,2},{1,3},{2,0},{3,1},{4,6},{5,7},{6,4},{7,5},{8,10},{9,11},{10,... | collective-permute-start | bytes 393224 | tf_op jit(solution)/shard_map/ppermute | solution.py:15
  15.8 4.1 %collective-permute-start.9 = (bf16[128,512]{1,0:T(8,128)(2,1)S(1)}, bf16[128,512]{1,0:T(8,128)(2,1)S(1)}, u32[]{:S(2)}, u32[]{:S(2)}) collective-permute-start(bf16[128,512]{1,0:T(8,128)(2,1)S(1)} %collective-permute-done.8.refs_12_), channel_id=1, source_target_pairs={{0,1},{1,0},{2,3},{3,2},{4,5},{5,4},{6,7},{7,6},{8,9},{9,8},{10,11... | collective-permute-start | bytes 393224 | tf_op jit(solution)/shard_map/ppermute | solution.py:15
  15.8 6.9 %collective-permute-start.6 = (bf16[128,512]{1,0:T(8,128)(2,1)S(1)}, bf16[128,512]{1,0:T(8,128)(2,1)S(1)}, u32[]{:S(2)}, u32[]{:S(2)}) collective-permute-start(bf16[128,512]{1,0:T(8,128)(2,1)S(1)} %collective-permute-done.4.refs_8_), channel_id=1, source_target_pairs={{0,2},{1,3},{2,0},{3,1},{4,6},{5,7},{6,4},{7,5},{8,10},{9,11},{10,... | collective-permute-start | bytes 393224 | tf_op jit(solution)/shard_map/ppermute | solution.py:15
  16.4 6.3 %collective-permute-start.5 = (bf16[128,512]{1,0:T(8,128)(2,1)S(1)}, bf16[128,512]{1,0:T(8,128)(2,1)S(1)}, u32[]{:S(2)}, u32[]{:S(2)}) collective-permute-start(bf16[128,512]{1,0:T(8,128)(2,1)S(1)} %collective-permute-done.4.refs_8_), channel_id=1, source_target_pairs={{0,1},{1,0},{2,3},{3,2},{4,5},{5,4},{6,7},{7,6},{8,9},{9,8},{10,11... | collective-permute-start | bytes 393224 | tf_op jit(solution)/shard_map/ppermute | solution.py:15
  17.7 7.4 %collective-permute-start.14 = (bf16[128,512]{1,0:T(8,128)(2,1)S(1)}, bf16[128,512]{1,0:T(8,128)(2,1)S(1)}, u32[]{:S(2)}, u32[]{:S(2)}) collective-permute-start(bf16[128,512]{1,0:T(8,128)(2,1)S(1)} %collective-permute-done.12.refs_16_), channel_id=1, source_target_pairs={{0,2},{1,3},{2,0},{3,1},{4,6},{5,7},{6,4},{7,5},{8,10},{9,11},{10,... | collective-permute-start | bytes 393224 | tf_op jit(solution)/shard_map/ppermute | solution.py:15
  19.9 5.2 %collective-permute-start.3 = (bf16[128,512]{1,0:T(8,128)(2,1)S(1)}, bf16[128,512]{1,0:T(8,128)(2,1)S(1)}, u32[]{:S(2)}, u32[]{:S(2)}) collective-permute-start(bf16[128,512]{1,0:T(8,128)(2,1)S(1)} %collective-permute-done.2.refs_6_), channel_id=1, source_target_pairs={{0,1},{1,0},{2,3},{3,2},{4,5},{5,4},{6,7},{7,6},{8,9},{9,8},{10,11... | collective-permute-start | bytes 393224 | tf_op jit(solution)/shard_map/ppermute | solution.py:15
  20.0 6.5 %collective-permute-start.13 = (bf16[128,512]{1,0:T(8,128)(2,1)S(1)}, bf16[128,512]{1,0:T(8,128)(2,1)S(1)}, u32[]{:S(2)}, u32[]{:S(2)}) collective-permute-start(bf16[128,512]{1,0:T(8,128)(2,1)S(1)} %collective-permute-done.12.refs_16_), channel_id=1, source_target_pairs={{0,1},{1,0},{2,3},{3,2},{4,5},{5,4},{6,7},{7,6},{8,9},{9,8},{10,11... | collective-permute-start | bytes 393224 | tf_op jit(solution)/shard_map/ppermute | solution.py:15
  22.8 5.2 %collective-permute-start.11 = (bf16[128,512]{1,0:T(8,128)(2,1)S(1)}, bf16[128,512]{1,0:T(8,128)(2,1)S(1)}, u32[]{:S(2)}, u32[]{:S(2)}) collective-permute-start(bf16[128,512]{1,0:T(8,128)(2,1)S(1)} %collective-permute-done.10.refs_14_), channel_id=1, source_target_pairs={{0,1},{1,0},{2,3},{3,2},{4,5},{5,4},{6,7},{7,6},{8,9},{9,8},{10,11... | collective-permute-start | bytes 393224 | tf_op jit(solution)/shard_map/ppermute | solution.py:15
  22.8 5.9 %collective-permute-start.7 = (bf16[128,512]{1,0:T(8,128)(2,1)S(1)}, bf16[128,512]{1,0:T(8,128)(2,1)S(1)}, u32[]{:S(2)}, u32[]{:S(2)}) collective-permute-start(bf16[128,512]{1,0:T(8,128)(2,1)S(1)} %collective-permute-done.6.refs_10_), channel_id=1, source_target_pairs={{0,1},{1,0},{2,3},{3,2},{4,5},{5,4},{6,7},{7,6},{8,9},{9,8},{10,11... | collective-permute-start | bytes 393224 | tf_op jit(solution)/shard_map/ppermute | solution.py:15
  25.1 3.6 %collective-permute-start.15 = (bf16[128,512]{1,0:T(8,128)(2,1)S(1)}, bf16[128,512]{1,0:T(8,128)(2,1)S(1)}, u32[]{:S(2)}, u32[]{:S(2)}) collective-permute-start(bf16[128,512]{1,0:T(8,128)(2,1)S(1)} %collective-permute-done.14.refs_18_), channel_id=1, source_target_pairs={{0,1},{1,0},{2,3},{3,2},{4,5},{5,4},{6,7},{7,6},{8,9},{9,8},{10,11... | collective-permute-start | bytes 393224 | tf_op jit(solution)/shard_map/ppermute | solution.py:15
  25.1 11.6 %collective-permute-start.21 = (bf16[128,1024]{1,0:T(8,128)(2,1)}, bf16[128,1024]{1,0:T(8,128)(2,1)S(1)}, u32[]{:S(2)}, u32[]{:S(2)}) collective-permute-start(bf16[128,1024]{1,0:T(8,128)(2,1)} %refs_1_.1), channel_id=1, source_target_pairs={{0,4},{1,5},{2,6},{3,7},{4,0},{5,1},{6,2},{7,3},{8,12},{9,13},{10,... | collective-permute-start | bytes 786440 | tf_op jit(solution)/shard_map/ppermute | solution.py:15
  26.4 22.4 %collective-permute-start.20 = (bf16[128,1024]{1,0:T(8,128)(2,1)}, bf16[128,1024]{1,0:T(8,128)(2,1)}, u32[]{:S(2)}, u32[]{:S(2)}) collective-permute-start(bf16[128,1024]{1,0:T(8,128)(2,1)} %refs_1_.1), channel_id=1, source_target_pairs={{0,2},{1,3},{2,0},{3,1},{4,6},{5,7},{6,4},{7,5},{8,10},{9,11},{10,... | collective-permute-start | bytes 786440 | tf_op jit(solution)/shard_map/ppermute | solution.py:15
  28.0 20.8 %collective-permute-start.22 = (bf16[128,1024]{1,0:T(8,128)(2,1)}, bf16[128,1024]{1,0:T(8,128)(2,1)}, u32[]{:S(2)}, u32[]{:S(2)}) collective-permute-start(bf16[128,1024]{1,0:T(8,128)(2,1)} %refs_1_.1), channel_id=1, source_target_pairs={{0,6},{1,7},{2,4},{3,5},{4,2},{5,3},{6,0},{7,1},{8,14},{9,15},{10,... | collective-permute-start | bytes 786440 | tf_op jit(solution)/shard_map/ppermute | solution.py:15
  33.8 15.0 %collective-permute-start.17 = (bf16[256,256]{1,0:T(8,128)(2,1)S(1)}, bf16[256,256]{1,0:T(8,128)(2,1)S(1)}, u32[]{:S(2)}, u32[]{:S(2)}) collective-permute-start(bf16[256,256]{1,0:T(8,128)(2,1)S(1)} %get-tuple-element.86), channel_id=1, source_target_pairs={{0,2},{1,3},{2,0},{3,1},{4,6},{5,7},{6,4},{7,5},{8,10},{9,11},{10,... | collective-permute-start | bytes 393224 | tf_op jit(solution)/shard_map/ppermute | solution.py:15
  35.4 13.4 %collective-permute-start.18 = (bf16[256,256]{1,0:T(8,128)(2,1)S(1)}, bf16[256,256]{1,0:T(8,128)(2,1)S(1)}, u32[]{:S(2)}, u32[]{:S(2)}) collective-permute-start(bf16[256,256]{1,0:T(8,128)(2,1)S(1)} %get-tuple-element.87), channel_id=1, source_target_pairs={{0,4},{1,5},{2,6},{3,7},{4,0},{5,1},{6,2},{7,3},{8,12},{9,13},{10,... | collective-permute-start | bytes 393224 | tf_op jit(solution)/shard_map/ppermute | solution.py:15
  36.7 12.1 %collective-permute-start.19 = (bf16[256,256]{1,0:T(8,128)(2,1)S(1)}, bf16[256,256]{1,0:T(8,128)(2,1)S(1)}, u32[]{:S(2)}, u32[]{:S(2)}) collective-permute-start(bf16[256,256]{1,0:T(8,128)(2,1)S(1)} %get-tuple-element.88), channel_id=1, source_target_pairs={{0,6},{1,7},{2,4},{3,5},{4,2},{5,3},{6,0},{7,1},{8,14},{9,15},{10,... | collective-permute-start | bytes 393224 | tf_op jit(solution)/shard_map/ppermute | solution.py:15
  50.6 2.0 %collective-permute-start.27 = (bf16[4,128,512]{2,1,0:T(8,128)(2,1)S(1)}, bf16[4,128,512]{2,1,0:T(8,128)(2,1)S(1)}, u32[]{:S(2)}, u32[]{:S(2)}) collective-permute-start(bf16[4,128,512]{2,1,0:T(8,128)(2,1)S(1)} %get-tuple-element.104), channel_id=1, source_target_pairs={{0,1},{1,0},{2,3},{3,2},{4,5},{5,4},{6,7},{7,6},{8,9},{9,8},{10,11... | collective-permute-start | bytes 1572872 | tf_op jit(solution)/shard_map/ppermute | solution.py:15
  51.4 1.9 %collective-permute-start = (bf16[128,1024]{1,0:T(8,128)(2,1)}, bf16[128,1024]{1,0:T(8,128)(2,1)}, u32[]{:S(2)}, u32[]{:S(2)}) collective-permute-start(bf16[128,1024]{1,0:T(8,128)(2,1)} %refs_1_.1), channel_id=1, source_target_pairs={{0,1},{1,0},{2,3},{3,2},{4,5},{5,4},{6,7},{7,6},{8,9},{9,8},{10,11... | collective-permute-start | bytes 786440 | tf_op jit(solution)/shard_map/ppermute | solution.py:15
  51.4 2.3 %collective-permute-start.37 = (bf16[4,128,256]{2,1,0:T(8,128)(2,1)}, bf16[4,128,256]{2,1,0:T(8,128)(2,1)S(1)}, u32[]{:S(2)}, u32[]{:S(2)}) collective-permute-start(bf16[4,128,256]{2,1,0:T(8,128)(2,1)} %copy-done.14), channel_id=1, source_target_pairs={{0,1},{1,0},{2,3},{3,2},{4,5},{5,4},{6,7},{7,6},{8,9},{9,8},{10,11... | collective-permute-start | bytes 786440 | tf_op jit(solution)/shard_map/ppermute | solution.py:15
  51.9 2.0 %collective-permute-start.23 = (bf16[128,1024]{1,0:T(8,128)(2,1)}, bf16[128,1024]{1,0:T(8,128)(2,1)S(1)}, u32[]{:S(2)}, u32[]{:S(2)}) collective-permute-start(bf16[128,1024]{1,0:T(8,128)(2,1)} %get-tuple-element.95.refs_3_), channel_id=1, source_target_pairs={{0,1},{1,0},{2,3},{3,2},{4,5},{5,4},{6,7},{7,6},{8,9},{9,8},{10,11... | collective-permute-start | bytes 786440 | tf_op jit(solution)/shard_map/ppermute | solution.py:15
  51.9 3.5 %collective-permute-start.24 = (bf16[128,1024]{1,0:T(8,128)(2,1)}, bf16[128,1024]{1,0:T(8,128)(2,1)S(1)}, u32[]{:S(2)}, u32[]{:S(2)}) collective-permute-start(bf16[128,1024]{1,0:T(8,128)(2,1)} %copy-done.12), channel_id=1, source_target_pairs={{0,1},{1,0},{2,3},{3,2},{4,5},{5,4},{6,7},{7,6},{8,9},{9,8},{10,11... | collective-permute-start | bytes 786440 | tf_op jit(solution)/shard_map/ppermute | solution.py:15
  52.6 4.1 %collective-permute-start.25 = (bf16[128,1024]{1,0:T(8,128)(2,1)}, bf16[128,1024]{1,0:T(8,128)(2,1)S(1)}, u32[]{:S(2)}, u32[]{:S(2)}) collective-permute-start(bf16[128,1024]{1,0:T(8,128)(2,1)} %get-tuple-element.97.refs_7_), channel_id=1, source_target_pairs={{0,1},{1,0},{2,3},{3,2},{4,5},{5,4},{6,7},{7,6},{8,9},{9,8},{10,11... | collective-permute-start | bytes 786440 | tf_op jit(solution)/shard_map/ppermute | solution.py:15
  53.3 11.0 %collective-permute-start.35 = (bf16[4,128,512]{2,1,0:T(8,128)(2,1)S(1)}, bf16[4,128,512]{2,1,0:T(8,128)(2,1)S(1)}, u32[]{:S(2)}, u32[]{:S(2)}) collective-permute-start(bf16[4,128,512]{2,1,0:T(8,128)(2,1)S(1)} %copy-done.1), channel_id=1, source_target_pairs={{0,1},{1,0},{2,3},{3,2},{4,5},{5,4},{6,7},{7,6},{8,9},{9,8},{10,11... | collective-permute-start | bytes 1572872 | tf_op jit(solution)/shard_map/ppermute | solution.py:15
  53.7 14.1 %collective-permute-start.36 = (bf16[4,128,512]{2,1,0:T(8,128)(2,1)S(1)}, bf16[4,128,512]{2,1,0:T(8,128)(2,1)S(1)}, u32[]{:S(2)}, u32[]{:S(2)}) collective-permute-start(bf16[4,128,512]{2,1,0:T(8,128)(2,1)S(1)} %copy-done.3), channel_id=1, source_target_pairs={{0,1},{1,0},{2,3},{3,2},{4,5},{5,4},{6,7},{7,6},{8,9},{9,8},{10,11... | collective-permute-start | bytes 1572872 | tf_op jit(solution)/shard_map/ppermute | solution.py:15
  53.9 15.7 %collective-permute-start.28 = (bf16[256,512]{1,0:T(8,128)(2,1)S(1)}, bf16[256,512]{1,0:T(8,128)(2,1)S(1)}, u32[]{:S(2)}, u32[]{:S(2)}) collective-permute-start(bf16[256,512]{1,0:T(8,128)(2,1)S(1)} %get-tuple-element.106), channel_id=1, source_target_pairs={{0,2},{1,3},{2,0},{3,1},{4,6},{5,7},{6,4},{7,5},{8,10},{9,11},{10,... | collective-permute-start | bytes 786440 | tf_op jit(solution)/shard_map/ppermute | solution.py:15
  55.4 14.4 %collective-permute-start.29 = (bf16[256,512]{1,0:T(8,128)(2,1)S(1)}, bf16[256,512]{1,0:T(8,128)(2,1)S(1)}, u32[]{:S(2)}, u32[]{:S(2)}) collective-permute-start(bf16[256,512]{1,0:T(8,128)(2,1)S(1)} %get-tuple-element.107), channel_id=1, source_target_pairs={{0,4},{1,5},{2,6},{3,7},{4,0},{5,1},{6,2},{7,3},{8,12},{9,13},{10,... | collective-permute-start | bytes 786440 | tf_op jit(solution)/shard_map/ppermute | solution.py:15
  56.7 14.8 %collective-permute-start.30 = (bf16[256,512]{1,0:T(8,128)(2,1)S(1)}, bf16[256,512]{1,0:T(8,128)(2,1)S(1)}, u32[]{:S(2)}, u32[]{:S(2)}) collective-permute-start(bf16[256,512]{1,0:T(8,128)(2,1)S(1)} %get-tuple-element.108), channel_id=1, source_target_pairs={{0,6},{1,7},{2,4},{3,5},{4,2},{5,3},{6,0},{7,1},{8,14},{9,15},{10,... | collective-permute-start | bytes 786440 | tf_op jit(solution)/shard_map/ppermute | solution.py:15
  64.3 16.3 %collective-permute-start.26 = (bf16[512,256]{1,0:T(8,128)(2,1)S(1)}, bf16[512,256]{1,0:T(8,128)(2,1)S(1)}, u32[]{:S(2)}, u32[]{:S(2)}) collective-permute-start(bf16[512,256]{1,0:T(8,128)(2,1)S(1)} %get-tuple-element.102.refs_6_.refs_3_), channel_id=1, source_target_pairs={{0,8},{1,9},{2,10},{3,11},{4,12},{5,13},{6,14},{7,15},{8,0},{9,1},... | collective-permute-start | bytes 786440 | tf_op jit(solution)/shard_map/ppermute | solution.py:15
  68.0 14.4 %collective-permute-start.38 = (bf16[256,512]{1,0:T(8,128)(2,1)S(1)}, bf16[256,512]{1,0:T(8,128)(2,1)S(1)}, u32[]{:S(2)}, u32[]{:S(2)}) collective-permute-start(bf16[256,512]{1,0:T(8,128)(2,1)S(1)} %get-tuple-element.124), channel_id=1, source_target_pairs={{0,2},{1,3},{2,0},{3,1},{4,6},{5,7},{6,4},{7,5},{8,10},{9,11},{10,... | collective-permute-start | bytes 786440 | tf_op jit(solution)/shard_map/ppermute | solution.py:15
  69.6 21.6 %collective-permute-start.39 = (bf16[256,512]{1,0:T(8,128)(2,1)S(1)}, bf16[256,512]{1,0:T(8,128)(2,1)S(1)}, u32[]{:S(2)}, u32[]{:S(2)}) collective-permute-start(bf16[256,512]{1,0:T(8,128)(2,1)S(1)} %get-tuple-element.125), channel_id=1, source_target_pairs={{0,4},{1,5},{2,6},{3,7},{4,0},{5,1},{6,2},{7,3},{8,12},{9,13},{10,... | collective-permute-start | bytes 786440 | tf_op jit(solution)/shard_map/ppermute | solution.py:15
  69.8 25.8 %collective-permute-start.40 = (bf16[256,512]{1,0:T(8,128)(2,1)S(1)}, bf16[256,512]{1,0:T(8,128)(2,1)S(1)}, u32[]{:S(2)}, u32[]{:S(2)}) collective-permute-start(bf16[256,512]{1,0:T(8,128)(2,1)S(1)} %get-tuple-element.126), channel_id=1, source_target_pairs={{0,6},{1,7},{2,4},{3,5},{4,2},{5,3},{6,0},{7,1},{8,14},{9,15},{10,... | collective-permute-start | bytes 786440 | tf_op jit(solution)/shard_map/ppermute | solution.py:15
  72.8 31.2 %collective-permute-start.34 = (bf16[512,512]{1,0:T(8,128)(2,1)S(1)}, bf16[512,512]{1,0:T(8,128)(2,1)S(1)}, u32[]{:S(2)}, u32[]{:S(2)}) collective-permute-start(bf16[512,512]{1,0:T(8,128)(2,1)S(1)} %get-tuple-element.109.refs_3_), channel_id=1, source_target_pairs={{0,8},{1,9},{2,10},{3,11},{4,12},{5,13},{6,14},{7,15},{8,0},{9,1},... | collective-permute-start | bytes 1572872 | tf_op jit(solution)/shard_map/ppermute | solution.py:15
  80.7 16.3 %collective-permute-start.31 = (bf16[128,256]{1,0:T(8,128)(2,1)S(1)}, bf16[128,256]{1,0:T(8,128)(2,1)S(1)}, u32[]{:S(2)}, u32[]{:S(2)}) collective-permute-start(bf16[128,256]{1,0:T(8,128)(2,1)S(1)} %get-tuple-element.111), channel_id=1, source_target_pairs={{0,2},{1,3},{2,0},{3,1},{4,6},{5,7},{6,4},{7,5},{8,10},{9,11},{10,... | collective-permute-start | bytes 196616 | tf_op jit(solution)/shard_map/ppermute | solution.py:15
  82.3 17.4 %collective-permute-start.32 = (bf16[128,256]{1,0:T(8,128)(2,1)S(1)}, bf16[128,256]{1,0:T(8,128)(2,1)S(1)}, u32[]{:S(2)}, u32[]{:S(2)}) collective-permute-start(bf16[128,256]{1,0:T(8,128)(2,1)S(1)} %get-tuple-element.112), channel_id=1, source_target_pairs={{0,4},{1,5},{2,6},{3,7},{4,0},{5,1},{6,2},{7,3},{8,12},{9,13},{10,... | collective-permute-start | bytes 196616 | tf_op jit(solution)/shard_map/ppermute | solution.py:15
  91.2 9.8 %collective-permute-start.33 = (bf16[128,256]{1,0:T(8,128)(2,1)S(1)}, bf16[128,256]{1,0:T(8,128)(2,1)S(1)}, u32[]{:S(2)}, u32[]{:S(2)}) collective-permute-start(bf16[128,256]{1,0:T(8,128)(2,1)S(1)} %get-tuple-element.113), channel_id=1, source_target_pairs={{0,6},{1,7},{2,4},{3,5},{4,2},{5,3},{6,0},{7,1},{8,14},{9,15},{10,... | collective-permute-start | bytes 196616 | tf_op jit(solution)/shard_map/ppermute | solution.py:15
  96.9 30.2 %collective-permute-start.44 = (bf16[512,512]{1,0:T(8,128)(2,1)S(1)}, bf16[512,512]{1,0:T(8,128)(2,1)S(1)}, u32[]{:S(2)}, u32[]{:S(2)}) collective-permute-start(bf16[512,512]{1,0:T(8,128)(2,1)S(1)} %get-tuple-element.127.refs_3_), channel_id=1, source_target_pairs={{0,8},{1,9},{2,10},{3,11},{4,12},{5,13},{6,14},{7,15},{8,0},{9,1},... | collective-permute-start | bytes 1572872 | tf_op jit(solution)/shard_map/ppermute | solution.py:15
  97.0 18.9 %collective-permute-start.45 = (bf16[256,512]{1,0:T(8,128)(2,1)S(1)}, bf16[256,512]{1,0:T(8,128)(2,1)S(1)}, u32[]{:S(2)}, u32[]{:S(2)}) collective-permute-start(bf16[256,512]{1,0:T(8,128)(2,1)S(1)} %get-tuple-element.137), channel_id=1, source_target_pairs={{0,2},{1,3},{2,0},{3,1},{4,6},{5,7},{6,4},{7,5},{8,10},{9,11},{10,... | collective-permute-start | bytes 786440 | tf_op jit(solution)/shard_map/ppermute | solution.py:15
  99.7 17.2 %collective-permute-start.46 = (bf16[256,512]{1,0:T(8,128)(2,1)S(1)}, bf16[256,512]{1,0:T(8,128)(2,1)S(1)}, u32[]{:S(2)}, u32[]{:S(2)}) collective-permute-start(bf16[256,512]{1,0:T(8,128)(2,1)S(1)} %get-tuple-element.138), channel_id=1, source_target_pairs={{0,4},{1,5},{2,6},{3,7},{4,0},{5,1},{6,2},{7,3},{8,12},{9,13},{10,... | collective-permute-start | bytes 786440 | tf_op jit(solution)/shard_map/ppermute | solution.py:15
  101.0 21.5 %collective-permute-start.47 = (bf16[256,512]{1,0:T(8,128)(2,1)S(1)}, bf16[256,512]{1,0:T(8,128)(2,1)S(1)}, u32[]{:S(2)}, u32[]{:S(2)}) collective-permute-start(bf16[256,512]{1,0:T(8,128)(2,1)S(1)} %get-tuple-element.139), channel_id=1, source_target_pairs={{0,6},{1,7},{2,4},{3,5},{4,2},{5,3},{6,0},{7,1},{8,14},{9,15},{10,... | collective-permute-start | bytes 786440 | tf_op jit(solution)/shard_map/ppermute | solution.py:15
  104.0 30.3 %collective-permute-start.52 = (bf16[256,256]{1,0:T(8,128)(2,1)S(1)}, bf16[256,256]{1,0:T(8,128)(2,1)S(1)}, u32[]{:S(2)}, u32[]{:S(2)}) collective-permute-start(bf16[256,256]{1,0:T(8,128)(2,1)S(1)} %get-tuple-element.150), channel_id=1, source_target_pairs={{0,2},{1,3},{2,0},{3,1},{4,6},{5,7},{6,4},{7,5},{8,10},{9,11},{10,... | collective-permute-start | bytes 393224 | tf_op jit(solution)/shard_map/ppermute | solution.py:15
  116.0 11.3 %collective-permute-start.41 = (bf16[128,512]{1,0:T(8,128)(2,1)S(1)}, bf16[128,512]{1,0:T(8,128)(2,1)S(1)}, u32[]{:S(2)}, u32[]{:S(2)}) collective-permute-start(bf16[128,512]{1,0:T(8,128)(2,1)S(1)} %get-tuple-element.129), channel_id=1, source_target_pairs={{0,2},{1,3},{2,0},{3,1},{4,6},{5,7},{6,4},{7,5},{8,10},{9,11},{10,... | collective-permute-start | bytes 393224 | tf_op jit(solution)/shard_map/ppermute | solution.py:15
  116.8 13.2 %collective-permute-start.42 = (bf16[128,512]{1,0:T(8,128)(2,1)S(1)}, bf16[128,512]{1,0:T(8,128)(2,1)S(1)}, u32[]{:S(2)}, u32[]{:S(2)}) collective-permute-start(bf16[128,512]{1,0:T(8,128)(2,1)S(1)} %get-tuple-element.130), channel_id=1, source_target_pairs={{0,4},{1,5},{2,6},{3,7},{4,0},{5,1},{6,2},{7,3},{8,12},{9,13},{10,... | collective-permute-start | bytes 393224 | tf_op jit(solution)/shard_map/ppermute | solution.py:15
  122.5 11.5 %collective-permute-start.43 = (bf16[128,512]{1,0:T(8,128)(2,1)S(1)}, bf16[128,512]{1,0:T(8,128)(2,1)S(1)}, u32[]{:S(2)}, u32[]{:S(2)}) collective-permute-start(bf16[128,512]{1,0:T(8,128)(2,1)S(1)} %get-tuple-element.131), channel_id=1, source_target_pairs={{0,6},{1,7},{2,4},{3,5},{4,2},{5,3},{6,0},{7,1},{8,14},{9,15},{10,... | collective-permute-start | bytes 393224 | tf_op jit(solution)/shard_map/ppermute | solution.py:15
  127.2 12.7 %collective-permute-start.53 = (bf16[256,256]{1,0:T(8,128)(2,1)S(1)}, bf16[256,256]{1,0:T(8,128)(2,1)S(1)}, u32[]{:S(2)}, u32[]{:S(2)}) collective-permute-start(bf16[256,256]{1,0:T(8,128)(2,1)S(1)} %get-tuple-element.151), channel_id=1, source_target_pairs={{0,4},{1,5},{2,6},{3,7},{4,0},{5,1},{6,2},{7,3},{8,12},{9,13},{10,... | collective-permute-start | bytes 393224 | tf_op jit(solution)/shard_map/ppermute | solution.py:15
  127.2 15.2 %collective-permute-start.54 = (bf16[256,256]{1,0:T(8,128)(2,1)S(1)}, bf16[256,256]{1,0:T(8,128)(2,1)S(1)}, u32[]{:S(2)}, u32[]{:S(2)}) collective-permute-start(bf16[256,256]{1,0:T(8,128)(2,1)S(1)} %get-tuple-element.152), channel_id=1, source_target_pairs={{0,6},{1,7},{2,4},{3,5},{4,2},{5,3},{6,0},{7,1},{8,14},{9,15},{10,... | collective-permute-start | bytes 393224 | tf_op jit(solution)/shard_map/ppermute | solution.py:15
  130.0 31.7 %collective-permute-start.51 = (bf16[512,512]{1,0:T(8,128)(2,1)S(1)}, bf16[512,512]{1,0:T(8,128)(2,1)S(1)}, u32[]{:S(2)}, u32[]{:S(2)}) collective-permute-start(bf16[512,512]{1,0:T(8,128)(2,1)S(1)} %get-tuple-element.140.refs_3_), channel_id=1, source_target_pairs={{0,8},{1,9},{2,10},{3,11},{4,12},{5,13},{6,14},{7,15},{8,0},{9,1},... | collective-permute-start | bytes 1572872 | tf_op jit(solution)/shard_map/ppermute | solution.py:15
  134.1 9.6 %collective-permute-start.48 = (bf16[128,512]{1,0:T(8,128)(2,1)S(1)}, bf16[128,512]{1,0:T(8,128)(2,1)S(1)}, u32[]{:S(2)}, u32[]{:S(2)}) collective-permute-start(bf16[128,512]{1,0:T(8,128)(2,1)S(1)} %get-tuple-element.142), channel_id=1, source_target_pairs={{0,2},{1,3},{2,0},{3,1},{4,6},{5,7},{6,4},{7,5},{8,10},{9,11},{10,... | collective-permute-start | bytes 393224 | tf_op jit(solution)/shard_map/ppermute | solution.py:15
  134.3 15.2 %collective-permute-start.49 = (bf16[128,512]{1,0:T(8,128)(2,1)S(1)}, bf16[128,512]{1,0:T(8,128)(2,1)S(1)}, u32[]{:S(2)}, u32[]{:S(2)}) collective-permute-start(bf16[128,512]{1,0:T(8,128)(2,1)S(1)} %get-tuple-element.143), channel_id=1, source_target_pairs={{0,4},{1,5},{2,6},{3,7},{4,0},{5,1},{6,2},{7,3},{8,12},{9,13},{10,... | collective-permute-start | bytes 393224 | tf_op jit(solution)/shard_map/ppermute | solution.py:15
  139.9 12.4 %collective-permute-start.50 = (bf16[128,512]{1,0:T(8,128)(2,1)S(1)}, bf16[128,512]{1,0:T(8,128)(2,1)S(1)}, u32[]{:S(2)}, u32[]{:S(2)}) collective-permute-start(bf16[128,512]{1,0:T(8,128)(2,1)S(1)} %get-tuple-element.144), channel_id=1, source_target_pairs={{0,6},{1,7},{2,4},{3,5},{4,2},{5,3},{6,0},{7,1},{8,14},{9,15},{10,... | collective-permute-start | bytes 393224 | tf_op jit(solution)/shard_map/ppermute | solution.py:15
  143.1 22.3 %collective-permute-start.58 = (bf16[512,256]{1,0:T(8,128)(2,1)S(1)}, bf16[512,256]{1,0:T(8,128)(2,1)S(1)}, u32[]{:S(2)}, u32[]{:S(2)}) collective-permute-start(bf16[512,256]{1,0:T(8,128)(2,1)S(1)} %get-tuple-element.153.refs_3_), channel_id=1, source_target_pairs={{0,8},{1,9},{2,10},{3,11},{4,12},{5,13},{6,14},{7,15},{8,0},{9,1},... | collective-permute-start | bytes 786440 | tf_op jit(solution)/shard_map/ppermute | solution.py:15
  161.8 6.4 %collective-permute-start.55 = (bf16[128,512]{1,0:T(8,128)(2,1)S(1)}, bf16[128,512]{1,0:T(8,128)(2,1)S(1)}, u32[]{:S(2)}, u32[]{:S(2)}) collective-permute-start(bf16[128,512]{1,0:T(8,128)(2,1)S(1)} %get-tuple-element.155), channel_id=1, source_target_pairs={{0,2},{1,3},{2,0},{3,1},{4,6},{5,7},{6,4},{7,5},{8,10},{9,11},{10,... | collective-permute-start | bytes 393224 | tf_op jit(solution)/shard_map/ppermute | solution.py:15
  163.1 5.2 %collective-permute-start.56 = (bf16[128,512]{1,0:T(8,128)(2,1)S(1)}, bf16[128,512]{1,0:T(8,128)(2,1)S(1)}, u32[]{:S(2)}, u32[]{:S(2)}) collective-permute-start(bf16[128,512]{1,0:T(8,128)(2,1)S(1)} %get-tuple-element.156), channel_id=1, source_target_pairs={{0,4},{1,5},{2,6},{3,7},{4,0},{5,1},{6,2},{7,3},{8,12},{9,13},{10,... | collective-permute-start | bytes 393224 | tf_op jit(solution)/shard_map/ppermute | solution.py:15
  163.1 7.4 %collective-permute-start.57 = (bf16[128,512]{1,0:T(8,128)(2,1)S(1)}, bf16[128,512]{1,0:T(8,128)(2,1)S(1)}, u32[]{:S(2)}, u32[]{:S(2)}) collective-permute-start(bf16[128,512]{1,0:T(8,128)(2,1)S(1)} %get-tuple-element.157), channel_id=1, source_target_pairs={{0,6},{1,7},{2,4},{3,5},{4,2},{5,3},{6,0},{7,1},{8,14},{9,15},{10,... | collective-permute-start | bytes 393224 | tf_op jit(solution)/shard_map/ppermute | solution.py:15
  165.5 5.8 %collective-permute-start.59 = (bf16[128,256]{1,0:T(8,128)(2,1)S(1)}, bf16[128,256]{1,0:T(8,128)(2,1)S(1)}, u32[]{:S(2)}, u32[]{:S(2)}) collective-permute-start(bf16[128,256]{1,0:T(8,128)(2,1)S(1)} %get-tuple-element.160), channel_id=1, source_target_pairs={{0,2},{1,3},{2,0},{3,1},{4,6},{5,7},{6,4},{7,5},{8,10},{9,11},{10,... | collective-permute-start | bytes 196616 | tf_op jit(solution)/shard_map/ppermute | solution.py:15
  166.8 11.4 %collective-permute-start.63 = (bf16[4,64,512]{2,1,0:T(8,128)(2,1)S(1)}, bf16[4,64,512]{2,1,0:T(8,128)(2,1)S(1)}, u32[]{:S(2)}, u32[]{:S(2)}) collective-permute-start(bf16[4,64,512]{2,1,0:T(8,128)(2,1)S(1)} %shard_map.77), channel_id=1, source_target_pairs={{0,1},{1,0},{2,3},{3,2},{4,5},{5,4},{6,7},{7,6},{8,9},{9,8},{10,11... | collective-permute-start | bytes 786440 | tf_op jit(solution)/shard_map/ppermute | solution.py:15
  168.3 10.0 %collective-permute-start.64 = (bf16[4,64,512]{2,1,0:T(8,128)(2,1)S(1)}, bf16[4,64,512]{2,1,0:T(8,128)(2,1)S(1)}, u32[]{:S(2)}, u32[]{:S(2)}) collective-permute-start(bf16[4,64,512]{2,1,0:T(8,128)(2,1)S(1)} %shard_map.78), channel_id=1, source_target_pairs={{0,1},{1,0},{2,3},{3,2},{4,5},{5,4},{6,7},{7,6},{8,9},{9,8},{10,11... | collective-permute-start | bytes 786440 | tf_op jit(solution)/shard_map/ppermute | solution.py:15
  170.6 7.7 %collective-permute-start.65 = (bf16[4,64,512]{2,1,0:T(8,128)(2,1)S(1)}, bf16[4,64,512]{2,1,0:T(8,128)(2,1)S(1)}, u32[]{:S(2)}, u32[]{:S(2)}) collective-permute-start(bf16[4,64,512]{2,1,0:T(8,128)(2,1)S(1)} %shard_map.79), channel_id=1, source_target_pairs={{0,1},{1,0},{2,3},{3,2},{4,5},{5,4},{6,7},{7,6},{8,9},{9,8},{10,11... | collective-permute-start | bytes 786440 | tf_op jit(solution)/shard_map/ppermute | solution.py:15
  170.6 5.0 %collective-permute-start.60 = (bf16[128,256]{1,0:T(8,128)(2,1)S(1)}, bf16[128,256]{1,0:T(8,128)(2,1)S(1)}, u32[]{:S(2)}, u32[]{:S(2)}) collective-permute-start(bf16[128,256]{1,0:T(8,128)(2,1)S(1)} %get-tuple-element.161), channel_id=1, source_target_pairs={{0,4},{1,5},{2,6},{3,7},{4,0},{5,1},{6,2},{7,3},{8,12},{9,13},{10,... | collective-permute-start | bytes 196616 | tf_op jit(solution)/shard_map/ppermute | solution.py:15
  171.3 5.5 %collective-permute-start.61 = (bf16[128,256]{1,0:T(8,128)(2,1)S(1)}, bf16[128,256]{1,0:T(8,128)(2,1)S(1)}, u32[]{:S(2)}, u32[]{:S(2)}) collective-permute-start(bf16[128,256]{1,0:T(8,128)(2,1)S(1)} %get-tuple-element.162), channel_id=1, source_target_pairs={{0,6},{1,7},{2,4},{3,5},{4,2},{5,3},{6,0},{7,1},{8,14},{9,15},{10,... | collective-permute-start | bytes 196616 | tf_op jit(solution)/shard_map/ppermute | solution.py:15
  (21 other events, 71.4 us)

commit v3 on v2

--- a/solution.py
+++ b/solution.py
@@ -422,7 +422,7 @@
             group,
             work,
         )
-        flat = call([step], tokens, 36)[0]
+        flat = call([step], tokens, 42)[0]
         for i, k in enumerate(ks):
             kept[k], other[k] = flat[2 * i : 2 * i + 2]
             if trade:
@@ -485,7 +485,7 @@
     final = {}
     for k in range(last):
         final[k] = swap(call([for_other_core(held[k], core)], [token])[0][0], 1)
-    sums[last] = call([add_sides(near[last], across[last], member, group, 0)], [clock])[0]
+    sums[last] = call([add_sides(near[last], across[last], member, group, MIDDLE)], [clock])[0]
     held[last] = [sums[last][0]] + send(sums[last])
     final[last] = swap(call([for_other_core(held[last], core)])[0][0], 1)
     ks = range(last + 1)

time: 182 us -> 182 us (level)
  no operation moved by 1% of the time
where the time goes in v3:
time: 182 us
  starting transfers between devices  75.7 us (42%)
  waiting for transfers between devices  67.2 us (37%)
  Pallas kernels  30.4 us (17%)
  local copies, waits for them, and re-layouts  4.84 us (3%)
  matrix products  2.53 us (1%)
    ppermute x67, starting transfers between devices, swap(): return lax.ppermute(x, 'blk', [(i, i ^ bits) for i in range(n)])  75.7 us
    ppermute x67, waiting for transfers between devices, swap(): return lax.ppermute(x, 'blk', [(i, i ^ bits) for i in range(n)])  67.2 us
    pallas_call x27, Pallas kernels, call(): pl.pallas_call(body, out_shape=[jax.ShapeDtypeStruct(shape, kind) for sha...  30.4 us
  transfers between devices with their start and end apart: 67, of which 27 were waited for; matrix products, arithmetic and copies ran while one was open for 2% of the time, Pallas kernels for 15%

profile of v3, /device:TPU:0, one launch (start us, length us, event | category | flops | bytes accessed | tf_op | source)
XLA Modules:
  0.0 181.8 jit_solution(2317885432097021461)
XLA Ops:
  0.0 0.8 dynamic_slice.11
  0.8 1.4 fusion.3.refs_4_
  2.2 4.1 %collective-permute-start.8 = (bf16[128,512]{1,0:T(8,128)(2,1)S(1)}, bf16[128,512]{1,0:T(8,128)(2,1)S(1)}, u32[]{:S(2)}, u32[]{:S(2)}) collective-permute-start(bf16[128,512]{1,0:T(8,128)(2,1)S(1)} %fusion.3.refs_4_), channel_id=1, source_target_pairs={{0,8},{1,9},{2,10},{3,11},{4,12},{5,13},{6,14},{7,15},{8,0},{9,1},... | collective-permute-start | bytes 393224 | tf_op jit(solution)/shard_map/ppermute | solution.py:15
  6.3 1.6 collective-permute-start.4
  7.9 1.5 collective-permute-start.2
  9.4 0.8 dynamic_slice.10
  10.2 0.8 dynamic_slice.9
  10.9 1.8 collective-permute-done.8.refs_12_
  13.3 0.9 fusion.5
  14.2 1.6 collective-permute-start.10
  16.6 1.1 collective-permute-done.12.refs_16_
  17.7 1.6 collective-permute-start.14
  20.5 2.3 %collective-permute-done.6.refs_10_ = bf16[128,512]{1,0:T(8,128)(2,1)S(1)} collective-permute-done((bf16[128,512]{1,0:T(8,128)(2,1)S(1)}, bf16[128,512]{1,0:T(8,128)(2,1)S(1)}, u32[]{:S(2)}, u32[]{:S(2)}) %collective-permute-start.6) | collective-permute-done | bytes 131104 | tf_op jit(solution)/shard_map/ppermute | solution.py:15
  23.3 1.8 collective-permute-done.14.refs_18_
  25.1 1.3 collective-permute-start.21
  26.4 1.6 collective-permute-start.20
  28.7 3.5 %shard_map.55 = (bf16[4,128,256]{2,1,0:T(8,128)(2,1)S(1)}, bf16[4,128,256]{2,1,0:T(8,128)(2,1)S(1)}) custom-call(s32[1]{0:T(128)} %bitcast.3.refs_0_, s32[1]{0:T(128)} %bitcast.refs_1_.refs_0_, s32[4]{0:T(128)S(1)} %iota_xor_fusion.refs_2_.refs_0_, bf16[32,128,2048]{2,1,0:T(8,128)(2,1)} %refs_3_.3, bf16[128,512]{1,0:T(8,128)(2,1)S(1)} %fusion.3.refs_4_, ...), custom_call_target="tpu_custom_call" | custom-call | tf_op jit(solution)/shard_map/pallas_call | solution.py:52
  32.3 1.4 collective-permute-done.16.refs_1_
  33.8 1.6 collective-permute-start.17
  35.4 1.3 collective-permute-start.18
  37.4 11.3 %shard_map.58 = (bf16[4,128,512]{2,1,0:T(8,128)(2,1)S(1)}, bf16[4,128,512]{2,1,0:T(8,128)(2,1)S(1)}, bf16[4,128,512]{2,1,0:T(8,128)(2,1)S(1)}, bf16[4,128,512]{2...) custom-call(s32[1]{0:T(128)} %bitcast.3.refs_0_, ...), custom_call_target="tpu_custom_call" | custom-call | tf_op jit(solution)/shard_map/pallas_call | solution.py:52
  48.9 0.9 copy-done
  49.8 0.8 copy-done.2
  53.9 1.5 collective-permute-start.28
  55.4 1.3 collective-permute-start.29
  57.4 6.2 %shard_map.60.refs_1_.refs_6_ = bf16[1024,1024]{1,0:T(8,128)(2,1)S(1)} custom-call(bf16[1024,1024]{1,0:T(8,128)(2,1)S(1)} %fusion.refs_0_, bf16[128,1024]{1,0:T(8,128)(2,1)} %refs_1_.1, bf16[128,1024]{1,0:T(8,128)(2,1)} %collective-permute-done.refs_2_, bf16[128,1024]{1,0:T(8,128)(2,1)} %get-tuple-element.95.refs_3_, ...), custom_call_target="tpu_custom_call" | custom-call | flops 99999997952 | tf_op jit(solution)/shard_map/pallas_call | solution.py:52
  64.3 3.4 %collective-permute-start.26 = (bf16[512,256]{1,0:T(8,128)(2,1)S(1)}, bf16[512,256]{1,0:T(8,128)(2,1)S(1)}, u32[]{:S(2)}, u32[]{:S(2)}) collective-permute-start(bf16[512,256]{1,0:T(8,128)(2,1)S(1)} %get-tuple-element.102.refs_6_.refs_3_), channel_id=1, source_target_pairs={{0,8},{1,9},{2,10},{3,11},{4,12},{5,13},{6,14},{7,15},{8,0},{9,1},... | collective-permute-start | bytes 786440 | tf_op jit(solution)/shard_map/ppermute | solution.py:15
  68.0 1.6 collective-permute-start.38
  69.8 1.7 collective-permute-start.40
  71.5 1.3 shard_map.63
  72.8 2.1 %collective-permute-start.34 = (bf16[512,512]{1,0:T(8,128)(2,1)S(1)}, bf16[512,512]{1,0:T(8,128)(2,1)S(1)}, u32[]{:S(2)}, u32[]{:S(2)}) collective-permute-start(bf16[512,512]{1,0:T(8,128)(2,1)S(1)} %get-tuple-element.109.refs_3_), channel_id=1, source_target_pairs={{0,8},{1,9},{2,10},{3,11},{4,12},{5,13},{6,14},{7,15},{8,0},{9,1},... | collective-permute-start | bytes 1572872 | tf_op jit(solution)/shard_map/ppermute | solution.py:15
  74.8 5.8 %collective-permute-done.26.refs_2_ = bf16[512,256]{1,0:T(8,128)(2,1)S(1)} collective-permute-done((bf16[512,256]{1,0:T(8,128)(2,1)S(1)}, bf16[512,256]{1,0:T(8,128)(2,1)S(1)}, u32[]{:S(2)}, u32[]{:S(2)}) %collective-permute-start.26) | collective-permute-done | bytes 262176 | tf_op jit(solution)/shard_map/ppermute | solution.py:15
  80.7 1.6 collective-permute-start.31
  82.3 8.9 %collective-permute-done.39.refs_4_ = bf16[256,512]{1,0:T(8,128)(2,1)S(1)} collective-permute-done((bf16[256,512]{1,0:T(8,128)(2,1)S(1)}, bf16[256,512]{1,0:T(8,128)(2,1)S(1)}, u32[]{:S(2)}, u32[]{:S(2)}) %collective-permute-start.39) | collective-permute-done | bytes 262176 | tf_op jit(solution)/shard_map/ppermute | solution.py:15
  91.2 4.5 %collective-permute-done.40.refs_5_ = bf16[256,512]{1,0:T(8,128)(2,1)S(1)} collective-permute-done((bf16[256,512]{1,0:T(8,128)(2,1)S(1)}, bf16[256,512]{1,0:T(8,128)(2,1)S(1)}, u32[]{:S(2)}, u32[]{:S(2)}) %collective-permute-start.40) | collective-permute-done | bytes 262176 | tf_op jit(solution)/shard_map/ppermute | solution.py:15
  95.7 1.2 shard_map.67
  97.0 2.7 %collective-permute-start.45 = (bf16[256,512]{1,0:T(8,128)(2,1)S(1)}, bf16[256,512]{1,0:T(8,128)(2,1)S(1)}, u32[]{:S(2)}, u32[]{:S(2)}) collective-permute-start(bf16[256,512]{1,0:T(8,128)(2,1)S(1)} %get-tuple-element.137), channel_id=1, source_target_pairs={{0,2},{1,3},{2,0},{3,1},{4,6},{5,7},{6,4},{7,5},{8,10},{9,11},{10,... | collective-permute-start | bytes 786440 | tf_op jit(solution)/shard_map/ppermute | solution.py:15
  99.7 1.3 collective-permute-start.46
  101.0 2.3 %collective-permute-start.47 = (bf16[256,512]{1,0:T(8,128)(2,1)S(1)}, bf16[256,512]{1,0:T(8,128)(2,1)S(1)}, u32[]{:S(2)}, u32[]{:S(2)}) collective-permute-start(bf16[256,512]{1,0:T(8,128)(2,1)S(1)} %get-tuple-element.139), channel_id=1, source_target_pairs={{0,6},{1,7},{2,4},{3,5},{4,2},{5,3},{6,0},{7,1},{8,14},{9,15},{10,... | collective-permute-start | bytes 786440 | tf_op jit(solution)/shard_map/ppermute | solution.py:15
  104.0 11.8 %collective-permute-start.52 = (bf16[256,256]{1,0:T(8,128)(2,1)S(1)}, bf16[256,256]{1,0:T(8,128)(2,1)S(1)}, u32[]{:S(2)}, u32[]{:S(2)}) collective-permute-start(bf16[256,256]{1,0:T(8,128)(2,1)S(1)} %get-tuple-element.150), channel_id=1, source_target_pairs={{0,2},{1,3},{2,0},{3,1},{4,6},{5,7},{6,4},{7,5},{8,10},{9,11},{10,... | collective-permute-start | bytes 393224 | tf_op jit(solution)/shard_map/ppermute | solution.py:15
  116.1 0.8 collective-permute-done.46.refs_4_
  116.8 2.5 %collective-permute-start.42 = (bf16[128,512]{1,0:T(8,128)(2,1)S(1)}, bf16[128,512]{1,0:T(8,128)(2,1)S(1)}, u32[]{:S(2)}, u32[]{:S(2)}) collective-permute-start(bf16[128,512]{1,0:T(8,128)(2,1)S(1)} %get-tuple-element.130), channel_id=1, source_target_pairs={{0,4},{1,5},{2,6},{3,7},{4,0},{5,1},{6,2},{7,3},{8,12},{9,13},{10,... | collective-permute-start | bytes 393224 | tf_op jit(solution)/shard_map/ppermute | solution.py:15
  119.3 3.2 %collective-permute-done.47.refs_5_ = bf16[256,512]{1,0:T(8,128)(2,1)S(1)} collective-permute-done((bf16[256,512]{1,0:T(8,128)(2,1)S(1)}, bf16[256,512]{1,0:T(8,128)(2,1)S(1)}, u32[]{:S(2)}, u32[]{:S(2)}) %collective-permute-start.47) | collective-permute-done | bytes 262176 | tf_op jit(solution)/shard_map/ppermute | solution.py:15
  122.5 3.4 %collective-permute-start.43 = (bf16[128,512]{1,0:T(8,128)(2,1)S(1)}, bf16[128,512]{1,0:T(8,128)(2,1)S(1)}, u32[]{:S(2)}, u32[]{:S(2)}) collective-permute-start(bf16[128,512]{1,0:T(8,128)(2,1)S(1)} %get-tuple-element.131), channel_id=1, source_target_pairs={{0,6},{1,7},{2,4},{3,5},{4,2},{5,3},{6,0},{7,1},{8,14},{9,15},{10,... | collective-permute-start | bytes 393224 | tf_op jit(solution)/shard_map/ppermute | solution.py:15
  125.9 1.3 shard_map.70
  127.2 2.7 %collective-permute-start.54 = (bf16[256,256]{1,0:T(8,128)(2,1)S(1)}, bf16[256,256]{1,0:T(8,128)(2,1)S(1)}, u32[]{:S(2)}, u32[]{:S(2)}) collective-permute-start(bf16[256,256]{1,0:T(8,128)(2,1)S(1)} %get-tuple-element.152), channel_id=1, source_target_pairs={{0,6},{1,7},{2,4},{3,5},{4,2},{5,3},{6,0},{7,1},{8,14},{9,15},{10,... | collective-permute-start | bytes 393224 | tf_op jit(solution)/shard_map/ppermute | solution.py:15
  130.0 4.0 %collective-permute-start.51 = (bf16[512,512]{1,0:T(8,128)(2,1)S(1)}, bf16[512,512]{1,0:T(8,128)(2,1)S(1)}, u32[]{:S(2)}, u32[]{:S(2)}) collective-permute-start(bf16[512,512]{1,0:T(8,128)(2,1)S(1)} %get-tuple-element.140.refs_3_), channel_id=1, source_target_pairs={{0,8},{1,9},{2,10},{3,11},{4,12},{5,13},{6,14},{7,15},{8,0},{9,1},... | collective-permute-start | bytes 1572872 | tf_op jit(solution)/shard_map/ppermute | solution.py:15
  134.3 0.8 collective-permute-start.49
  135.1 4.8 %collective-permute-done.53.refs_4_ = bf16[256,256]{1,0:T(8,128)(2,1)S(1)} collective-permute-done((bf16[256,256]{1,0:T(8,128)(2,1)S(1)}, bf16[256,256]{1,0:T(8,128)(2,1)S(1)}, u32[]{:S(2)}, u32[]{:S(2)}) %collective-permute-start.53) | collective-permute-done | bytes 131104 | tf_op jit(solution)/shard_map/ppermute | solution.py:15
  139.9 2.5 %collective-permute-done.54.refs_5_ = bf16[256,256]{1,0:T(8,128)(2,1)S(1)} collective-permute-done((bf16[256,256]{1,0:T(8,128)(2,1)S(1)}, bf16[256,256]{1,0:T(8,128)(2,1)S(1)}, u32[]{:S(2)}, u32[]{:S(2)}) %collective-permute-start.54) | collective-permute-done | bytes 131104 | tf_op jit(solution)/shard_map/ppermute | solution.py:15
  142.4 0.7 shard_map.73
  143.8 5.7 %collective-permute-done.49.refs_5_.refs_3_.refs_13_ = bf16[128,512]{1,0:T(8,128)(2,1)S(1)} collective-permute-done((bf16[128,512]{1,0:T(8,128)(2,1)S(1)}, bf16[128,512]{1,0:T(8,128)(2,1)S(1)}, u32[]{:S(2)}, u32[]{:S(2)}) %collective-permute-start.49) | collective-permute-done | bytes 131104 | tf_op jit(solution)/shard_map/ppermute | solution.py:15
  149.5 2.8 %collective-permute-done.50.refs_6_.refs_4_.refs_14_ = bf16[128,512]{1,0:T(8,128)(2,1)S(1)} collective-permute-done((bf16[128,512]{1,0:T(8,128)(2,1)S(1)}, bf16[128,512]{1,0:T(8,128)(2,1)S(1)}, u32[]{:S(2)}, u32[]{:S(2)}) %collective-permute-start.50) | collective-permute-done | bytes 131104 | tf_op jit(solution)/shard_map/ppermute | solution.py:15
  152.3 9.4 %collective-permute-done.51.refs_2_ = bf16[512,512]{1,0:T(8,128)(2,1)S(1)} collective-permute-done((bf16[512,512]{1,0:T(8,128)(2,1)S(1)}, bf16[512,512]{1,0:T(8,128)(2,1)S(1)}, u32[]{:S(2)}, u32[]{:S(2)}) %collective-permute-start.51) | collective-permute-done | bytes 524320 | tf_op jit(solution)/shard_map/ppermute | solution.py:15
  161.8 1.3 collective-permute-start.55
  163.1 2.3 %collective-permute-start.57 = (bf16[128,512]{1,0:T(8,128)(2,1)S(1)}, bf16[128,512]{1,0:T(8,128)(2,1)S(1)}, u32[]{:S(2)}, u32[]{:S(2)}) collective-permute-start(bf16[128,512]{1,0:T(8,128)(2,1)S(1)} %get-tuple-element.157), channel_id=1, source_target_pairs={{0,6},{1,7},{2,4},{3,5},{4,2},{5,3},{6,0},{7,1},{8,14},{9,15},{10,... | collective-permute-start | bytes 393224 | tf_op jit(solution)/shard_map/ppermute | solution.py:15
  165.5 1.3 collective-permute-start.59
  166.9 1.4 collective-permute-done.55.refs_2_.refs_16_
  168.4 2.2 %collective-permute-done.57.refs_4_.refs_18_ = bf16[128,512]{1,0:T(8,128)(2,1)S(1)} collective-permute-done((bf16[128,512]{1,0:T(8,128)(2,1)S(1)}, bf16[128,512]{1,0:T(8,128)(2,1)S(1)}, u32[]{:S(2)}, u32[]{:S(2)}) %collective-permute-start.57) | collective-permute-done | bytes 131104 | tf_op jit(solution)/shard_map/ppermute | solution.py:15
  171.3 1.7 collective-permute-start.61
  173.0 2.6 %collective-permute-done.60.refs_3_.refs_21_ = bf16[128,256]{1,0:T(8,128)(2,1)S(1)} collective-permute-done((bf16[128,256]{1,0:T(8,128)(2,1)S(1)}, bf16[128,256]{1,0:T(8,128)(2,1)S(1)}, u32[]{:S(2)}, u32[]{:S(2)}) %collective-permute-start.60) | collective-permute-done | bytes 65568 | tf_op jit(solution)/shard_map/ppermute | solution.py:15
  175.6 1.2 collective-permute-done.61.refs_4_.refs_22_
  176.9 1.3 collective-permute-done.66.refs_27_
  178.2 3.4 %shard_map.81 = bf16[32,64,512]{2,1,0:T(8,128)(2,1)} custom-call(s32[4]{0:T(128)S(1)} %copy-done.16, s32[1]{0:T(128)} %bitcast.refs_1_.refs_0_, f32[64,512]{1,0:T(8,128)S(1)} %convolution_multiply_fusion.refs_20_.refs_2_, bf16[128,256]{1,0:T(8,128)(2,1)S(1)} %get-tuple-element.110.refs_6_.refs_1_.refs_3_, ...), custom_call_target="tpu_custom_call" | custom-call | tf_op jit(solution)/shard_map/pallas_call | solution.py:52
  (147 shorter events, 13.2 us)
Async XLA Ops:
  2.2 10.5 %collective-permute-start.8 = (bf16[128,512]{1,0:T(8,128)(2,1)S(1)}, bf16[128,512]{1,0:T(8,128)(2,1)S(1)}, u32[]{:S(2)}, u32[]{:S(2)}) collective-permute-start(bf16[128,512]{1,0:T(8,128)(2,1)S(1)} %fusion.3.refs_4_), channel_id=1, source_target_pairs={{0,8},{1,9},{2,10},{3,11},{4,12},{5,13},{6,14},{7,15},{8,0},{9,1},... | collective-permute-start | bytes 393224 | tf_op jit(solution)/shard_map/ppermute | solution.py:15
  6.3 9.5 %collective-permute-start.4 = (bf16[128,512]{1,0:T(8,128)(2,1)S(1)}, bf16[128,512]{1,0:T(8,128)(2,1)S(1)}, u32[]{:S(2)}, u32[]{:S(2)}) collective-permute-start(bf16[128,512]{1,0:T(8,128)(2,1)S(1)} %fusion.3.refs_4_), channel_id=1, source_target_pairs={{0,4},{1,5},{2,6},{3,7},{4,0},{5,1},{6,2},{7,3},{8,12},{9,13},{10,... | collective-permute-start | bytes 393224 | tf_op jit(solution)/shard_map/ppermute | solution.py:15
  7.9 7.9 %collective-permute-start.2 = (bf16[128,512]{1,0:T(8,128)(2,1)S(1)}, bf16[128,512]{1,0:T(8,128)(2,1)S(1)}, u32[]{:S(2)}, u32[]{:S(2)}) collective-permute-start(bf16[128,512]{1,0:T(8,128)(2,1)S(1)} %fusion.3.refs_4_), channel_id=1, source_target_pairs={{0,2},{1,3},{2,0},{3,1},{4,6},{5,7},{6,4},{7,5},{8,10},{9,11},{10,... | collective-permute-start | bytes 393224 | tf_op jit(solution)/shard_map/ppermute | solution.py:15
  9.4 7.0 %collective-permute-start.1 = (bf16[128,512]{1,0:T(8,128)(2,1)S(1)}, bf16[128,512]{1,0:T(8,128)(2,1)S(1)}, u32[]{:S(2)}, u32[]{:S(2)}) collective-permute-start(bf16[128,512]{1,0:T(8,128)(2,1)S(1)} %fusion.3.refs_4_), channel_id=1, source_target_pairs={{0,1},{1,0},{2,3},{3,2},{4,5},{5,4},{6,7},{7,6},{8,9},{9,8},{10,11... | collective-permute-start | bytes 393224 | tf_op jit(solution)/shard_map/ppermute | solution.py:15
  12.7 5.0 %collective-permute-start.12 = (bf16[128,512]{1,0:T(8,128)(2,1)S(1)}, bf16[128,512]{1,0:T(8,128)(2,1)S(1)}, u32[]{:S(2)}, u32[]{:S(2)}) collective-permute-start(bf16[128,512]{1,0:T(8,128)(2,1)S(1)} %collective-permute-done.8.refs_12_), channel_id=1, source_target_pairs={{0,4},{1,5},{2,6},{3,7},{4,0},{5,1},{6,2},{7,3},{8,12},{9,13},{10,... | collective-permute-start | bytes 393224 | tf_op jit(solution)/shard_map/ppermute | solution.py:15
  14.2 5.7 %collective-permute-start.10 = (bf16[128,512]{1,0:T(8,128)(2,1)S(1)}, bf16[128,512]{1,0:T(8,128)(2,1)S(1)}, u32[]{:S(2)}, u32[]{:S(2)}) collective-permute-start(bf16[128,512]{1,0:T(8,128)(2,1)S(1)} %collective-permute-done.8.refs_12_), channel_id=1, source_target_pairs={{0,2},{1,3},{2,0},{3,1},{4,6},{5,7},{6,4},{7,5},{8,10},{9,11},{10,... | collective-permute-start | bytes 393224 | tf_op jit(solution)/shard_map/ppermute | solution.py:15
  15.8 4.1 %collective-permute-start.9 = (bf16[128,512]{1,0:T(8,128)(2,1)S(1)}, bf16[128,512]{1,0:T(8,128)(2,1)S(1)}, u32[]{:S(2)}, u32[]{:S(2)}) collective-permute-start(bf16[128,512]{1,0:T(8,128)(2,1)S(1)} %collective-permute-done.8.refs_12_), channel_id=1, source_target_pairs={{0,1},{1,0},{2,3},{3,2},{4,5},{5,4},{6,7},{7,6},{8,9},{9,8},{10,11... | collective-permute-start | bytes 393224 | tf_op jit(solution)/shard_map/ppermute | solution.py:15
  15.8 6.9 %collective-permute-start.6 = (bf16[128,512]{1,0:T(8,128)(2,1)S(1)}, bf16[128,512]{1,0:T(8,128)(2,1)S(1)}, u32[]{:S(2)}, u32[]{:S(2)}) collective-permute-start(bf16[128,512]{1,0:T(8,128)(2,1)S(1)} %collective-permute-done.4.refs_8_), channel_id=1, source_target_pairs={{0,2},{1,3},{2,0},{3,1},{4,6},{5,7},{6,4},{7,5},{8,10},{9,11},{10,... | collective-permute-start | bytes 393224 | tf_op jit(solution)/shard_map/ppermute | solution.py:15
  16.4 6.3 %collective-permute-start.5 = (bf16[128,512]{1,0:T(8,128)(2,1)S(1)}, bf16[128,512]{1,0:T(8,128)(2,1)S(1)}, u32[]{:S(2)}, u32[]{:S(2)}) collective-permute-start(bf16[128,512]{1,0:T(8,128)(2,1)S(1)} %collective-permute-done.4.refs_8_), channel_id=1, source_target_pairs={{0,1},{1,0},{2,3},{3,2},{4,5},{5,4},{6,7},{7,6},{8,9},{9,8},{10,11... | collective-permute-start | bytes 393224 | tf_op jit(solution)/shard_map/ppermute | solution.py:15
  17.7 7.4 %collective-permute-start.14 = (bf16[128,512]{1,0:T(8,128)(2,1)S(1)}, bf16[128,512]{1,0:T(8,128)(2,1)S(1)}, u32[]{:S(2)}, u32[]{:S(2)}) collective-permute-start(bf16[128,512]{1,0:T(8,128)(2,1)S(1)} %collective-permute-done.12.refs_16_), channel_id=1, source_target_pairs={{0,2},{1,3},{2,0},{3,1},{4,6},{5,7},{6,4},{7,5},{8,10},{9,11},{10,... | collective-permute-start | bytes 393224 | tf_op jit(solution)/shard_map/ppermute | solution.py:15
  19.9 5.2 %collective-permute-start.3 = (bf16[128,512]{1,0:T(8,128)(2,1)S(1)}, bf16[128,512]{1,0:T(8,128)(2,1)S(1)}, u32[]{:S(2)}, u32[]{:S(2)}) collective-permute-start(bf16[128,512]{1,0:T(8,128)(2,1)S(1)} %collective-permute-done.2.refs_6_), channel_id=1, source_target_pairs={{0,1},{1,0},{2,3},{3,2},{4,5},{5,4},{6,7},{7,6},{8,9},{9,8},{10,11... | collective-permute-start | bytes 393224 | tf_op jit(solution)/shard_map/ppermute | solution.py:15
  20.0 6.5 %collective-permute-start.13 = (bf16[128,512]{1,0:T(8,128)(2,1)S(1)}, bf16[128,512]{1,0:T(8,128)(2,1)S(1)}, u32[]{:S(2)}, u32[]{:S(2)}) collective-permute-start(bf16[128,512]{1,0:T(8,128)(2,1)S(1)} %collective-permute-done.12.refs_16_), channel_id=1, source_target_pairs={{0,1},{1,0},{2,3},{3,2},{4,5},{5,4},{6,7},{7,6},{8,9},{9,8},{10,11... | collective-permute-start | bytes 393224 | tf_op jit(solution)/shard_map/ppermute | solution.py:15
  22.8 5.2 %collective-permute-start.11 = (bf16[128,512]{1,0:T(8,128)(2,1)S(1)}, bf16[128,512]{1,0:T(8,128)(2,1)S(1)}, u32[]{:S(2)}, u32[]{:S(2)}) collective-permute-start(bf16[128,512]{1,0:T(8,128)(2,1)S(1)} %collective-permute-done.10.refs_14_), channel_id=1, source_target_pairs={{0,1},{1,0},{2,3},{3,2},{4,5},{5,4},{6,7},{7,6},{8,9},{9,8},{10,11... | collective-permute-start | bytes 393224 | tf_op jit(solution)/shard_map/ppermute | solution.py:15
  22.8 5.9 %collective-permute-start.7 = (bf16[128,512]{1,0:T(8,128)(2,1)S(1)}, bf16[128,512]{1,0:T(8,128)(2,1)S(1)}, u32[]{:S(2)}, u32[]{:S(2)}) collective-permute-start(bf16[128,512]{1,0:T(8,128)(2,1)S(1)} %collective-permute-done.6.refs_10_), channel_id=1, source_target_pairs={{0,1},{1,0},{2,3},{3,2},{4,5},{5,4},{6,7},{7,6},{8,9},{9,8},{10,11... | collective-permute-start | bytes 393224 | tf_op jit(solution)/shard_map/ppermute | solution.py:15
  25.1 3.6 %collective-permute-start.15 = (bf16[128,512]{1,0:T(8,128)(2,1)S(1)}, bf16[128,512]{1,0:T(8,128)(2,1)S(1)}, u32[]{:S(2)}, u32[]{:S(2)}) collective-permute-start(bf16[128,512]{1,0:T(8,128)(2,1)S(1)} %collective-permute-done.14.refs_18_), channel_id=1, source_target_pairs={{0,1},{1,0},{2,3},{3,2},{4,5},{5,4},{6,7},{7,6},{8,9},{9,8},{10,11... | collective-permute-start | bytes 393224 | tf_op jit(solution)/shard_map/ppermute | solution.py:15
  25.1 11.6 %collective-permute-start.21 = (bf16[128,1024]{1,0:T(8,128)(2,1)}, bf16[128,1024]{1,0:T(8,128)(2,1)S(1)}, u32[]{:S(2)}, u32[]{:S(2)}) collective-permute-start(bf16[128,1024]{1,0:T(8,128)(2,1)} %refs_1_.1), channel_id=1, source_target_pairs={{0,4},{1,5},{2,6},{3,7},{4,0},{5,1},{6,2},{7,3},{8,12},{9,13},{10,... | collective-permute-start | bytes 786440 | tf_op jit(solution)/shard_map/ppermute | solution.py:15
  26.4 22.4 %collective-permute-start.20 = (bf16[128,1024]{1,0:T(8,128)(2,1)}, bf16[128,1024]{1,0:T(8,128)(2,1)}, u32[]{:S(2)}, u32[]{:S(2)}) collective-permute-start(bf16[128,1024]{1,0:T(8,128)(2,1)} %refs_1_.1), channel_id=1, source_target_pairs={{0,2},{1,3},{2,0},{3,1},{4,6},{5,7},{6,4},{7,5},{8,10},{9,11},{10,... | collective-permute-start | bytes 786440 | tf_op jit(solution)/shard_map/ppermute | solution.py:15
  28.0 20.8 %collective-permute-start.22 = (bf16[128,1024]{1,0:T(8,128)(2,1)}, bf16[128,1024]{1,0:T(8,128)(2,1)}, u32[]{:S(2)}, u32[]{:S(2)}) collective-permute-start(bf16[128,1024]{1,0:T(8,128)(2,1)} %refs_1_.1), channel_id=1, source_target_pairs={{0,6},{1,7},{2,4},{3,5},{4,2},{5,3},{6,0},{7,1},{8,14},{9,15},{10,... | collective-permute-start | bytes 786440 | tf_op jit(solution)/shard_map/ppermute | solution.py:15
  33.8 15.0 %collective-permute-start.17 = (bf16[256,256]{1,0:T(8,128)(2,1)S(1)}, bf16[256,256]{1,0:T(8,128)(2,1)S(1)}, u32[]{:S(2)}, u32[]{:S(2)}) collective-permute-start(bf16[256,256]{1,0:T(8,128)(2,1)S(1)} %get-tuple-element.86), channel_id=1, source_target_pairs={{0,2},{1,3},{2,0},{3,1},{4,6},{5,7},{6,4},{7,5},{8,10},{9,11},{10,... | collective-permute-start | bytes 393224 | tf_op jit(solution)/shard_map/ppermute | solution.py:15
  35.4 13.4 %collective-permute-start.18 = (bf16[256,256]{1,0:T(8,128)(2,1)S(1)}, bf16[256,256]{1,0:T(8,128)(2,1)S(1)}, u32[]{:S(2)}, u32[]{:S(2)}) collective-permute-start(bf16[256,256]{1,0:T(8,128)(2,1)S(1)} %get-tuple-element.87), channel_id=1, source_target_pairs={{0,4},{1,5},{2,6},{3,7},{4,0},{5,1},{6,2},{7,3},{8,12},{9,13},{10,... | collective-permute-start | bytes 393224 | tf_op jit(solution)/shard_map/ppermute | solution.py:15
  36.7 12.1 %collective-permute-start.19 = (bf16[256,256]{1,0:T(8,128)(2,1)S(1)}, bf16[256,256]{1,0:T(8,128)(2,1)S(1)}, u32[]{:S(2)}, u32[]{:S(2)}) collective-permute-start(bf16[256,256]{1,0:T(8,128)(2,1)S(1)} %get-tuple-element.88), channel_id=1, source_target_pairs={{0,6},{1,7},{2,4},{3,5},{4,2},{5,3},{6,0},{7,1},{8,14},{9,15},{10,... | collective-permute-start | bytes 393224 | tf_op jit(solution)/shard_map/ppermute | solution.py:15
  50.6 2.0 %collective-permute-start.27 = (bf16[4,128,512]{2,1,0:T(8,128)(2,1)S(1)}, bf16[4,128,512]{2,1,0:T(8,128)(2,1)S(1)}, u32[]{:S(2)}, u32[]{:S(2)}) collective-permute-start(bf16[4,128,512]{2,1,0:T(8,128)(2,1)S(1)} %get-tuple-element.104), channel_id=1, source_target_pairs={{0,1},{1,0},{2,3},{3,2},{4,5},{5,4},{6,7},{7,6},{8,9},{9,8},{10,11... | collective-permute-start | bytes 1572872 | tf_op jit(solution)/shard_map/ppermute | solution.py:15
  51.4 1.9 %collective-permute-start = (bf16[128,1024]{1,0:T(8,128)(2,1)}, bf16[128,1024]{1,0:T(8,128)(2,1)}, u32[]{:S(2)}, u32[]{:S(2)}) collective-permute-start(bf16[128,1024]{1,0:T(8,128)(2,1)} %refs_1_.1), channel_id=1, source_target_pairs={{0,1},{1,0},{2,3},{3,2},{4,5},{5,4},{6,7},{7,6},{8,9},{9,8},{10,11... | collective-permute-start | bytes 786440 | tf_op jit(solution)/shard_map/ppermute | solution.py:15
  51.4 2.3 %collective-permute-start.37 = (bf16[4,128,256]{2,1,0:T(8,128)(2,1)}, bf16[4,128,256]{2,1,0:T(8,128)(2,1)S(1)}, u32[]{:S(2)}, u32[]{:S(2)}) collective-permute-start(bf16[4,128,256]{2,1,0:T(8,128)(2,1)} %copy-done.14), channel_id=1, source_target_pairs={{0,1},{1,0},{2,3},{3,2},{4,5},{5,4},{6,7},{7,6},{8,9},{9,8},{10,11... | collective-permute-start | bytes 786440 | tf_op jit(solution)/shard_map/ppermute | solution.py:15
  51.9 2.0 %collective-permute-start.23 = (bf16[128,1024]{1,0:T(8,128)(2,1)}, bf16[128,1024]{1,0:T(8,128)(2,1)S(1)}, u32[]{:S(2)}, u32[]{:S(2)}) collective-permute-start(bf16[128,1024]{1,0:T(8,128)(2,1)} %get-tuple-element.95.refs_3_), channel_id=1, source_target_pairs={{0,1},{1,0},{2,3},{3,2},{4,5},{5,4},{6,7},{7,6},{8,9},{9,8},{10,11... | collective-permute-start | bytes 786440 | tf_op jit(solution)/shard_map/ppermute | solution.py:15
  51.9 3.5 %collective-permute-start.24 = (bf16[128,1024]{1,0:T(8,128)(2,1)}, bf16[128,1024]{1,0:T(8,128)(2,1)S(1)}, u32[]{:S(2)}, u32[]{:S(2)}) collective-permute-start(bf16[128,1024]{1,0:T(8,128)(2,1)} %copy-done.12), channel_id=1, source_target_pairs={{0,1},{1,0},{2,3},{3,2},{4,5},{5,4},{6,7},{7,6},{8,9},{9,8},{10,11... | collective-permute-start | bytes 786440 | tf_op jit(solution)/shard_map/ppermute | solution.py:15
  52.6 4.1 %collective-permute-start.25 = (bf16[128,1024]{1,0:T(8,128)(2,1)}, bf16[128,1024]{1,0:T(8,128)(2,1)S(1)}, u32[]{:S(2)}, u32[]{:S(2)}) collective-permute-start(bf16[128,1024]{1,0:T(8,128)(2,1)} %get-tuple-element.97.refs_7_), channel_id=1, source_target_pairs={{0,1},{1,0},{2,3},{3,2},{4,5},{5,4},{6,7},{7,6},{8,9},{9,8},{10,11... | collective-permute-start | bytes 786440 | tf_op jit(solution)/shard_map/ppermute | solution.py:15
  53.3 11.0 %collective-permute-start.35 = (bf16[4,128,512]{2,1,0:T(8,128)(2,1)S(1)}, bf16[4,128,512]{2,1,0:T(8,128)(2,1)S(1)}, u32[]{:S(2)}, u32[]{:S(2)}) collective-permute-start(bf16[4,128,512]{2,1,0:T(8,128)(2,1)S(1)} %copy-done.1), channel_id=1, source_target_pairs={{0,1},{1,0},{2,3},{3,2},{4,5},{5,4},{6,7},{7,6},{8,9},{9,8},{10,11... | collective-permute-start | bytes 1572872 | tf_op jit(solution)/shard_map/ppermute | solution.py:15
  53.7 14.1 %collective-permute-start.36 = (bf16[4,128,512]{2,1,0:T(8,128)(2,1)S(1)}, bf16[4,128,512]{2,1,0:T(8,128)(2,1)S(1)}, u32[]{:S(2)}, u32[]{:S(2)}) collective-permute-start(bf16[4,128,512]{2,1,0:T(8,128)(2,1)S(1)} %copy-done.3), channel_id=1, source_target_pairs={{0,1},{1,0},{2,3},{3,2},{4,5},{5,4},{6,7},{7,6},{8,9},{9,8},{10,11... | collective-permute-start | bytes 1572872 | tf_op jit(solution)/shard_map/ppermute | solution.py:15
  53.9 15.7 %collective-permute-start.28 = (bf16[256,512]{1,0:T(8,128)(2,1)S(1)}, bf16[256,512]{1,0:T(8,128)(2,1)S(1)}, u32[]{:S(2)}, u32[]{:S(2)}) collective-permute-start(bf16[256,512]{1,0:T(8,128)(2,1)S(1)} %get-tuple-element.106), channel_id=1, source_target_pairs={{0,2},{1,3},{2,0},{3,1},{4,6},{5,7},{6,4},{7,5},{8,10},{9,11},{10,... | collective-permute-start | bytes 786440 | tf_op jit(solution)/shard_map/ppermute | solution.py:15
  55.4 14.4 %collective-permute-start.29 = (bf16[256,512]{1,0:T(8,128)(2,1)S(1)}, bf16[256,512]{1,0:T(8,128)(2,1)S(1)}, u32[]{:S(2)}, u32[]{:S(2)}) collective-permute-start(bf16[256,512]{1,0:T(8,128)(2,1)S(1)} %get-tuple-element.107), channel_id=1, source_target_pairs={{0,4},{1,5},{2,6},{3,7},{4,0},{5,1},{6,2},{7,3},{8,12},{9,13},{10,... | collective-permute-start | bytes 786440 | tf_op jit(solution)/shard_map/ppermute | solution.py:15
  56.7 14.8 %collective-permute-start.30 = (bf16[256,512]{1,0:T(8,128)(2,1)S(1)}, bf16[256,512]{1,0:T(8,128)(2,1)S(1)}, u32[]{:S(2)}, u32[]{:S(2)}) collective-permute-start(bf16[256,512]{1,0:T(8,128)(2,1)S(1)} %get-tuple-element.108), channel_id=1, source_target_pairs={{0,6},{1,7},{2,4},{3,5},{4,2},{5,3},{6,0},{7,1},{8,14},{9,15},{10,... | collective-permute-start | bytes 786440 | tf_op jit(solution)/shard_map/ppermute | solution.py:15
  64.3 16.3 %collective-permute-start.26 = (bf16[512,256]{1,0:T(8,128)(2,1)S(1)}, bf16[512,256]{1,0:T(8,128)(2,1)S(1)}, u32[]{:S(2)}, u32[]{:S(2)}) collective-permute-start(bf16[512,256]{1,0:T(8,128)(2,1)S(1)} %get-tuple-element.102.refs_6_.refs_3_), channel_id=1, source_target_pairs={{0,8},{1,9},{2,10},{3,11},{4,12},{5,13},{6,14},{7,15},{8,0},{9,1},... | collective-permute-start | bytes 786440 | tf_op jit(solution)/shard_map/ppermute | solution.py:15
  68.0 14.3 %collective-permute-start.38 = (bf16[256,512]{1,0:T(8,128)(2,1)S(1)}, bf16[256,512]{1,0:T(8,128)(2,1)S(1)}, u32[]{:S(2)}, u32[]{:S(2)}) collective-permute-start(bf16[256,512]{1,0:T(8,128)(2,1)S(1)} %get-tuple-element.124), channel_id=1, source_target_pairs={{0,2},{1,3},{2,0},{3,1},{4,6},{5,7},{6,4},{7,5},{8,10},{9,11},{10,... | collective-permute-start | bytes 786440 | tf_op jit(solution)/shard_map/ppermute | solution.py:15
  69.6 21.6 %collective-permute-start.39 = (bf16[256,512]{1,0:T(8,128)(2,1)S(1)}, bf16[256,512]{1,0:T(8,128)(2,1)S(1)}, u32[]{:S(2)}, u32[]{:S(2)}) collective-permute-start(bf16[256,512]{1,0:T(8,128)(2,1)S(1)} %get-tuple-element.125), channel_id=1, source_target_pairs={{0,4},{1,5},{2,6},{3,7},{4,0},{5,1},{6,2},{7,3},{8,12},{9,13},{10,... | collective-permute-start | bytes 786440 | tf_op jit(solution)/shard_map/ppermute | solution.py:15
  69.8 25.8 %collective-permute-start.40 = (bf16[256,512]{1,0:T(8,128)(2,1)S(1)}, bf16[256,512]{1,0:T(8,128)(2,1)S(1)}, u32[]{:S(2)}, u32[]{:S(2)}) collective-permute-start(bf16[256,512]{1,0:T(8,128)(2,1)S(1)} %get-tuple-element.126), channel_id=1, source_target_pairs={{0,6},{1,7},{2,4},{3,5},{4,2},{5,3},{6,0},{7,1},{8,14},{9,15},{10,... | collective-permute-start | bytes 786440 | tf_op jit(solution)/shard_map/ppermute | solution.py:15
  72.8 31.2 %collective-permute-start.34 = (bf16[512,512]{1,0:T(8,128)(2,1)S(1)}, bf16[512,512]{1,0:T(8,128)(2,1)S(1)}, u32[]{:S(2)}, u32[]{:S(2)}) collective-permute-start(bf16[512,512]{1,0:T(8,128)(2,1)S(1)} %get-tuple-element.109.refs_3_), channel_id=1, source_target_pairs={{0,8},{1,9},{2,10},{3,11},{4,12},{5,13},{6,14},{7,15},{8,0},{9,1},... | collective-permute-start | bytes 1572872 | tf_op jit(solution)/shard_map/ppermute | solution.py:15
  80.7 16.3 %collective-permute-start.31 = (bf16[128,256]{1,0:T(8,128)(2,1)S(1)}, bf16[128,256]{1,0:T(8,128)(2,1)S(1)}, u32[]{:S(2)}, u32[]{:S(2)}) collective-permute-start(bf16[128,256]{1,0:T(8,128)(2,1)S(1)} %get-tuple-element.111), channel_id=1, source_target_pairs={{0,2},{1,3},{2,0},{3,1},{4,6},{5,7},{6,4},{7,5},{8,10},{9,11},{10,... | collective-permute-start | bytes 196616 | tf_op jit(solution)/shard_map/ppermute | solution.py:15
  82.3 17.4 %collective-permute-start.32 = (bf16[128,256]{1,0:T(8,128)(2,1)S(1)}, bf16[128,256]{1,0:T(8,128)(2,1)S(1)}, u32[]{:S(2)}, u32[]{:S(2)}) collective-permute-start(bf16[128,256]{1,0:T(8,128)(2,1)S(1)} %get-tuple-element.112), channel_id=1, source_target_pairs={{0,4},{1,5},{2,6},{3,7},{4,0},{5,1},{6,2},{7,3},{8,12},{9,13},{10,... | collective-permute-start | bytes 196616 | tf_op jit(solution)/shard_map/ppermute | solution.py:15
  91.2 9.8 %collective-permute-start.33 = (bf16[128,256]{1,0:T(8,128)(2,1)S(1)}, bf16[128,256]{1,0:T(8,128)(2,1)S(1)}, u32[]{:S(2)}, u32[]{:S(2)}) collective-permute-start(bf16[128,256]{1,0:T(8,128)(2,1)S(1)} %get-tuple-element.113), channel_id=1, source_target_pairs={{0,6},{1,7},{2,4},{3,5},{4,2},{5,3},{6,0},{7,1},{8,14},{9,15},{10,... | collective-permute-start | bytes 196616 | tf_op jit(solution)/shard_map/ppermute | solution.py:15
  96.9 30.2 %collective-permute-start.44 = (bf16[512,512]{1,0:T(8,128)(2,1)S(1)}, bf16[512,512]{1,0:T(8,128)(2,1)S(1)}, u32[]{:S(2)}, u32[]{:S(2)}) collective-permute-start(bf16[512,512]{1,0:T(8,128)(2,1)S(1)} %get-tuple-element.127.refs_3_), channel_id=1, source_target_pairs={{0,8},{1,9},{2,10},{3,11},{4,12},{5,13},{6,14},{7,15},{8,0},{9,1},... | collective-permute-start | bytes 1572872 | tf_op jit(solution)/shard_map/ppermute | solution.py:15
  97.0 19.0 %collective-permute-start.45 = (bf16[256,512]{1,0:T(8,128)(2,1)S(1)}, bf16[256,512]{1,0:T(8,128)(2,1)S(1)}, u32[]{:S(2)}, u32[]{:S(2)}) collective-permute-start(bf16[256,512]{1,0:T(8,128)(2,1)S(1)} %get-tuple-element.137), channel_id=1, source_target_pairs={{0,2},{1,3},{2,0},{3,1},{4,6},{5,7},{6,4},{7,5},{8,10},{9,11},{10,... | collective-permute-start | bytes 786440 | tf_op jit(solution)/shard_map/ppermute | solution.py:15
  99.7 17.1 %collective-permute-start.46 = (bf16[256,512]{1,0:T(8,128)(2,1)S(1)}, bf16[256,512]{1,0:T(8,128)(2,1)S(1)}, u32[]{:S(2)}, u32[]{:S(2)}) collective-permute-start(bf16[256,512]{1,0:T(8,128)(2,1)S(1)} %get-tuple-element.138), channel_id=1, source_target_pairs={{0,4},{1,5},{2,6},{3,7},{4,0},{5,1},{6,2},{7,3},{8,12},{9,13},{10,... | collective-permute-start | bytes 786440 | tf_op jit(solution)/shard_map/ppermute | solution.py:15
  101.0 21.5 %collective-permute-start.47 = (bf16[256,512]{1,0:T(8,128)(2,1)S(1)}, bf16[256,512]{1,0:T(8,128)(2,1)S(1)}, u32[]{:S(2)}, u32[]{:S(2)}) collective-permute-start(bf16[256,512]{1,0:T(8,128)(2,1)S(1)} %get-tuple-element.139), channel_id=1, source_target_pairs={{0,6},{1,7},{2,4},{3,5},{4,2},{5,3},{6,0},{7,1},{8,14},{9,15},{10,... | collective-permute-start | bytes 786440 | tf_op jit(solution)/shard_map/ppermute | solution.py:15
  104.0 30.3 %collective-permute-start.52 = (bf16[256,256]{1,0:T(8,128)(2,1)S(1)}, bf16[256,256]{1,0:T(8,128)(2,1)S(1)}, u32[]{:S(2)}, u32[]{:S(2)}) collective-permute-start(bf16[256,256]{1,0:T(8,128)(2,1)S(1)} %get-tuple-element.150), channel_id=1, source_target_pairs={{0,2},{1,3},{2,0},{3,1},{4,6},{5,7},{6,4},{7,5},{8,10},{9,11},{10,... | collective-permute-start | bytes 393224 | tf_op jit(solution)/shard_map/ppermute | solution.py:15
  116.0 11.2 %collective-permute-start.41 = (bf16[128,512]{1,0:T(8,128)(2,1)S(1)}, bf16[128,512]{1,0:T(8,128)(2,1)S(1)}, u32[]{:S(2)}, u32[]{:S(2)}) collective-permute-start(bf16[128,512]{1,0:T(8,128)(2,1)S(1)} %get-tuple-element.129), channel_id=1, source_target_pairs={{0,2},{1,3},{2,0},{3,1},{4,6},{5,7},{6,4},{7,5},{8,10},{9,11},{10,... | collective-permute-start | bytes 393224 | tf_op jit(solution)/shard_map/ppermute | solution.py:15
  116.8 13.2 %collective-permute-start.42 = (bf16[128,512]{1,0:T(8,128)(2,1)S(1)}, bf16[128,512]{1,0:T(8,128)(2,1)S(1)}, u32[]{:S(2)}, u32[]{:S(2)}) collective-permute-start(bf16[128,512]{1,0:T(8,128)(2,1)S(1)} %get-tuple-element.130), channel_id=1, source_target_pairs={{0,4},{1,5},{2,6},{3,7},{4,0},{5,1},{6,2},{7,3},{8,12},{9,13},{10,... | collective-permute-start | bytes 393224 | tf_op jit(solution)/shard_map/ppermute | solution.py:15
  122.5 11.5 %collective-permute-start.43 = (bf16[128,512]{1,0:T(8,128)(2,1)S(1)}, bf16[128,512]{1,0:T(8,128)(2,1)S(1)}, u32[]{:S(2)}, u32[]{:S(2)}) collective-permute-start(bf16[128,512]{1,0:T(8,128)(2,1)S(1)} %get-tuple-element.131), channel_id=1, source_target_pairs={{0,6},{1,7},{2,4},{3,5},{4,2},{5,3},{6,0},{7,1},{8,14},{9,15},{10,... | collective-permute-start | bytes 393224 | tf_op jit(solution)/shard_map/ppermute | solution.py:15
  127.1 12.7 %collective-permute-start.53 = (bf16[256,256]{1,0:T(8,128)(2,1)S(1)}, bf16[256,256]{1,0:T(8,128)(2,1)S(1)}, u32[]{:S(2)}, u32[]{:S(2)}) collective-permute-start(bf16[256,256]{1,0:T(8,128)(2,1)S(1)} %get-tuple-element.151), channel_id=1, source_target_pairs={{0,4},{1,5},{2,6},{3,7},{4,0},{5,1},{6,2},{7,3},{8,12},{9,13},{10,... | collective-permute-start | bytes 393224 | tf_op jit(solution)/shard_map/ppermute | solution.py:15
  127.2 15.2 %collective-permute-start.54 = (bf16[256,256]{1,0:T(8,128)(2,1)S(1)}, bf16[256,256]{1,0:T(8,128)(2,1)S(1)}, u32[]{:S(2)}, u32[]{:S(2)}) collective-permute-start(bf16[256,256]{1,0:T(8,128)(2,1)S(1)} %get-tuple-element.152), channel_id=1, source_target_pairs={{0,6},{1,7},{2,4},{3,5},{4,2},{5,3},{6,0},{7,1},{8,14},{9,15},{10,... | collective-permute-start | bytes 393224 | tf_op jit(solution)/shard_map/ppermute | solution.py:15
  130.0 31.7 %collective-permute-start.51 = (bf16[512,512]{1,0:T(8,128)(2,1)S(1)}, bf16[512,512]{1,0:T(8,128)(2,1)S(1)}, u32[]{:S(2)}, u32[]{:S(2)}) collective-permute-start(bf16[512,512]{1,0:T(8,128)(2,1)S(1)} %get-tuple-element.140.refs_3_), channel_id=1, source_target_pairs={{0,8},{1,9},{2,10},{3,11},{4,12},{5,13},{6,14},{7,15},{8,0},{9,1},... | collective-permute-start | bytes 1572872 | tf_op jit(solution)/shard_map/ppermute | solution.py:15
  134.1 9.7 %collective-permute-start.48 = (bf16[128,512]{1,0:T(8,128)(2,1)S(1)}, bf16[128,512]{1,0:T(8,128)(2,1)S(1)}, u32[]{:S(2)}, u32[]{:S(2)}) collective-permute-start(bf16[128,512]{1,0:T(8,128)(2,1)S(1)} %get-tuple-element.142), channel_id=1, source_target_pairs={{0,2},{1,3},{2,0},{3,1},{4,6},{5,7},{6,4},{7,5},{8,10},{9,11},{10,... | collective-permute-start | bytes 393224 | tf_op jit(solution)/shard_map/ppermute | solution.py:15
  134.3 15.2 %collective-permute-start.49 = (bf16[128,512]{1,0:T(8,128)(2,1)S(1)}, bf16[128,512]{1,0:T(8,128)(2,1)S(1)}, u32[]{:S(2)}, u32[]{:S(2)}) collective-permute-start(bf16[128,512]{1,0:T(8,128)(2,1)S(1)} %get-tuple-element.143), channel_id=1, source_target_pairs={{0,4},{1,5},{2,6},{3,7},{4,0},{5,1},{6,2},{7,3},{8,12},{9,13},{10,... | collective-permute-start | bytes 393224 | tf_op jit(solution)/shard_map/ppermute | solution.py:15
  139.9 12.4 %collective-permute-start.50 = (bf16[128,512]{1,0:T(8,128)(2,1)S(1)}, bf16[128,512]{1,0:T(8,128)(2,1)S(1)}, u32[]{:S(2)}, u32[]{:S(2)}) collective-permute-start(bf16[128,512]{1,0:T(8,128)(2,1)S(1)} %get-tuple-element.144), channel_id=1, source_target_pairs={{0,6},{1,7},{2,4},{3,5},{4,2},{5,3},{6,0},{7,1},{8,14},{9,15},{10,... | collective-permute-start | bytes 393224 | tf_op jit(solution)/shard_map/ppermute | solution.py:15
  143.1 22.3 %collective-permute-start.58 = (bf16[512,256]{1,0:T(8,128)(2,1)S(1)}, bf16[512,256]{1,0:T(8,128)(2,1)S(1)}, u32[]{:S(2)}, u32[]{:S(2)}) collective-permute-start(bf16[512,256]{1,0:T(8,128)(2,1)S(1)} %get-tuple-element.153.refs_3_), channel_id=1, source_target_pairs={{0,8},{1,9},{2,10},{3,11},{4,12},{5,13},{6,14},{7,15},{8,0},{9,1},... | collective-permute-start | bytes 786440 | tf_op jit(solution)/shard_map/ppermute | solution.py:15
  161.8 6.4 %collective-permute-start.55 = (bf16[128,512]{1,0:T(8,128)(2,1)S(1)}, bf16[128,512]{1,0:T(8,128)(2,1)S(1)}, u32[]{:S(2)}, u32[]{:S(2)}) collective-permute-start(bf16[128,512]{1,0:T(8,128)(2,1)S(1)} %get-tuple-element.155), channel_id=1, source_target_pairs={{0,2},{1,3},{2,0},{3,1},{4,6},{5,7},{6,4},{7,5},{8,10},{9,11},{10,... | collective-permute-start | bytes 393224 | tf_op jit(solution)/shard_map/ppermute | solution.py:15
  163.1 5.2 %collective-permute-start.56 = (bf16[128,512]{1,0:T(8,128)(2,1)S(1)}, bf16[128,512]{1,0:T(8,128)(2,1)S(1)}, u32[]{:S(2)}, u32[]{:S(2)}) collective-permute-start(bf16[128,512]{1,0:T(8,128)(2,1)S(1)} %get-tuple-element.156), channel_id=1, source_target_pairs={{0,4},{1,5},{2,6},{3,7},{4,0},{5,1},{6,2},{7,3},{8,12},{9,13},{10,... | collective-permute-start | bytes 393224 | tf_op jit(solution)/shard_map/ppermute | solution.py:15
  163.1 7.4 %collective-permute-start.57 = (bf16[128,512]{1,0:T(8,128)(2,1)S(1)}, bf16[128,512]{1,0:T(8,128)(2,1)S(1)}, u32[]{:S(2)}, u32[]{:S(2)}) collective-permute-start(bf16[128,512]{1,0:T(8,128)(2,1)S(1)} %get-tuple-element.157), channel_id=1, source_target_pairs={{0,6},{1,7},{2,4},{3,5},{4,2},{5,3},{6,0},{7,1},{8,14},{9,15},{10,... | collective-permute-start | bytes 393224 | tf_op jit(solution)/shard_map/ppermute | solution.py:15
  165.5 5.8 %collective-permute-start.59 = (bf16[128,256]{1,0:T(8,128)(2,1)S(1)}, bf16[128,256]{1,0:T(8,128)(2,1)S(1)}, u32[]{:S(2)}, u32[]{:S(2)}) collective-permute-start(bf16[128,256]{1,0:T(8,128)(2,1)S(1)} %get-tuple-element.160), channel_id=1, source_target_pairs={{0,2},{1,3},{2,0},{3,1},{4,6},{5,7},{6,4},{7,5},{8,10},{9,11},{10,... | collective-permute-start | bytes 196616 | tf_op jit(solution)/shard_map/ppermute | solution.py:15
  166.8 11.4 %collective-permute-start.63 = (bf16[4,64,512]{2,1,0:T(8,128)(2,1)S(1)}, bf16[4,64,512]{2,1,0:T(8,128)(2,1)S(1)}, u32[]{:S(2)}, u32[]{:S(2)}) collective-permute-start(bf16[4,64,512]{2,1,0:T(8,128)(2,1)S(1)} %shard_map.77), channel_id=1, source_target_pairs={{0,1},{1,0},{2,3},{3,2},{4,5},{5,4},{6,7},{7,6},{8,9},{9,8},{10,11... | collective-permute-start | bytes 786440 | tf_op jit(solution)/shard_map/ppermute | solution.py:15
  168.3 9.9 %collective-permute-start.64 = (bf16[4,64,512]{2,1,0:T(8,128)(2,1)S(1)}, bf16[4,64,512]{2,1,0:T(8,128)(2,1)S(1)}, u32[]{:S(2)}, u32[]{:S(2)}) collective-permute-start(bf16[4,64,512]{2,1,0:T(8,128)(2,1)S(1)} %shard_map.78), channel_id=1, source_target_pairs={{0,1},{1,0},{2,3},{3,2},{4,5},{5,4},{6,7},{7,6},{8,9},{9,8},{10,11... | collective-permute-start | bytes 786440 | tf_op jit(solution)/shard_map/ppermute | solution.py:15
  170.6 7.7 %collective-permute-start.65 = (bf16[4,64,512]{2,1,0:T(8,128)(2,1)S(1)}, bf16[4,64,512]{2,1,0:T(8,128)(2,1)S(1)}, u32[]{:S(2)}, u32[]{:S(2)}) collective-permute-start(bf16[4,64,512]{2,1,0:T(8,128)(2,1)S(1)} %shard_map.79), channel_id=1, source_target_pairs={{0,1},{1,0},{2,3},{3,2},{4,5},{5,4},{6,7},{7,6},{8,9},{9,8},{10,11... | collective-permute-start | bytes 786440 | tf_op jit(solution)/shard_map/ppermute | solution.py:15
  170.6 5.0 %collective-permute-start.60 = (bf16[128,256]{1,0:T(8,128)(2,1)S(1)}, bf16[128,256]{1,0:T(8,128)(2,1)S(1)}, u32[]{:S(2)}, u32[]{:S(2)}) collective-permute-start(bf16[128,256]{1,0:T(8,128)(2,1)S(1)} %get-tuple-element.161), channel_id=1, source_target_pairs={{0,4},{1,5},{2,6},{3,7},{4,0},{5,1},{6,2},{7,3},{8,12},{9,13},{10,... | collective-permute-start | bytes 196616 | tf_op jit(solution)/shard_map/ppermute | solution.py:15
  171.3 5.5 %collective-permute-start.61 = (bf16[128,256]{1,0:T(8,128)(2,1)S(1)}, bf16[128,256]{1,0:T(8,128)(2,1)S(1)}, u32[]{:S(2)}, u32[]{:S(2)}) collective-permute-start(bf16[128,256]{1,0:T(8,128)(2,1)S(1)} %get-tuple-element.162), channel_id=1, source_target_pairs={{0,6},{1,7},{2,4},{3,5},{4,2},{5,3},{6,0},{7,1},{8,14},{9,15},{10,... | collective-permute-start | bytes 196616 | tf_op jit(solution)/shard_map/ppermute | solution.py:15
  (21 other events, 71.3 us)
